TPU v7x, 32 devices: a whole 2x2x4 slice. The times are simulated.
32 devices in a mesh: rows: 2 (over core), seq: 16 (over z, y, x).
Axes of the slice: x: 2, y: 2, z: 4, core: 2. Of those that a mesh axis runs over, the one named last changes fastest.
Arguments:
- tokens: bfloat16 [2, 4096, 768], P('rows', 'seq'), may hold values from -6 to 6
- cotangent: bfloat16 [2, 4096, 768], P('rows', 'seq'), may hold values from -6 to 6
- w_query: bfloat16 [768, 768], replicated, may hold values from -0.21875 to 0.21875
- w_key: bfloat16 [768, 768], replicated, may hold values from -0.21875 to 0.21875
- w_value: bfloat16 [768, 768], replicated, may hold values from -0.21875 to 0.21875
- w_output: bfloat16 [768, 768], replicated, may hold values from -1.75 to 1.75
- w_inner: bfloat16 [768, 3072], replicated, may hold values from -0.21875 to 0.21875
- w_outer: bfloat16 [3072, 768], replicated, may hold values from -0.109375 to 0.109375
- rel_table: bfloat16 [512, 768], replicated, may hold values from -6 to 6
- mid_gain: float32 [768], replicated, may hold values from 0.1 to 1.9
- mid_bias: float32 [768], replicated, may hold values from -3 to 3
- end_gain: float32 [768], replicated, may hold values from 0.1 to 1.9
- end_bias: float32 [768], replicated, may hold values from -3 to 3
- seq_lengths: int32 [2, 4], P('rows'), may hold values from 1 to 4093, as said below
- pad_mask: int32 [2, 4096], P('rows'), may hold values 0 or 1
- rel_buckets: int32 [512], replicated, may hold values from -256 to 255
Outputs:
- layer_out: bfloat16 [2, 4096, 768], P('rows', 'seq')
- tokens_grad: bfloat16 [2, 4096, 768], P('rows', 'seq')
- w_query_grad: float32 [768, 768], replicated
- w_key_grad: float32 [768, 768], replicated
- w_value_grad: float32 [768, 768], replicated
- w_output_grad: float32 [768, 768], replicated
- w_inner_grad: float32 [768, 3072], replicated
- w_outer_grad: float32 [3072, 768], replicated
- rel_table_grad: float32 [512, 768], replicated
- mid_gain_grad: float32 [768], replicated
- mid_bias_grad: float32 [768], replicated
- end_gain_grad: float32 [768], replicated
- end_bias_grad: float32 [768], replicated
Inputs may be any that keep to these rules, and one draw needn't show every extreme that they name: `seq_lengths`: in each row the 4 lengths sum to 4096; all but one are at most 64, and in one row those are all 1.
All inputs are finite; a program needn't handle non-finite values. No bound on the sum of `pad_mask` on one device may be relied on, other than what follows from the above.
Results may differ from a plain program's by a relative error of at most 0.02.
Values may be sent and summed in bfloat16 or wider, within the bound.
A program may use at most 256 MiB of HBM per device.

v0:
```python
from functools import partial
import math

import jax
import jax.numpy as jnp
from jax import lax
from jax.sharding import PartitionSpec as P

H = 12
DH = 64
SPAN = 256


norm_eps = 1e-07
masked_score = -1e30


def with_halo(block, sides, width):
    for axis, dim in sides:
        count = lax.axis_size(axis)
        forward = [(i, i + 1) for i in range(count - 1)]
        backward = [(target, source) for source, target in forward]
        low = lax.ppermute(
            lax.slice_in_dim(block, block.shape[dim] - width, None, axis=dim), axis, forward
        )
        high = lax.ppermute(lax.slice_in_dim(block, 0, width, axis=dim), axis, backward)
        block = jnp.concatenate([low, block, high], axis=dim)
    return block


def shifted(shard, axis, by):
    count = lax.axis_size(axis)
    pairs = [(i, i + by) for i in range(count) if 0 <= i + by < count]
    return lax.ppermute(shard, axis, pairs)


def layer_norm(values, norm_gain, norm_bias):
    centre = values - jnp.mean(values, axis=-1, keepdims=True)
    spread = jnp.mean(centre * centre, axis=-1, keepdims=True)
    return centre * lax.rsqrt(spread + norm_eps) * norm_gain + norm_bias


def project(left, right):
    return jnp.einsum("rtd,de->rte", left, right, preferred_element_type=jnp.float32)


def segment_of(slot_ids, seq_ends):
    return jnp.sum((slot_ids[None, :, None] >= seq_ends[:, None, :]).astype(jnp.int32), axis=2)


def band_masks(block_len):
    ext_len = block_len + 2 * SPAN
    query_pos = jnp.arange(block_len, dtype=jnp.int32)[:, None]
    key_pos = jnp.arange(ext_len, dtype=jnp.int32)[None, :]
    inside = jnp.abs(query_pos - key_pos + SPAN) < SPAN
    diagonal = key_pos == query_pos + SPAN
    return (inside, diagonal)


def shift_cols(values, cols_out, offset):
    lead_dims = values.shape[:-2]
    row_count, band_count = values.shape[-2:]
    pad_front = max(0, row_count - 1 - offset)
    pad_width = max(cols_out + offset + pad_front, band_count + pad_front, cols_out + 1)
    widths = [(0, 0)] * len(lead_dims) + [(0, 0), (pad_front, pad_width - band_count - pad_front)]
    padded = jnp.pad(values, widths)
    flat = padded.reshape(lead_dims + (row_count * pad_width,))
    shift_start = offset + pad_front
    taken = flat[..., shift_start : shift_start + row_count * (pad_width - 1)]
    return taken.reshape(lead_dims + (row_count, pad_width - 1))[..., :cols_out]


def unshift_cols(values, pad_front, cols_out):
    lead_dims = values.shape[:-2]
    row_count, col_total = values.shape[-2:]
    pad_width = max(col_total + pad_front, row_count + cols_out)
    widths = [(0, 0)] * len(lead_dims) + [(0, 0), (pad_front, pad_width - col_total - pad_front)]
    padded = jnp.pad(values, widths)
    flat = padded.reshape(lead_dims + (row_count * pad_width,))
    flat = jnp.pad(flat, [(0, 0)] * len(lead_dims) + [(0, row_count)])
    return flat.reshape(lead_dims + (row_count, pad_width + 1))[..., :cols_out]


def shards(
    tokens,
    cotangent,
    w_query,
    w_key,
    w_value,
    w_output,
    w_inner,
    w_outer,
    rel_table,
    mid_gain,
    mid_bias,
    end_gain,
    end_bias,
    seq_lengths,
    pad_mask,
    rel_buckets,
):
    rows_here, block_len, model_width = tokens.shape
    ext_len = block_len + 2 * SPAN
    band_len = 2 * SPAN
    score_scale = 1.0 / math.sqrt(3 * DH)
    seq_place = lax.axis_index("seq")
    row_len = block_len * lax.axis_size("seq")
    seq_ends = jnp.cumsum(seq_lengths, axis=1)
    query_slots = seq_place * block_len + jnp.arange(block_len, dtype=jnp.int32)
    key_slots = seq_place * block_len - SPAN + jnp.arange(ext_len, dtype=jnp.int32)
    seg_query = segment_of(query_slots, seq_ends)
    in_row = (key_slots >= 0) & (key_slots < row_len)
    seg_key = jnp.where(in_row[None, :], segment_of(key_slots, seq_ends), -1)
    keep_key = lax.dynamic_slice_in_dim(
        jnp.pad(pad_mask, ((0, 0), (SPAN, SPAN))), seq_place * block_len, ext_len, 1
    )
    inside, diagonal = band_masks(block_len)
    allowed = (
        (seg_query[:, :, None] == seg_key[:, None, :])
        & inside[None]
        & ((keep_key[:, None, :] == 1) | diagonal[None])
    )[:, None]
    band_ids = jnp.arange(band_len, dtype=jnp.int32)
    band_bucket = jnp.take(rel_buckets, jnp.clip(band_len - band_ids, 0, band_len - 1))
    to_band_pos = jnp.clip(band_bucket + SPAN, 0, band_len - 1)
    from_band_pos = jnp.clip(SPAN - band_bucket, 0, band_len - 1)
    table_ids = jnp.arange(band_len, dtype=jnp.int32)[None, :]
    to_onehot = (to_band_pos[:, None] == table_ids).astype(jnp.bfloat16)
    from_onehot_rev = (from_band_pos[::-1][:, None] == table_ids).astype(jnp.bfloat16)
    w_pair = jnp.concatenate([w_key, w_value], axis=1)
    query_low = project(tokens, w_query).astype(jnp.bfloat16)
    pair_low = project(tokens, w_pair).astype(jnp.bfloat16)
    pair_ext = with_halo(pair_low, (("seq", 1),), SPAN)
    rel_key_flat = jnp.dot(rel_table, w_key, preferred_element_type=jnp.float32).astype(
        jnp.bfloat16
    )
    rel_query_flat = jnp.dot(rel_table, w_query, preferred_element_type=jnp.float32).astype(
        jnp.bfloat16
    )
    rel_key = rel_key_flat.reshape(band_len, H, DH)
    rel_query = rel_query_flat.reshape(band_len, H, DH)
    relative_key_banded = (
        jnp.dot(to_onehot, rel_key_flat, preferred_element_type=jnp.float32)
        .astype(jnp.bfloat16)
        .reshape(band_len, H, DH)
    )
    rel_query_rev = (
        jnp.dot(from_onehot_rev, rel_query_flat, preferred_element_type=jnp.float32)
        .astype(jnp.bfloat16)
        .reshape(band_len, H, DH)
    )
    pair_rows = 1

    def grouped(values):
        return values.reshape((rows_here // pair_rows, pair_rows) + values.shape[1:])

    query_heads = grouped(query_low.reshape(rows_here, block_len, H, DH))
    allowed_groups = grouped(allowed)

    def split_pair(pair_block_rows):
        group_total_count = pair_block_rows.shape[0]
        key_ext = pair_block_rows[..., :model_width].reshape(group_total_count, ext_len, H, DH)
        value_ext = pair_block_rows[..., model_width:].reshape(group_total_count, ext_len, H, DH)
        return (key_ext, value_ext)

    def scores_of(query_block_rows, key_ext, vis_mask):
        content = jnp.einsum(
            "gihd,gjhd->ghij", query_block_rows, key_ext, preferred_element_type=jnp.float32
        )
        to_band = jnp.einsum(
            "kjwy,owy->kwjo",
            query_block_rows,
            relative_key_banded,
            preferred_element_type=jnp.float32,
        )
        from_rev = jnp.einsum(
            "gjhd,phd->ghjp", key_ext, rel_query_rev, preferred_element_type=jnp.float32
        )
        to_term = shift_cols(to_band, ext_len, 0)
        from_term = jnp.swapaxes(shift_cols(from_rev, block_len, band_len - 1), 2, 3)
        return jnp.where(vis_mask, (content + to_term + from_term) * score_scale, masked_score)

    def attend(block_items):
        query_block_rows, pair_block_rows, vis_mask = block_items
        key_ext, value_ext = split_pair(pair_block_rows)
        scores = scores_of(query_block_rows, key_ext, vis_mask)
        row_top = jnp.max(scores, axis=3, keepdims=True)
        weights = jnp.exp(scores - row_top)
        row_total = jnp.sum(weights, axis=3, keepdims=True)
        probability_reduced = (weights / row_total).astype(jnp.bfloat16)
        attn_blk = jnp.einsum(
            "ghij,gjhd->gihd", probability_reduced, value_ext, preferred_element_type=jnp.float32
        )
        attn_blk = attn_blk.reshape(query_block_rows.shape[0], block_len, model_width).astype(
            jnp.bfloat16
        )
        return (attn_blk, (row_top + jnp.log(row_total))[..., 0])

    attn_low, log_total = lax.map(attend, (query_heads, grouped(pair_ext), allowed_groups))
    attn_low = attn_low.reshape(rows_here, block_len, model_width)
    mixed_out = project(attn_low, w_output)
    hidden, mid_back = jax.vjp(
        layer_norm, tokens.astype(jnp.float32) + mixed_out, mid_gain, mid_bias
    )
    hidden_low = hidden.astype(jnp.bfloat16)
    inner_pre = project(hidden_low, w_inner)
    active, gelu_backward_pass = jax.vjp(partial(jax.nn.gelu, approximate=False), inner_pre)
    active_low = active.astype(jnp.bfloat16)
    outer_out = project(active_low, w_outer)
    final_out, end_back = jax.vjp(layer_norm, hidden + outer_out, end_gain, end_bias)
    layer_out = final_out.astype(jnp.bfloat16)
    summed_gradient, end_gain_part, end_bias_part = end_back(cotangent.astype(jnp.float32))
    outer_low = summed_gradient.astype(jnp.bfloat16)
    outer_w_part = jnp.einsum(
        "rti,rto->io", active_low, outer_low, preferred_element_type=jnp.float32
    )
    active_grad = jnp.einsum("rto,io->rti", outer_low, w_outer, preferred_element_type=jnp.float32)
    inner_low = gelu_backward_pass(active_grad)[0].astype(jnp.bfloat16)
    inner_w_part = jnp.einsum(
        "rtd,rtf->df", hidden_low, inner_low, preferred_element_type=jnp.float32
    )
    hidden_grad = summed_gradient + jnp.einsum(
        "rtf,df->rtd", inner_low, w_inner, preferred_element_type=jnp.float32
    )
    resid_grad, mid_gain_part, mid_bias_part = mid_back(hidden_grad)
    mixed_low = resid_grad.astype(jnp.bfloat16)
    output_w_part = jnp.einsum(
        "rtd,rte->de", attn_low, mixed_low, preferred_element_type=jnp.float32
    )
    attn_grad = jnp.einsum(
        "rte,de->rtd", mixed_low, w_output, preferred_element_type=jnp.float32
    ).astype(jnp.bfloat16)

    def attend_back(block_items):
        query_block_rows, pair_block_rows, vis_mask, grad_blk, log_sum = block_items
        group_total_count = query_block_rows.shape[0]
        key_ext, value_ext = split_pair(pair_block_rows)
        scores = scores_of(query_block_rows, key_ext, vis_mask)
        prob_vals = jnp.exp(scores - log_sum[..., None])
        probability_reduced = prob_vals.astype(jnp.bfloat16)
        grad_heads = grad_blk.reshape(group_total_count, block_len, H, DH)
        prob_grad = jnp.einsum(
            "gihd,gjhd->ghij", grad_heads, value_ext, preferred_element_type=jnp.float32
        )
        score_grad = prob_vals * (prob_grad - jnp.sum(prob_vals * prob_grad, axis=3, keepdims=True))
        score_low = score_grad.astype(jnp.bfloat16)
        to_band_grad = unshift_cols(score_low, 0, band_len)
        from_rev_grad = unshift_cols(jnp.swapaxes(score_low, 2, 3), band_len - 1, band_len)
        to_grad = (
            score_scale
            * jnp.einsum(
                "ghim,mr->ghir", to_band_grad, to_onehot, preferred_element_type=jnp.float32
            )
        ).astype(jnp.bfloat16)
        from_grad = (
            score_scale
            * jnp.einsum(
                "ghjp,pr->ghrj", from_rev_grad, from_onehot_rev, preferred_element_type=jnp.float32
            )
        ).astype(jnp.bfloat16)
        query_grad = score_scale * jnp.einsum(
            "ghij,gjhd->gihd", score_low, key_ext, preferred_element_type=jnp.float32
        )
        query_grad = query_grad + jnp.einsum(
            "ghir,rhd->gihd", to_grad, rel_key, preferred_element_type=jnp.float32
        )
        key_grad = score_scale * jnp.einsum(
            "ghij,gihd->gjhd", score_low, query_block_rows, preferred_element_type=jnp.float32
        )
        key_grad = key_grad + jnp.einsum(
            "ghrj,rhd->gjhd", from_grad, rel_query, preferred_element_type=jnp.float32
        )
        value_grad = jnp.einsum(
            "ghij,gihd->gjhd", probability_reduced, grad_heads, preferred_element_type=jnp.float32
        )
        pair_grad = jnp.concatenate(
            [
                key_grad.reshape(group_total_count, ext_len, model_width),
                value_grad.reshape(group_total_count, ext_len, model_width),
            ],
            axis=2,
        )
        rel_key_grad = jnp.einsum(
            "ghir,gihd->rhd", to_grad, query_block_rows, preferred_element_type=jnp.float32
        )
        rel_query_grad = jnp.einsum(
            "ghrj,gjhd->rhd", from_grad, key_ext, preferred_element_type=jnp.float32
        )
        return (
            query_grad.reshape(group_total_count, block_len, model_width),
            pair_grad,
            rel_key_grad,
            rel_query_grad,
        )

    query_grad, pair_grad, rel_key_grad, rel_query_grad = lax.map(
        attend_back, (query_heads, grouped(pair_ext), allowed_groups, grouped(attn_grad), log_total)
    )
    query_grad_low = query_grad.reshape(rows_here, block_len, model_width).astype(jnp.bfloat16)
    pair_grad = pair_grad.reshape(rows_here, ext_len, 2 * model_width)
    rel_key_sum = jnp.sum(rel_key_grad, axis=0).reshape(band_len, model_width)
    rel_query_sum = jnp.sum(rel_query_grad, axis=0).reshape(band_len, model_width)
    from_next = shifted(pair_grad[:, :SPAN].astype(jnp.bfloat16), "seq", -1).astype(jnp.float32)
    from_prev = shifted(pair_grad[:, SPAN + block_len :].astype(jnp.bfloat16), "seq", 1).astype(
        jnp.float32
    )
    pair_total = pair_grad[:, SPAN : SPAN + block_len]
    pair_total = pair_total + from_prev
    pair_total = pair_total + from_next
    pair_grad_low = pair_total.astype(jnp.bfloat16)
    query_w_part = jnp.einsum(
        "rtd,rte->de", tokens, query_grad_low, preferred_element_type=jnp.float32
    )
    pair_w_part = jnp.einsum(
        "rtd,rte->de", tokens, pair_grad_low, preferred_element_type=jnp.float32
    )
    tokens_grad = resid_grad + jnp.einsum(
        "rte,de->rtd", query_grad_low, w_query, preferred_element_type=jnp.float32
    )
    tokens_grad = (
        tokens_grad
        + jnp.einsum("rte,de->rtd", pair_grad_low, w_pair, preferred_element_type=jnp.float32)
    ).astype(jnp.bfloat16)
    shared = lax.psum(
        (rel_key_sum, rel_query_sum, mid_gain_part, mid_bias_part, end_gain_part, end_bias_part),
        ("rows", "seq"),
    )
    rel_key_low = shared[0].astype(jnp.bfloat16)
    rel_query_low = shared[1].astype(jnp.bfloat16)
    grad_parts = (
        query_w_part,
        pair_w_part[:, :model_width],
        pair_w_part[:, model_width:],
        output_w_part,
        inner_w_part,
        outer_w_part,
    )
    col_count = model_width // lax.axis_size("seq")
    col_start = lax.axis_index("seq") * col_count
    over_rows = (
        lax.psum_scatter(
            grad_parts[0].astype(jnp.bfloat16), "rows", scatter_dimension=0, tiled=True
        ).astype(jnp.float32),
        lax.psum_scatter(
            grad_parts[1].astype(jnp.bfloat16), "rows", scatter_dimension=0, tiled=True
        ).astype(jnp.float32),
        lax.psum_scatter(
            grad_parts[2].astype(jnp.bfloat16), "rows", scatter_dimension=0, tiled=True
        ).astype(jnp.float32),
        lax.psum_scatter(
            grad_parts[3].astype(jnp.bfloat16), "rows", scatter_dimension=0, tiled=True
        ).astype(jnp.float32),
        lax.psum_scatter(
            grad_parts[4].astype(jnp.bfloat16), "rows", scatter_dimension=0, tiled=True
        ).astype(jnp.float32),
        lax.psum_scatter(
            grad_parts[5].astype(jnp.bfloat16), "rows", scatter_dimension=0, tiled=True
        ).astype(jnp.float32),
    )
    over_both = (
        lax.psum_scatter(
            over_rows[0].astype(jnp.bfloat16), "seq", scatter_dimension=1, tiled=True
        ).astype(jnp.float32),
        lax.psum_scatter(
            over_rows[1].astype(jnp.bfloat16), "seq", scatter_dimension=1, tiled=True
        ).astype(jnp.float32),
        lax.psum_scatter(
            over_rows[2].astype(jnp.bfloat16), "seq", scatter_dimension=1, tiled=True
        ).astype(jnp.float32),
        lax.psum_scatter(
            over_rows[3].astype(jnp.bfloat16), "seq", scatter_dimension=1, tiled=True
        ).astype(jnp.float32),
        lax.psum_scatter(
            over_rows[4].astype(jnp.bfloat16), "seq", scatter_dimension=1, tiled=True
        ).astype(jnp.float32),
        lax.psum_scatter(
            over_rows[5].astype(jnp.bfloat16), "seq", scatter_dimension=1, tiled=True
        ).astype(jnp.float32),
    )
    row_count = model_width // lax.axis_size("rows")
    table_count = band_len // lax.axis_size("rows")
    row_start = lax.axis_index("rows") * row_count
    table_start = lax.axis_index("rows") * table_count
    table_cols = lax.dynamic_slice_in_dim(rel_table, row_start, row_count, 1)
    extra_query = jnp.einsum(
        "ra,rc->ac",
        table_cols,
        lax.dynamic_slice_in_dim(rel_query_low, col_start, col_count, 1),
        preferred_element_type=jnp.float32,
    )
    extra_key = jnp.einsum(
        "ra,rc->ac",
        table_cols,
        lax.dynamic_slice_in_dim(rel_key_low, col_start, col_count, 1),
        preferred_element_type=jnp.float32,
    )
    key_rows = lax.dynamic_slice_in_dim(rel_key_low, table_start, table_count, 0)
    query_rows = lax.dynamic_slice_in_dim(rel_query_low, table_start, table_count, 0)
    table_share = jnp.einsum(
        "re,ce->rc",
        key_rows,
        lax.dynamic_slice_in_dim(w_key, col_start, col_count, 0),
        preferred_element_type=jnp.float32,
    )
    table_share = table_share + jnp.einsum(
        "re,ce->rc",
        query_rows,
        lax.dynamic_slice_in_dim(w_query, col_start, col_count, 0),
        preferred_element_type=jnp.float32,
    )
    band_rows = (
        lax.all_gather(
            (over_both[0] + extra_query).astype(jnp.bfloat16), "seq", axis=1, tiled=True
        ).astype(jnp.float32),
        lax.all_gather(
            (over_both[1] + extra_key).astype(jnp.bfloat16), "seq", axis=1, tiled=True
        ).astype(jnp.float32),
        lax.all_gather(over_both[2].astype(jnp.bfloat16), "seq", axis=1, tiled=True).astype(
            jnp.float32
        ),
        lax.all_gather(over_both[3].astype(jnp.bfloat16), "seq", axis=1, tiled=True).astype(
            jnp.float32
        ),
        lax.all_gather(over_both[4].astype(jnp.bfloat16), "seq", axis=1, tiled=True).astype(
            jnp.float32
        ),
        lax.all_gather(over_both[5].astype(jnp.bfloat16), "seq", axis=1, tiled=True).astype(
            jnp.float32
        ),
        lax.all_gather(table_share.astype(jnp.bfloat16), "seq", axis=1, tiled=True).astype(
            jnp.float32
        ),
    )
    gathered = (
        lax.all_gather(band_rows[0].astype(jnp.bfloat16), "rows", axis=0, tiled=True).astype(
            jnp.float32
        ),
        lax.all_gather(band_rows[1].astype(jnp.bfloat16), "rows", axis=0, tiled=True).astype(
            jnp.float32
        ),
        lax.all_gather(band_rows[2].astype(jnp.bfloat16), "rows", axis=0, tiled=True).astype(
            jnp.float32
        ),
        lax.all_gather(band_rows[3].astype(jnp.bfloat16), "rows", axis=0, tiled=True).astype(
            jnp.float32
        ),
        lax.all_gather(band_rows[4].astype(jnp.bfloat16), "rows", axis=0, tiled=True).astype(
            jnp.float32
        ),
        lax.all_gather(band_rows[5].astype(jnp.bfloat16), "rows", axis=0, tiled=True).astype(
            jnp.float32
        ),
        lax.all_gather(band_rows[6].astype(jnp.bfloat16), "rows", axis=0, tiled=True).astype(
            jnp.float32
        ),
    )
    return (
        layer_out,
        tokens_grad,
        gathered[0],
        gathered[1],
        gathered[2],
        gathered[3],
        gathered[4],
        gathered[5],
        gathered[6],
        shared[2],
        shared[3],
        shared[4],
        shared[5],
    )


def solution(mesh):
    placed = (
        P("rows", "seq", None),
        P("rows", "seq", None),
        P(),
        P(),
        P(),
        P(),
        P(),
        P(),
        P(),
        P(),
        P(),
        P(),
        P(),
        P("rows", None),
        P("rows", None),
        P(),
    )
    return jax.shard_map(
        shards,
        mesh=mesh,
        in_specs=placed,
        out_specs=(
            P("rows", "seq", None),
            P("rows", "seq", None),
            P(),
            P(),
            P(),
            P(),
            P(),
            P(),
            P(),
            P(),
            P(),
            P(),
            P(),
        ),
        check_vma=False,
    )
```

profile of v0, /device:TPU:0, one launch (start us, length us, event | category | flops | bytes accessed | tf_op | source)
XLA Modules:
  0.0 1900.5 jit_solution(16611510371407561699)
XLA Ops:
  12.0 6.4 collective-permute-start
  21.4 3.5 gather_fusion
  30.8 3.7 convolution_bitcast_fusion.1
  34.5 6.6 copy.126
  41.1 10.0 pad.34.clone
  51.0 23.0 %reshape.834 = f32[1,12,261888]{2,0,1:T(1,128)} reshape(f32[1,12,256,1023]{3,2,0,1:T(8,128)} %pad.34.clone) | data formatting | bytes 25141248 | tf_op jit(solution)/shard_map/while/body/eval_jaxpr/reshape | solution.py:67
  74.0 39.2 %slice_reduce_fusion.1 = f32[12,261632]{1,0:T(8,128)} fusion(f32[1,12,261888]{2,0,1:T(1,128)} %reshape.834), kind=kLoop, calls=%fused_computation.3 | loop fusion | bytes 25116672 | tf_op jit(solution)/shard_map/while/body/eval_jaxpr/slice | solution.py:69
  113.3 22.5 %reshape.835 = f32[1,12,256,1022]{3,2,0,1:T(8,128)} reshape(f32[12,261632]{1,0:T(8,128)} %slice_reduce_fusion.1) | data formatting | bytes 25116672 | tf_op jit(solution)/shard_map/while/body/eval_jaxpr/reshape | solution.py:70
  143.2 7.9 convolution_bitcast_fusion
  151.1 19.0 copy.125
  170.1 21.0 %pad.35.clone = f32[1,12,768,1023]{3,2,0,1:T(8,128)} pad(f32[1,12,768,512]{3,2,0,1:T(8,128)} %copy.125, f32[]{:T(128)} %constant.65.clone.1), padding=0_0x0_0x0_0x256_255 | pad | bytes 56586244 | tf_op jit(solution)/shard_map/while/body/eval_jaxpr/jit(_pad)/pad | solution.py:66
  191.1 65.1 %reshape.837 = f32[1,12,785664]{2,0,1:T(1,128)} reshape(f32[1,12,768,1023]{3,2,0,1:T(8,128)} %pad.35.clone) | data formatting | bytes 75423744 | tf_op jit(solution)/shard_map/while/body/eval_jaxpr/reshape | solution.py:67
  256.2 117.7 %slice_reduce_fusion = f32[12,784896]{1,0:T(8,128)} fusion(f32[1,12,785664]{2,0,1:T(1,128)} %reshape.837), kind=kLoop, calls=%fused_computation.1 | loop fusion | bytes 75350016 | tf_op jit(solution)/shard_map/while/body/eval_jaxpr/slice | solution.py:69
  374.0 61.6 %reshape.838 = f32[1,12,768,1022]{3,2,0,1:T(8,128)} reshape(f32[12,784896]{1,0:T(8,128)} %slice_reduce_fusion) | data formatting | bytes 75350016 | tf_op jit(solution)/shard_map/while/body/eval_jaxpr/reshape | solution.py:70
  435.6 8.0 slice.83
  443.6 9.6 copy.124
  453.2 8.1 fusion.116
  463.4 2.8 copy-done.2
  466.2 3.4 fusion.50
  470.6 8.0 multiply_convert_fusion.2
  485.9 3.7 convolution_convert_fusion.1
  489.7 5.3 convolution_convert_fusion
  499.8 6.4 multiply_reduce_fusion
  509.0 5.7 fusion.6
  516.9 3.7 fusion.5
  520.6 6.4 reshape.846
  527.0 6.5 pad.36
  533.5 15.4 reshape.847
  548.9 6.6 copy.127
  555.5 10.1 pad.37.clone
  565.6 34.0 %reshape.850 = bf16[1,12,983040]{2,1,0:T(8,128)(2,1)} reshape(bf16[1,12,768,1280]{3,2,1,0:T(8,128)(2,1)} %pad.37.clone) | data formatting | bytes 47185920 | tf_op jit(solution)/shard_map/while/body/eval_jaxpr/reshape | solution.py:79
  599.5 21.3 %pad.38 = bf16[1,12,983808]{2,1,0:T(8,128)(2,1)} pad(bf16[1,12,983040]{2,1,0:T(8,128)(2,1)} %reshape.850, bf16[]{:T(256)} %constant.188.clone.1), padding=0_0x0_0x0_768 | pad | bytes 47204352 | tf_op jit(solution)/shard_map/while/body/eval_jaxpr/jit(_pad)/pad | solution.py:80
  620.8 171.8 %reshape.851 = bf16[1,12,768,1281]{3,2,1,0:T(8,128)(2,1)} reshape(bf16[1,12,983808]{2,1,0:T(8,128)(2,1)} %pad.38) | data formatting | bytes 47222784 | tf_op jit(solution)/shard_map/while/body/eval_jaxpr/reshape | solution.py:81
  792.6 3.9 multiply_convert_fusion.1
  799.2 3.9 fusion.54
  807.1 11.5 fusion
  820.3 5.8 fusion.119
  826.1 3.4 bitcast_add_fusion
  837.7 4.7 collective-permute-start.2
  842.4 16.3 collective-permute-done.3
  858.7 16.9 collective-permute-done.2
  884.3 4.3 copy.120
  888.7 4.3 copy.122
  899.7 4.3 reduce-scatter.41.cloned.1.call-done
  906.2 132.2 %reduce-scatter.45.cloned.1.call-done = bf16[192,384]{1,0:T(8,128)(2,1)} async-done(((bf16[3072,384]{1,0:T(8,128)(2,1)}), bf16[192,384]{1,0:T(8,128)(2,1)}) %reduce-scatter.45.cloned.1.call-update) | async-done | bytes 147472
  1038.4 132.9 %reduce-scatter.47.cloned.1.call-done = bf16[48,1536]{1,0:T(8,128)(2,1)} async-done(((bf16[768,1536]{1,0:T(8,128)(2,1)}), bf16[48,1536]{1,0:T(8,128)(2,1)}) %reduce-scatter.47.cloned.1.call-update) | async-done | bytes 147472
  1171.4 7.9 fusion.120
  1181.2 84.6 %all-reduce.8 = (bf16[512,768]{0,1:T(8,128)(2,1)}, bf16[512,768]{0,1:T(8,128)(2,1)}, f32[768]{0:T(1024)}, f32[768]{0:T(1024)}, f32[768]{0:T(1024)}, /*index=5*/f32[768]{0:T(1024)}) all-reduce(f32[512,768]{0,1:T(8,128)} %bitcast.261, f32[512,768]{0,1:T(8,128)} %bitcast.262, ...), channel_id=1, replica_groups=mesh['rows'=2,'seq'=16] {'rows','seq'}, use_global_device_ids=true, to_apply=%region_16.17 | all-reduce | flops 789504 | bytes 4743168 | tf_op jit(solution)/shard_map/psum | solution.py:324
  1265.8 32.5 %reduce-scatter.25.cloned.1.call-done = bf16[384,48]{0,1:T(8,128)(2,1)} async-done(((bf16[384,768]{0,1:T(8,128)(2,1)}), bf16[384,48]{0,1:T(8,128)(2,1)}) %reduce-scatter.25.cloned.1.call-update) | async-done | bytes 36880 | tf_op jit(solution)/shard_map/reduce_scatter | solution.py:361
  1299.3 44.9 %all_gather.42 = bf16[384,768]{0,1:T(8,128)(2,1)} all-gather(bf16[384,48]{0,1:T(8,128)(2,1)S(1)} %fusion.57), channel_id=1, replica_groups=mesh['rows'=2,'seq'=16] {'seq'}, dimensions={1}, use_global_device_ids=true | all-gather | bytes 626688 | tf_op jit(solution)/shard_map/all_gather | solution.py:412
  1344.3 80.7 %reduce-scatter.43.cloned.1.call-done = bf16[48,384]{1,0:T(8,128)(2,1)} async-done(((bf16[768,384]{1,0:T(8,128)(2,1)}), bf16[48,384]{1,0:T(8,128)(2,1)}) %reduce-scatter.43.cloned.1.call-update) | async-done | bytes 36880
  1424.9 45.2 %all_gather.48 = bf16[384,768]{0,1:T(8,128)(2,1)} all-gather(bf16[384,48]{0,1:T(8,128)(2,1)} %bitcast.278), channel_id=1, replica_groups=mesh['rows'=2,'seq'=16] {'seq'}, dimensions={1}, use_global_device_ids=true | all-gather | bytes 626688 | tf_op jit(solution)/shard_map/all_gather | solution.py:421
  1470.2 80.8 %reduce-scatter.27.cloned.1.call-done = bf16[384,48]{0,1:T(8,128)(2,1)} async-done(((bf16[384,768]{0,1:T(8,128)(2,1)}), bf16[384,48]{0,1:T(8,128)(2,1)}) %reduce-scatter.27.cloned.1.call-update) | async-done | bytes 36880 | tf_op jit(solution)/shard_map/reduce_scatter | solution.py:364
  1552.0 44.8 %all_gather.44 = bf16[384,768]{0,1:T(8,128)(2,1)} all-gather(bf16[384,48]{0,1:T(8,128)(2,1)S(1)} %fusion.58), channel_id=1, replica_groups=mesh['rows'=2,'seq'=16] {'seq'}, dimensions={1}, use_global_device_ids=true | all-gather | bytes 626688 | tf_op jit(solution)/shard_map/all_gather | solution.py:415
  1596.9 81.1 %reduce-scatter.29.cloned.1.call-done = bf16[384,48]{0,1:T(8,128)(2,1)} async-done(((bf16[384,768]{0,1:T(8,128)(2,1)}), bf16[384,48]{0,1:T(8,128)(2,1)}) %reduce-scatter.29.cloned.1.call-update) | async-done | bytes 36880 | tf_op jit(solution)/shard_map/reduce_scatter | solution.py:367
  1677.9 46.2 %all_gather.46 = bf16[384,768]{0,1:T(8,128)(2,1)} all-gather(bf16[384,48]{0,1:T(8,128)(2,1)} %reduce-scatter.29.cloned.1.call-done), channel_id=1, replica_groups=mesh['rows'=2,'seq'=16] {'seq'}, dimensions={1}, use_global_device_ids=true | all-gather | bytes 626688 | tf_op jit(solution)/shard_map/all_gather | solution.py:418
  1724.2 19.2 %all-gather.17.cloned.1.call-done = bf16[384,3072]{0,1:T(8,128)(2,1)} async-done(((bf16[384,192]{0,1:T(8,128)(2,1)}), bf16[384,3072]{0,1:T(8,128)(2,1)}) %all-gather.17.cloned.1.call-update) | async-done | bytes 2359312 | tf_op jit(solution)/shard_map/all_gather | solution.py:424
  1743.5 63.7 %all-gather.21.cloned.1.call-done = bf16[1536,768]{0,1:T(8,128)(2,1)} async-done(((bf16[1536,48]{0,1:T(8,128)(2,1)}), bf16[1536,768]{0,1:T(8,128)(2,1)}) %all-gather.21.cloned.1.call-update) | async-done | bytes 2359312 | tf_op jit(solution)/shard_map/all_gather | solution.py:427
  1808.7 41.0 %all_gather.54 = bf16[256,768]{0,1:T(8,128)(2,1)S(1)} all-gather(bf16[256,48]{0,1:T(8,128)(2,1)S(1)} %fusion.59), channel_id=1, replica_groups=mesh['rows'=2,'seq'=16] {'seq'}, dimensions={1}, use_global_device_ids=true | all-gather | bytes 417792 | tf_op jit(solution)/shard_map/all_gather | solution.py:430
  1849.7 2.9 all_gather.55
  1863.8 2.8 copy.106
  1869.4 7.4 copy.109
  1876.8 9.3 all-gather.23.cloned.1.call-done
  1886.1 7.4 copy.110
  (270 shorter events, 94.3 us)
Async XLA Ops:
  7.2 12.9 copy-start
  7.2 877.1 %reduce-scatter.33.cloned.1.call-start = ((), (), s32[]{:S(2)}) async-start(), calls=%async_computation.20 | async-start | bytes 7077888 | tf_op jit(solution)/shard_map/reduce_scatter | solution.py:353
  8.9 9.5 copy-start.31
  8.9 9.5 copy-start.35
  9.0 11.0 copy-start.37
  10.7 126.5 %collective-permute-start.1 = (bf16[1,256,1536]{2,1,0:T(8,128)(2,1)}, bf16[1,256,1536]{2,1,0:T(8,128)(2,1)}, u32[]{:S(2)}, u32[]{:S(2)}) collective-permute-start(bf16[1,256,1536]{2,1,0:T(8,128)(2,1)} %fusion.28), channel_id=1, source_target_pairs={{1,0},{2,1},{3,2},{4,3},{5,4},{6,5},{7,6},{8,7},{9,8},{10,9},{11,1... | collective-permute-start | bytes 2359304 | tf_op jit(solution)/shard_map/ppermute | solution.py:26
  12.0 125.2 %collective-permute-start = (bf16[1,256,1536]{2,1,0:T(8,128)(2,1)}, bf16[1,256,1536]{2,1,0:T(8,128)(2,1)}, u32[]{:S(2)}, u32[]{:S(2)}) collective-permute-start(bf16[1,256,1536]{2,1,0:T(8,128)(2,1)} %fusion.28), channel_id=1, source_target_pairs={{0,1},{1,2},{2,3},{3,4},{4,5},{5,6},{6,7},{7,8},{8,9},{9,10},{10,1... | collective-permute-start | bytes 2359304 | tf_op jit(solution)/shard_map/ppermute | solution.py:23
  20.8 4.2 copy-start.34
  24.9 5.7 copy-start.55
  30.8 422.4 %copy-start.10 = (bf16[256,768]{0,1:T(8,128)(2,1)}, bf16[256,768]{0,1:T(8,128)(2,1)S(1)}, u32[]{:S(2)}) copy-start(bf16[256,768]{0,1:T(8,128)(2,1)S(1)} %copy.90) | copy-start | bytes 1179652
  113.2 22.5 %copy-start.57 = (s32[1,4]{1,0:T(1,128)S(1)}, s32[1,4]{1,0:T(1,128)}, u32[]{:S(2)}) copy-start(s32[1,4]{1,0:T(1,128)} %param.29) | copy-start | bytes 52
  113.2 22.7 %copy-start.50 = (s32[1,4096]{1,0:T(1,128)S(1)}, s32[1,4096]{1,0:T(1,128)}, u32[]{:S(2)}) copy-start(s32[1,4096]{1,0:T(1,128)} %param.30) | copy-start | bytes 49156
  443.6 9.6 copy-start.33
  461.4 4.8 copy-start.2
  461.4 4.8 copy-start.40
  461.4 4.8 copy-start.15
  461.4 9.1 slice-start.8
  463.4 6.3 copy-start.43
  466.2 4.3 slice-start.9
  466.2 12.4 slice-start.6
  469.6 8.9 copy-start.28
  470.6 8.0 slice-start.7
  489.7 399.0 %reduce-scatter.35.cloned.1.call-start = ((), (), s32[]{:S(2)}) async-start(), calls=%async_computation.23 | async-start | bytes 7077888 | tf_op jit(solution)/shard_map/reduce_scatter | solution.py:356
  495.1 398.0 %reduce-scatter.37.cloned.1.call-start = ((), (), s32[]{:S(2)}) async-start(), calls=%async_computation.26 | async-start | bytes 1769472
  499.8 7.7 copy-start.17
  508.1 6.6 copy-start.18
  509.0 6.0 slice-start
  509.0 7.4 slice-start.1
  509.0 7.9 slice-start.2
  792.6 5.6 copy-start.25
  803.1 3.9 copy-start.21
  807.0 11.6 copy-start.9
  807.1 11.6 copy-start.29
  807.1 88.2 %reduce-scatter.31.cloned.1.call-start = ((), (), s32[]{:S(2)}) async-start(), calls=%async_computation.18 | async-start | bytes 1769472 | tf_op jit(solution)/shard_map/reduce_scatter | solution.py:350
  807.1 11.5 copy-start.48
  820.3 5.8 copy-start.11
  820.3 9.2 slice-start.3
  820.3 9.2 slice-start.4
  834.7 62.9 %reduce-scatter.39.cloned.1.call-start = ((), (), s32[]{:S(2)}) async-start(), calls=%async_computation.27 | async-start | bytes 1769472
  834.7 40.9 %copy-start.4 = (f32[1,768,12,64]{1,3,2,0:T(8,128)S(1)}, f32[1,768,12,64]{1,3,2,0:T(8,128)}, u32[]{:S(2)}) copy-start(f32[1,768,12,64]{1,3,2,0:T(8,128)} %copy-done.3) | copy-start | bytes 7077892
  836.4 22.3 %collective-permute-start.3 = (bf16[1,256,1536]{1,2,0:T(8,128)(2,1)S(1)}, bf16[1,256,1536]{1,2,0:T(8,128)(2,1)S(1)}, u32[]{:S(2)}, u32[]{:S(2)}) collective-permute-start(bf16[1,256,1536]{1,2,0:T(8,128)(2,1)S(1)} %get-tuple-element.158), channel_id=1, source_target_pairs={{1,0},{2,1},{3,2},{4,3},{5,4},{6,5},{7,6},{8,7},{9,8},{10,9},{11,1... | collective-permute-start | bytes 2359304 | tf_op jit(solution)/shard_map/ppermute | solution.py:34
  837.7 39.3 %copy-start.14 = (bf16[1,256,768]{2,1,0:T(8,128)(2,1)S(1)}, bf16[1,256,768]{2,1,0:T(8,128)(2,1)}, u32[]{:S(2)}) copy-start(bf16[1,256,768]{2,1,0:T(8,128)(2,1)} %param.16) | copy-start | bytes 1179652
  837.7 37.9 %collective-permute-start.2 = (bf16[1,256,1536]{1,2,0:T(8,128)(2,1)S(1)}, bf16[1,256,1536]{1,2,0:T(8,128)(2,1)S(1)}, u32[]{:S(2)}, u32[]{:S(2)}) collective-permute-start(bf16[1,256,1536]{1,2,0:T(8,128)(2,1)S(1)} %get-tuple-element.157), channel_id=1, source_target_pairs={{0,1},{1,2},{2,3},{3,4},{4,5},{5,6},{6,7},{7,8},{8,9},{9,10},{10,1... | collective-permute-start | bytes 2359304 | tf_op jit(solution)/shard_map/ppermute | solution.py:34
  881.8 22.2 %reduce-scatter.41.cloned.1.call-start = ((), (), s32[]{:S(2)}) async-start(), calls=%async_computation.28 | async-start | bytes 1769472
  884.2 154.1 %reduce-scatter.45.cloned.1.call-start = ((), (), s32[]{:S(2)}) async-start(), calls=%async_computation.30 | async-start | bytes 2506752
  888.6 282.7 %reduce-scatter.47.cloned.1.call-start = ((), (), s32[]{:S(2)}) async-start(), calls=%async_computation.31 | async-start | bytes 2506752
  893.0 405.3 %reduce-scatter.25.cloned.1.call-start = ((), (), s32[]{:S(2)}) async-start(), calls=%async_computation.12 | async-start | bytes 626688 | tf_op jit(solution)/shard_map/reduce_scatter | solution.py:361
  895.2 529.7 %reduce-scatter.43.cloned.1.call-start = ((), (), s32[]{:S(2)}) async-start(), calls=%async_computation.29 | async-start | bytes 626688
  897.5 653.5 %reduce-scatter.27.cloned.1.call-start = ((), (), s32[]{:S(2)}) async-start(), calls=%async_computation.14 | async-start | bytes 626688 | tf_op jit(solution)/shard_map/reduce_scatter | solution.py:364
  899.7 778.2 %reduce-scatter.29.cloned.1.call-start = ((), (), s32[]{:S(2)}) async-start(), calls=%async_computation.16 | async-start | bytes 626688 | tf_op jit(solution)/shard_map/reduce_scatter | solution.py:367
  906.1 837.3 %all-gather.17.cloned.1.call-start = ((), (), s32[]{:S(2)}) async-start(), calls=%async_computation.21 | async-start | bytes 2506752 | tf_op jit(solution)/shard_map/all_gather | solution.py:424
  1038.4 768.8 %all-gather.21.cloned.1.call-start = ((), (), s32[]{:S(2)}) async-start(), calls=%async_computation.24 | async-start | bytes 2506752 | tf_op jit(solution)/shard_map/all_gather | solution.py:427
  1171.4 687.0 %all-gather.9.cloned.1.call-start = ((), (), s32[]{:S(2)}) async-start(), calls=%async_computation.13 | async-start | bytes 1769472 | tf_op jit(solution)/shard_map/all_gather | solution.py:435
  1171.4 7.9 copy-start.7
  1179.4 118.9 %copy-start.36 = (bf16[512,768]{1,0:T(8,128)(2,1)S(1)}, bf16[512,768]{1,0:T(8,128)(2,1)}, u32[]{:S(2)}) copy-start(bf16[512,768]{1,0:T(8,128)(2,1)} %param.24) | copy-start | bytes 2359300
  1344.2 516.8 %all-gather.15.cloned.1.call-start = ((), (), s32[]{:S(2)}) async-start(), calls=%async_computation.19 | async-start | bytes 1769472 | tf_op jit(solution)/shard_map/all_gather | solution.py:444
  1470.1 393.7 %all-gather.11.cloned.1.call-start = ((), (), s32[]{:S(2)}) async-start(), calls=%async_computation.15 | async-start | bytes 1769472 | tf_op jit(solution)/shard_map/all_gather | solution.py:438
  1596.8 211.7 %copy-start.39 = (bf16[512,768]{0,1:T(8,128)(2,1)S(1)}, bf16[512,768]{0,1:T(8,128)(2,1)}, u32[]{:S(2)}) copy-start(bf16[512,768]{0,1:T(8,128)(2,1)} %get-tuple-element.143) | copy-start | bytes 2359300
  1596.8 269.8 %all-gather.13.cloned.1.call-start = ((), (), s32[]{:S(2)}) async-start(), calls=%async_computation.17 | async-start | bytes 1769472 | tf_op jit(solution)/shard_map/all_gather | solution.py:441
  1724.2 145.2 %all-gather.19.cloned.1.call-start = ((), (), s32[]{:S(2)}) async-start(), calls=%async_computation.22 | async-start | bytes 7077888 | tf_op jit(solution)/shard_map/all_gather | solution.py:447
  1743.4 142.7 %all-gather.23.cloned.1.call-start = ((), (), s32[]{:S(2)}) async-start(), calls=%async_computation.25 | async-start | bytes 7077888 | tf_op jit(solution)/shard_map/all_gather | solution.py:450
  1807.2 47.9 %copy-start.22 = (bf16[1,256,12,64]{1,3,2,0:T(8,128)(2,1)S(1)}, bf16[1,256,12,64]{1,3,2,0:T(8,128)(2,1)}, u32[]{:S(2)}) copy-start(bf16[1,256,12,64]{1,3,2,0:T(8,128)(2,1)} %copy-done.21) | copy-start | bytes 1179652
  1807.2 47.9 %copy-start.49 = (f32[256]{0:T(256)S(1)}, f32[256]{0:T(256)}, u32[]{:S(2)}) copy-start(f32[256]{0:T(256)} %copy-done.47) | copy-start | bytes 3076
  1849.6 6.0 copy-start.24
  (28 other events, 52.9 us)
Sparse Core Ops, SparseCore 0:
  489.8 14.2 reduce-scatter.32
  506.5 13.7 reduce-scatter.34
  807.2 10.7 reduce-scatter.36
  834.8 10.7 reduce-scatter.30
  881.9 9.3 reduce-scatter.38
  894.1 9.8 reduce-scatter.40
  909.5 128.8 reduce-scatter.44
  1044.6 126.7 reduce-scatter.46
  1176.0 122.1 reduce-scatter.24
  1303.5 121.3 reduce-scatter.42
  1429.6 121.3 reduce-scatter.26
  1556.8 121.0 reduce-scatter.28
  1680.7 62.6 all-gather.16
  1746.1 61.0 all-gather.20
  1808.6 8.0 all-gather.8
  1818.0 10.3 all-gather.14
  1829.8 10.3 all-gather.10
  1841.6 10.6 all-gather.12
  1853.9 15.1 all-gather.18
  1870.4 15.6 all-gather.22
where the time goes:
time: 1910 us; the launch traced here: 1900 us
  local copies, waits for them, and re-layouts  759 us (40%)
  waiting for transfers between devices  670 us (35%)
  blocking collectives  309 us (16%)
  matrix products  116 us (6%)
    unnamed x26, waiting for transfers between devices  350 us
    reshape x2, local copies, waits for them, and re-layouts, unshift_cols(): return flat.reshape(lead_dims + (row_count, pad_width + 1))[..., :cols_out]  187 us
    slice x2, local copies, waits for them, and re-layouts, shift_cols(): taken = flat[..., shift_start:shift_start + row_count * (pad_width - 1)]  157 us
    unnamed x157, local copies, waits for them, and re-layouts  108 us
    reshape x2, local copies, waits for them, and re-layouts, shift_cols(): flat = padded.reshape(lead_dims + (row_count * pad_width,))  88 us
    psum x1, blocking collectives, shards(): lax.psum((rel_key_sum, rel_query_sum, mid_gain_part, mid_bias_part, end_g...  84.6 us
    reshape x2, local copies, waits for them, and re-layouts, shift_cols(): return taken.reshape(lead_dims + (row_count, pad_width - 1))[..., :cols_out]  84.1 us
    reduce_scatter x1, waiting for transfers between devices, shards(): lax.psum_scatter(over_rows[2].astype(jnp.bfloat16), 'seq', scatter_dimens...  81.1 us
  transfers between devices with their start and end apart: 24, of which 12 were waited for; matrix products, arithmetic and copies ran while one was open for 27% of the time, Pallas kernels for 0%

commit v1 on v0

v1 whole, which is shorter than its diff:
```python
import functools
import math

import jax
import jax.numpy as jnp
from jax import lax
from jax.experimental import pallas as pl
from jax.experimental.pallas import tpu as pltpu
from jax.sharding import PartitionSpec as P

H = 12
DH = 64
SPAN = 256
TILE = 128
REACH = 640
PAIR = 128
score_scale = 1.0 / math.sqrt(3 * DH)


def nt(left, right):
    return lax.dot_general(left, right, (((1,), (1,)), ((), ())), preferred_element_type=jnp.float32)


def nn(left, right):
    return lax.dot_general(left, right, (((1,), (0,)), ((), ())), preferred_element_type=jnp.float32)


def head_lanes(values, head):
    lane = lax.broadcasted_iota(jnp.int32, values.shape, 1)
    mine = (lane < DH) if head == 0 else (lane >= DH)
    return jnp.where(mine, values, jnp.zeros_like(values))


def unit(reverse):
    row = lax.broadcasted_iota(jnp.int32, (TILE, TILE), 0)
    col = lax.broadcasted_iota(jnp.int32, (TILE, TILE), 1)
    hit = (row + col == TILE - 1) if reverse else (row == col)
    return jnp.where(hit, 1.0, 0.0).astype(jnp.bfloat16)


def attend_kernel(q_ref, k_ref, vt_ref, relk_ref, relq_ref, bias_ref, attn_ref, prob_ref, score_ref):
    eye = unit(False)
    log_two = score_scale * math.log2(math.e)
    tiles = q_ref.shape[0] // TILE
    for tile in range(tiles):
        first = tile * TILE
        q_tile = q_ref[pl.ds(first, TILE), :]
        for head in range(2):
            q_head = head_lanes(q_tile, head)
            band = nt(q_head, relk_ref[...])
            band = jnp.concatenate([band, jnp.zeros((TILE, REACH - 2 * SPAN), jnp.float32)], axis=1)
            to_term = pltpu.roll(band, 0, 1, stride=1, stride_axis=0).astype(jnp.bfloat16)
            for part in range(REACH // TILE):
                at = first + part * TILE
                k_part = k_ref[pl.ds(at, TILE), :]
                window = relq_ref[pl.ds((REACH // TILE - 1 - part) * TILE, 2 * TILE), :]
                from_band = nt(head_lanes(k_part, head), window)
                from_term = pltpu.roll(from_band, TILE + 1, 1, stride=1, stride_axis=0)[:, :TILE]
                left = jnp.concatenate([k_part, eye], axis=1)
                right = jnp.concatenate(
                    [q_head, to_term[:, part * TILE : (part + 1) * TILE]], axis=1
                )
                score_ref[pl.ds(part * TILE, TILE), :] = (
                    nt(left, right) + from_term + bias_ref[pl.ds(at, TILE), pl.ds(first, TILE)]
                )
            scores = score_ref[...]
            top = jnp.max(scores, axis=0, keepdims=True)
            weights = jnp.exp2((scores - top) * log_two)
            total = jnp.sum(weights, axis=0, keepdims=True)
            probs = (weights * (1.0 / total)).astype(jnp.bfloat16)
            prob_ref[head, tile] = probs
            out = nn(vt_ref[pl.ds(head * DH, DH), pl.ds(first, REACH)], probs)
            attn_ref[pl.ds(head * DH, DH), pl.ds(first, TILE)] = out.astype(attn_ref.dtype)


def attend(query, key_ext, value_ext_t, relk, relq, bias):
    block_len, width = query.shape
    ext_len = key_ext.shape[0]
    tiles = block_len // TILE
    pairs = width // PAIR
    return pl.pallas_call(
        attend_kernel,
        grid=(pairs,),
        in_specs=[
            pl.BlockSpec((block_len, PAIR), lambda p: (0, p)),
            pl.BlockSpec((ext_len, PAIR), lambda p: (0, p)),
            pl.BlockSpec((PAIR, ext_len), lambda p: (p, 0)),
            pl.BlockSpec((2 * SPAN, PAIR), lambda p: (0, p)),
            pl.BlockSpec((2 * SPAN + 2 * TILE, PAIR), lambda p: (0, p)),
            pl.BlockSpec((ext_len, block_len), lambda p: (0, 0)),
        ],
        out_specs=[
            pl.BlockSpec((PAIR, block_len), lambda p: (p, 0)),
            pl.BlockSpec((2, tiles, REACH, TILE), lambda p: (p, 0, 0, 0)),
        ],
        out_shape=[
            jax.ShapeDtypeStruct((width, block_len), jnp.bfloat16),
            jax.ShapeDtypeStruct((2 * pairs, tiles, REACH, TILE), jnp.bfloat16),
        ],
        scratch_shapes=[pltpu.VMEM((REACH, TILE), jnp.float32)],
        compiler_params=pltpu.CompilerParams(vmem_limit_bytes=48 * 2**20),
        name="attend",
    )(query, key_ext, value_ext_t, relk, relq, bias)


def attend_back_kernel(
    q_ref, k_ref, v_ref, grad_ref, prob_ref, relk_ref, relq_ref,
    dq_ref, dk_ref, dv_ref, drelk_ref, drelq_ref, qt_ref, kt_ref,
):
    swap = unit(True)
    for source, result in ((q_ref, qt_ref), (k_ref, kt_ref)):
        for at in range(0, source.shape[0], TILE):
            flipped = nn(swap, source[pl.ds(at, TILE), :])
            result[:, pl.ds(at, TILE)] = flipped.T.astype(jnp.bfloat16)
    row = lax.broadcasted_iota(jnp.int32, (TILE, TILE), 0)
    col = lax.broadcasted_iota(jnp.int32, (TILE, TILE), 1)
    parts = REACH // TILE
    tiles = q_ref.shape[0] // TILE
    dk_ref[...] = jnp.zeros_like(dk_ref)
    dv_ref[...] = jnp.zeros_like(dv_ref)
    drelk_ref[...] = jnp.zeros_like(drelk_ref)
    drelq_ref[...] = jnp.zeros_like(drelq_ref)
    for tile in range(tiles):
        first = tile * TILE
        q_tile = q_ref[pl.ds(first, TILE), :]
        grad_tile = grad_ref[pl.ds(first, TILE), :]
        v_tile = v_ref[pl.ds(first, REACH), :]
        q_heads = [head_lanes(q_tile, head) for head in range(2)]
        grad_heads = [head_lanes(grad_tile, head) for head in range(2)]
        dq_heads = []
        lefts = [[] for _ in range(parts)]
        for head in range(2):
            lanes = pl.ds(head * DH, DH)
            probs = prob_ref[head, tile].astype(jnp.float32)
            weighted = probs * nt(v_tile, grad_heads[head])
            delta = jnp.sum(weighted, axis=0, keepdims=True)
            dscore = ((weighted - probs * delta) * score_scale).astype(jnp.bfloat16)
            turned = nt(swap, dscore)
            dband = pltpu.roll(turned, REACH - TILE + 1, 1, stride=1, stride_axis=0)
            dband = dband[:, : 2 * SPAN].astype(jnp.bfloat16)
            dq_heads.append(
                nn(turned.astype(jnp.bfloat16), k_ref[pl.ds(first, REACH), :])
                + nn(dband, relk_ref[...])
            )
            drelk_ref[lanes, :] += nn(qt_ref[lanes, pl.ds(first, TILE)], dband)
            for part in range(parts):
                flipped = nn(swap, dscore[part * TILE : (part + 1) * TILE, :])
                spun = pltpu.roll(flipped, 0, 1, stride=1, stride_axis=0)
                low = jnp.where(col >= row, spun, 0.0)
                dfrom = jnp.concatenate([low, spun - low], axis=1).astype(jnp.bfloat16)
                window = pl.ds((parts - 1 - part) * TILE, 2 * TILE)
                drelq_ref[lanes, window] += nn(kt_ref[lanes, pl.ds(first + part * TILE, TILE)], dfrom)
                lefts[part] += [flipped.astype(jnp.bfloat16), dfrom]
        dq_turned = jnp.where(col < DH, dq_heads[0], dq_heads[1]).astype(jnp.bfloat16)
        dq_ref[pl.ds(first, TILE), :] = nn(swap, dq_turned).astype(dq_ref.dtype)
        dv_ref[pl.ds(first, REACH), :] += nn(
            jnp.concatenate([prob_ref[0, tile], prob_ref[1, tile]], axis=1),
            jnp.concatenate(grad_heads, axis=0),
        )
        for part in range(parts):
            window = relq_ref[pl.ds((parts - 1 - part) * TILE, 2 * TILE), :]
            right = jnp.concatenate(
                [q_heads[0], head_lanes(window, 0), q_heads[1], head_lanes(window, 1)], axis=0
            )
            dk_ref[pl.ds(first + part * TILE, TILE), :] += nn(
                jnp.concatenate(lefts[part], axis=1), right
            )


def attend_back(query, key_ext, value_ext, grad, probs, relk, relq):
    block_len, width = query.shape
    ext_len = key_ext.shape[0]
    tiles = block_len // TILE
    pairs = width // PAIR
    table = 2 * SPAN
    cols = lambda n: pl.BlockSpec((n, PAIR), lambda p: (0, p))
    rows = lambda n: pl.BlockSpec((PAIR, n), lambda p: (p, 0))
    f32 = lambda *s: jax.ShapeDtypeStruct(s, jnp.float32)
    return pl.pallas_call(
        attend_back_kernel,
        grid=(pairs,),
        in_specs=[
            cols(block_len), cols(ext_len), cols(ext_len), cols(block_len),
            pl.BlockSpec((2, tiles, REACH, TILE), lambda p: (p, 0, 0, 0)),
            cols(table), cols(table + 2 * TILE),
        ],
        out_specs=[cols(block_len), cols(ext_len), cols(ext_len), rows(table), rows(table + 2 * TILE)],
        out_shape=[
            jax.ShapeDtypeStruct((block_len, width), jnp.bfloat16),
            f32(ext_len, width), f32(ext_len, width), f32(width, table), f32(width, table + 2 * TILE),
        ],
        scratch_shapes=[
            pltpu.VMEM((PAIR, block_len), jnp.bfloat16), pltpu.VMEM((PAIR, ext_len), jnp.bfloat16),
        ],
        compiler_params=pltpu.CompilerParams(vmem_limit_bytes=48 * 2**20),
        name="attend_back",
    )(query, key_ext, value_ext, grad, probs, relk, relq)


norm_eps = 1e-07
masked_score = -1e30


def shifted(shard, axis, by):
    count = lax.axis_size(axis)
    pairs = [(i, i + by) for i in range(count) if 0 <= i + by < count]
    return lax.ppermute(shard, axis, pairs)


def layer_norm(values, norm_gain, norm_bias):
    centre = values - jnp.mean(values, axis=-1, keepdims=True)
    spread = jnp.mean(centre * centre, axis=-1, keepdims=True)
    return centre * lax.rsqrt(spread + norm_eps) * norm_gain + norm_bias


def f32dot(spec, left, right):
    return jnp.einsum(spec, left, right, preferred_element_type=jnp.float32)


def segment_of(slot_ids, seq_ends):
    return jnp.sum((slot_ids[:, None] >= seq_ends[None, :]).astype(jnp.int32), axis=1)


def mask_bias(seq_lengths, pad_mask, block_len, seq_count):
    ext_len = block_len + 2 * SPAN
    seq_place = lax.axis_index("seq")
    row_len = block_len * seq_count
    seg_ids = jnp.arange(seq_lengths.shape[0], dtype=jnp.int32)
    seq_ends = jnp.sum(
        jnp.where(seg_ids[None, :] <= seg_ids[:, None], seq_lengths[None, :], 0), axis=1
    )
    query_slots = seq_place * block_len + jnp.arange(block_len, dtype=jnp.int32)
    key_slots = seq_place * block_len - SPAN + jnp.arange(ext_len, dtype=jnp.int32)
    seg_query = segment_of(query_slots, seq_ends)
    in_row = (key_slots >= 0) & (key_slots < row_len)
    seg_key = jnp.where(in_row, segment_of(key_slots, seq_ends), -1)
    keep_key = lax.dynamic_slice_in_dim(
        jnp.pad(pad_mask, (SPAN, SPAN)), seq_place * block_len, ext_len, 0
    )
    apart = key_slots[:, None] - query_slots[None, :]
    allowed = (
        (seg_key[:, None] == seg_query[None, :])
        & (jnp.abs(apart) < SPAN)
        & ((keep_key[:, None] == 1) | (apart == 0))
    )
    return jnp.where(allowed, 0.0, masked_score).astype(jnp.float32)


def band_tables(rel_buckets):
    span_ids = jnp.arange(2 * SPAN, dtype=jnp.int32)[None, :]
    back = rel_buckets[::-1]
    to_bucket = jnp.concatenate([back[:1], back[:-1]])
    from_bucket = jnp.concatenate([rel_buckets[1:], rel_buckets[-1:]])
    to_pos = jnp.clip(to_bucket + SPAN, 0, 2 * SPAN - 1)
    from_pos = jnp.clip(SPAN - from_bucket, 0, 2 * SPAN - 1)
    to_hot = (to_pos[:, None] == span_ids).astype(jnp.bfloat16)
    from_hot = (from_pos[:, None] == span_ids).astype(jnp.bfloat16)
    return to_hot, from_hot


def low(values):
    return values.astype(jnp.bfloat16)


def shards(
    tokens, cotangent, w_query, w_key, w_value, w_output, w_inner, w_outer, rel_table,
    mid_gain, mid_bias, end_gain, end_bias, seq_lengths, pad_mask, rel_buckets,
):
    tokens, cotangent = tokens[0], cotangent[0]
    block_len, width = tokens.shape
    seq_count = lax.axis_size("seq")
    prev = shifted(tokens, "seq", 1)
    following = shifted(tokens, "seq", -1)
    bias = mask_bias(seq_lengths[0], pad_mask[0], block_len, seq_count)
    to_hot, from_hot = band_tables(rel_buckets)
    to_table = low(f32dot("mr,re->me", to_hot, rel_table))
    from_table = low(f32dot("mr,re->me", from_hot, rel_table))
    relk = low(f32dot("me,ed->md", to_table, w_key))
    relq = low(f32dot("me,ed->md", from_table, w_query))
    relq = jnp.pad(relq, ((TILE, TILE), (0, 0)))
    query = low(f32dot("te,ed->td", tokens, w_query))
    tokens_ext = jnp.concatenate([prev, tokens, following], axis=0)
    key_ext = low(f32dot("te,ed->td", tokens_ext, w_key))
    value_ext = low(f32dot("te,ed->td", tokens_ext, w_value))
    attn_t, probs = attend(query, key_ext, value_ext.T, relk, relq, bias)

    mixed = f32dot("dt,de->te", attn_t, w_output)
    hidden, mid_back = jax.vjp(layer_norm, tokens.astype(jnp.float32) + mixed, mid_gain, mid_bias)
    hidden_low = low(hidden)
    inner = f32dot("td,df->tf", hidden_low, w_inner)
    active, gelu_back = jax.vjp(functools.partial(jax.nn.gelu, approximate=False), inner)
    active_low = low(active)
    outer = f32dot("tf,fd->td", active_low, w_outer)
    final, end_back = jax.vjp(layer_norm, hidden + outer, end_gain, end_bias)
    layer_out = low(final)
    sum_grad, end_gain_part, end_bias_part = end_back(cotangent.astype(jnp.float32))
    outer_low = low(sum_grad)
    outer_part = low(f32dot("tf,td->fd", active_low, outer_low))
    inner_low = low(gelu_back(f32dot("td,fd->tf", outer_low, w_outer))[0])
    inner_part = low(f32dot("td,tf->df", hidden_low, inner_low))
    hidden_grad = sum_grad + f32dot("tf,df->td", inner_low, w_inner)
    resid_grad, mid_gain_part, mid_bias_part = mid_back(hidden_grad)
    mixed_low = low(resid_grad)
    output_part = low(f32dot("dt,te->de", attn_t, mixed_low))
    attn_grad = low(f32dot("te,de->td", mixed_low, w_output))

    dquery, dkey, dvalue, drelk, drelq = attend_back(
        query, key_ext, value_ext, attn_grad, probs, relk, relq
    )
    pair = jnp.concatenate([dkey, dvalue], axis=1)
    from_next = shifted(low(pair[:SPAN]), "seq", -1).astype(jnp.float32)
    from_prev = shifted(low(pair[SPAN + block_len :]), "seq", 1).astype(jnp.float32)
    pair = low(pair[SPAN : SPAN + block_len] + from_prev + from_next)
    swap = unit(True)
    dkey = low(
        f32dot("ab,nbd->nad", swap, pair[:, :width].reshape(-1, TILE, width))
    ).reshape(block_len, width)
    dvalue = pair[:, width:]
    drelk = low(drelk)
    drelq = low(drelq[:, TILE : TILE + 2 * SPAN])
    query_part = low(f32dot("te,td->ed", tokens, dquery) + f32dot("me,dm->ed", from_table, drelq))
    key_part = low(f32dot("te,td->ed", tokens, dkey) + f32dot("me,dm->ed", to_table, drelk))
    value_part = low(f32dot("te,td->ed", tokens, dvalue))
    table_part = low(
        f32dot("mr,me->re", to_hot, low(f32dot("dm,ed->me", drelk, w_key)))
        + f32dot("mr,me->re", from_hot, low(f32dot("dm,ed->me", drelq, w_query)))
    )
    tokens_grad = low(
        resid_grad
        + f32dot("td,ed->te", dquery, w_query)
        + f32dot("td,ed->te", dkey, w_key)
        + f32dot("td,ed->te", dvalue, w_value)
    )
    norm_parts = lax.psum(
        (mid_gain_part, mid_bias_part, end_gain_part, end_bias_part), ("rows", "seq")
    )
    groups = (
        (outer_part,),
        tuple(inner_part[:, at : at + width] for at in range(0, inner_part.shape[1], width)),
        (query_part, key_part, value_part, output_part, table_part),
    )
    outs = []
    for group in groups:
        packed = jnp.concatenate(group, axis=0)
        share = lax.psum_scatter(packed, ("rows", "seq"), scatter_dimension=0, tiled=True)
        whole = lax.all_gather(share, ("rows", "seq"), axis=0, tiled=True).astype(jnp.float32)
        pieces, at = [], 0
        for piece in group:
            pieces.append(whole[at : at + piece.shape[0]])
            at += piece.shape[0]
        outs.append(pieces)
    (outer_w,), inner_w, (query_w, key_w, value_w, output_w, table_w) = outs
    inner_w = jnp.concatenate(inner_w, axis=1)
    return (
        layer_out[None], tokens_grad[None], query_w, key_w, value_w, output_w, inner_w, outer_w,
        table_w, *norm_parts,
    )


def solution(mesh):
    split = P("rows", "seq", None)
    return jax.shard_map(
        shards,
        mesh=mesh,
        in_specs=(split, split) + (P(),) * 11 + (P("rows", None), P("rows", None), P()),
        out_specs=(split, split) + (P(),) * 11,
        check_vma=False,
    )
```

time: 1910 us -> 653 us (0.34)
  local copies, waits for them, and re-layouts: 759 us -> 30.1 us
  blocking collectives: 309 us -> 40.8 us
  waiting for transfers between devices: 670 us -> 412 us
  matrix products: 116 us -> 67.9 us
  Pallas kernels: 0 us -> 47.3 us
    reshape x8 -> x0, local copies, waits for them, and re-layouts: 400 us -> none  [the longest x2 187 us: unshift_cols(): return flat.reshape(lead_dims + (row_count, pad_width + 1))[..., :cols_out]]
    unnamed x26 -> x6, waiting for transfers between devices: 350 us -> 0.1 us
    all_gather x6 -> x0, blocking collectives: 225 us -> none  [the longest x1 46.2 us: shards(): lax.all_gather(over_both[2].astype(jnp.bfloat16), 'seq', axis=1, tiled=True)]
    slice x8, local copies, waits for them, and re-layouts: 172 us -> 15.3 us  [the longest x3 11.7 us: shards(): pieces.append(whole[at:at + piece.shape[0]])]
    unnamed x157 -> x121, local copies, waits for them, and re-layouts: 108 us -> 11.8 us
    pad x5 -> x1, local copies, waits for them, and re-layouts: 68.8 us -> 1.21 us  [shards(): relq = jnp.pad(relq, ((TILE, TILE), (0, 0)))]
    all_gather x8 -> x3, waiting for transfers between devices: 92.2 us -> 142 us  [shards(): lax.all_gather(share, ('rows', 'seq'), axis=0, tiled=True)]
    reduce_scatter x6 -> x3, waiting for transfers between devices: 194 us -> 243 us  [shards(): lax.psum_scatter(packed, ('rows', 'seq'), scatter_dimension=0, tiled=True)]
  transfers between devices with their start and end apart: 24 -> 10, of which waited for: 12 -> 8; matrix products, arithmetic and copies ran while one was open for 27% -> 12% of each run, Pallas kernels for 0% -> 4%
where the time goes in v1:
time: 653 us; the launch traced here: 650 us
  waiting for transfers between devices  412 us (63%)
  matrix products  67.9 us (10%)
  Pallas kernels  47.3 us (7%)
  blocking collectives  40.8 us (6%)
  local copies, waits for them, and re-layouts  30.1 us (5%)
  other arithmetic  22.1 us (3%)
  between operations  15.1 us (2%)
  starting transfers between devices  14.3 us (2%)
    reduce_scatter x3, waiting for transfers between devices, shards(): lax.psum_scatter(packed, ('rows', 'seq'), scatter_dimension=0, tiled=True)  243 us
    all_gather x3, waiting for transfers between devices, shards(): lax.all_gather(share, ('rows', 'seq'), axis=0, tiled=True)  142 us
    dot_general x27, matrix products, f32dot(): return jnp.einsum(spec, left, right, preferred_element_type=jnp.float32)  67.9 us
    psum x1, blocking collectives, shards(): lax.psum((mid_gain_part, mid_bias_part, end_gain_part, end_bias_part), ('...  40.8 us
    pallas_call x1, Pallas kernels, attend_back(): pl.pallas_call(attend_back_kernel, grid=(pairs,), in_specs=[cols(block_le...  28.1 us
    ppermute x4, waiting for transfers between devices, shifted(): return lax.ppermute(shard, axis, pairs)  27.2 us
    pallas_call x1, Pallas kernels, attend(): pl.pallas_call(attend_kernel, grid=(pairs,), in_specs=[pl.BlockSpec((bloc...  19.2 us
    ppermute x4, starting transfers between devices, shifted(): return lax.ppermute(shard, axis, pairs)  14.1 us
  transfers between devices with their start and end apart: 10, of which 8 were waited for; matrix products, arithmetic and copies ran while one was open for 12% of the time, Pallas kernels for 4%

profile of v1, /device:TPU:0, one launch (start us, length us, event | category | flops | bytes accessed | tf_op | source)
XLA Modules:
  0.0 649.8 jit_solution(8190866701839312665)
XLA Ops:
  7.2 5.7 collective-permute-start
  13.0 1.3 collective-permute-start.1
  14.3 0.8 slice.73
  15.0 1.3 slice.72
  16.3 0.8 select_reduce_fusion
  17.4 2.2 convolution_convert_fusion.14.q_ref
  19.7 0.8 fusion.47
  20.5 0.6 copy-done.52
  21.0 1.8 convolution_convert_fusion.10
  22.8 0.9 copy-done.38
  23.7 1.7 convolution_convert_fusion.8
  25.4 1.5 convolution_convert_fusion.11
  27.0 2.0 fusion.28.bias_ref
  28.9 1.2 pad.8.relq_ref
  30.2 2.8 convolution_convert_fusion.9.relk_ref
  33.0 2.2 convolution_convert_fusion.4.v_ref
  35.2 1.5 copy.30.vt_ref
  36.6 2.9 convolution_convert_fusion.5.k_ref
  39.6 19.2 %attend.1 = (bf16[768,256]{1,0:T(8,128)(2,1)S(1)}, bf16[12,2,640,128]{3,2,1,0:T(8,128)(2,1)}) custom-call(bf16[256,768]{1,0:T(8,128)(2,1)S(1)} %copy-done.4, bf16[768,768]{1,0:T(8,128)(2,1)S(1)} %convolution_convert_fusion.5.k_ref, bf16[768,768]{1,0:T(8,128)(2,1)S(1)} %copy-done.3, bf16[512,768]{1,0:T(8,128)(2,1)S(1)} %copy-done.6, ...), custom_call_target="tpu_custom_call" | custom-call | tf_op jit(solution)/shard_map/attend/pallas_call | solution.py:81
  58.8 0.6 fusion.73
  59.7 11.5 %multiply_convert_fusion = (bf16[256,3072]{1,0:T(8,128)(2,1)S(1)}, f32[256,3072]{1,0:T(8,128)}, f32[256,3072]{1,0:T(8,128)}) fusion(bf16[768,3072]{1,0:T(8,128)(2,1)} %param.22, f32[256,768]{1,0:T(8,128)S(1)} %get-tuple-element.58, f32[768]{0:T(1024)S(1)} %copy-done.40, f32[768]{0:T(1024)S(1)} %copy-done.39, f32[256]{0:T(256)S(1)} %fusion.49, ...), kind=kOutput, calls=%fused_computation.7 | convolution fusion | flops 1260060672 | bytes 13377536 | tf_op jit(solution)/shard_map/td,df->tf/dot_general | solution.py:217
  71.3 1.5 fusion.74
  73.5 1.1 fusion.67
  74.6 0.9 copy-done.29
  75.5 3.6 convolution_convert_fusion
  79.3 6.4 add_convert_fusion
  85.7 1.1 copy-done.32
  86.8 1.6 convolution_convert_fusion.1
  88.8 2.5 pad_maximum_fusion.1
  91.3 0.6 copy-done.45
  92.0 5.8 multiply_reduce_fusion
  98.2 0.5 convolution_convert_fusion.13.grad_ref
  99.7 28.1 %attend_back.1 = (bf16[256,768]{1,0:T(8,128)(2,1)S(1)}, f32[768,768]{1,0:T(8,128)}, f32[768,768]{1,0:T(8,128)}, f32[768,512]{1,0:T(8,128)}, f32[768,768]{1,0:T(8,128)}) custom-call(bf16[256,768]{1,0:T(8,128)(2,1)S(1)} %copy-done.5, bf16[768,768]{1,0:T(8,128)(2,1)S(1)} %copy-done.2, bf16[768,768]{1,0:T(8,128)(2,1)S(1)} %convolution_convert_fusion.4.v_ref, ...), custom_call_target="tpu_custom_call" | custom-call | tf_op jit(solution)/shard_map/attend_back/pallas_call | solution.py:179
  127.9 2.2 constant_dynamic-update-slice_fusion.1
  131.0 1.9 copy-done.13
  132.9 1.2 fusion.72
  134.2 5.8 collective-permute-start.2
  139.9 1.3 collective-permute-start.3
  141.3 0.5 fusion.56
  141.8 4.7 fusion.16
  146.5 3.5 fusion.10
  150.0 25.0 %collective-permute-done.2 = bf16[256,1536]{1,0:T(8,128)(2,1)} collective-permute-done((bf16[256,1536]{1,0:T(8,128)(2,1)}, bf16[256,1536]{1,0:T(8,128)(2,1)}, u32[]{:S(2)}, u32[]{:S(2)}) %collective-permute-start.2) | collective-permute-done | bytes 786464 | tf_op jit(solution)/shard_map/ppermute | solution.py:207
  175.0 2.2 collective-permute-done.3
  177.2 2.1 fusion.9
  179.6 0.5 fusion.54
  180.2 0.9 copy-done.31
  181.2 1.8 fusion.11
  183.0 1.5 fusion.14
  184.6 1.6 fusion.12
  186.1 4.6 fusion.15
  190.8 15.2 %reduce-scatter.8.cloned.1.call-done = bf16[96,768]{1,0:T(8,128)(2,1)} async-done(((bf16[3072,768]{1,0:T(8,128)(2,1)}), bf16[96,768]{1,0:T(8,128)(2,1)}) %reduce-scatter.8.cloned.1.call-update) | async-done | bytes 147472 | tf_op jit(solution)/shard_map/reduce_scatter | solution.py:345
  206.1 112.5 %reduce-scatter.6.cloned.1.call-done = bf16[96,768]{1,0:T(8,128)(2,1)} async-done(((bf16[3072,768]{1,0:T(8,128)(2,1)}), bf16[96,768]{1,0:T(8,128)(2,1)}) %reduce-scatter.6.cloned.1.call-update) | async-done | bytes 147472 | tf_op jit(solution)/shard_map/reduce_scatter | solution.py:345
  318.6 115.6 %reduce-scatter.4.cloned.1.call-done = bf16[112,768]{1,0:T(8,128)(2,1)} async-done(((bf16[3584,768]{1,0:T(8,128)(2,1)}), bf16[112,768]{1,0:T(8,128)(2,1)}) %reduce-scatter.4.cloned.1.call-update) | async-done | bytes 172048 | tf_op jit(solution)/shard_map/reduce_scatter | solution.py:345
  434.4 40.8 %all-reduce.2 = (f32[768]{0:T(1024)}, f32[768]{0:T(1024)}, f32[768]{0:T(1024)}, f32[768]{0:T(1024)}) all-reduce(f32[768]{0:T(1024)S(1)} %copy-done.49, f32[768]{0:T(1024)S(1)} %copy-done.50, f32[768]{0:T(1024)S(1)} %get-tuple-element.29, f32[768]{0:T(1024)S(1)} %convert_reduce_fusion), channel_id=1, replica_groups=mesh['rows'=2,'seq'=16] {'rows','seq'}, use_global_device_ids=true, to_apply=%region_15.16 | all-reduce | flops 3072 | bytes 24576 | tf_op jit(solution)/shard_map/psum | solution.py:334
  475.8 0.7 copy-done.34
  477.1 1.3 fusion.18
  478.3 22.1 %all-gather.8.cloned.1.call-done = bf16[3072,768]{1,0:T(8,128)(2,1)} async-done(((bf16[96,768]{1,0:T(8,128)(2,1)}), bf16[3072,768]{1,0:T(8,128)(2,1)}) %all-gather.8.cloned.1.call-update) | async-done | bytes 4718608 | tf_op jit(solution)/shard_map/all_gather | solution.py:346
  500.4 6.8 %convert_element_type.169 = f32[3072,768]{1,0:T(8,128)} convert(bf16[3072,768]{1,0:T(8,128)(2,1)} %all-gather.8.cloned.1.call-done) | non-fusion elementwise | flops 2359296 | bytes 14155776 | tf_op jit(solution)/shard_map/convert_element_type | solution.py:346
  507.2 58.7 %all-gather.6.cloned.1.call-done = bf16[3072,768]{1,0:T(8,128)(2,1)} async-done(((bf16[96,768]{1,0:T(8,128)(2,1)}), bf16[3072,768]{1,0:T(8,128)(2,1)}) %all-gather.6.cloned.1.call-update) | async-done | bytes 4718608 | tf_op jit(solution)/shard_map/all_gather | solution.py:346
  565.9 3.2 fusion.70
  569.1 4.1 pad_maximum_fusion
  573.2 60.9 %all-gather.4.cloned.1.call-done = bf16[3584,768]{1,0:T(8,128)(2,1)} async-done(((bf16[112,768]{1,0:T(8,128)(2,1)}), bf16[3584,768]{1,0:T(8,128)(2,1)}) %all-gather.4.cloned.1.call-update) | async-done | bytes 5505040 | tf_op jit(solution)/shard_map/all_gather | solution.py:346
  634.1 6.2 fusion.69
  640.3 2.4 slice.112
  (153 shorter events, 6.1 us)
Async XLA Ops:
  7.2 10.3 %copy-start = (bf16[768,768]{1,0:T(8,128)(2,1)S(1)}, bf16[768,768]{1,0:T(8,128)(2,1)}, u32[]{:S(2)}) copy-start(bf16[768,768]{1,0:T(8,128)(2,1)} %param.18) | copy-start | bytes 3538948
  7.2 198.8 %reduce-scatter.8.cloned.1.call-start = ((), (), s32[]{:S(2)}) async-start(), calls=%async_computation.7 | async-start | bytes 4866048 | tf_op jit(solution)/shard_map/reduce_scatter | solution.py:345
  7.2 25.7 %collective-permute-start = (bf16[256,768]{1,0:T(8,128)(2,1)}, bf16[256,768]{1,0:T(8,128)(2,1)}, u32[]{:S(2)}, u32[]{:S(2)}) collective-permute-start(bf16[256,768]{1,0:T(8,128)(2,1)} %bitcast.92), channel_id=1, source_target_pairs={{0,1},{1,2},{2,3},{3,4},{4,5},{5,6},{6,7},{7,8},{8,9},{9,10},{10,1... | collective-permute-start | bytes 1179656 | tf_op jit(solution)/shard_map/ppermute | solution.py:207
  13.0 20.0 %collective-permute-start.1 = (bf16[256,768]{1,0:T(8,128)(2,1)}, bf16[256,768]{1,0:T(8,128)(2,1)}, u32[]{:S(2)}, u32[]{:S(2)}) collective-permute-start(bf16[256,768]{1,0:T(8,128)(2,1)} %bitcast.93), channel_id=1, source_target_pairs={{1,0},{2,1},{3,2},{4,3},{5,4},{6,5},{7,6},{8,7},{9,8},{10,9},{11,1... | collective-permute-start | bytes 1179656 | tf_op jit(solution)/shard_map/ppermute | solution.py:207
  19.7 5.7 copy-start.56
  20.5 6.4 copy-start.54
  22.8 0.9 copy-start.38
  23.7 3.2 copy-start.42
  25.4 4.8 copy-start.33
  27.0 6.0 copy-start.19
  27.0 6.0 copy-start.35
  36.6 2.9 copy-start.3
  36.6 2.9 copy-start.4
  36.6 2.9 copy-start.6
  36.6 2.9 copy-start.8
  39.6 19.8 %copy-start.1 = (bf16[768,768]{1,0:T(8,128)(2,1)}, bf16[768,768]{1,0:T(8,128)(2,1)S(1)}, u32[]{:S(2)}) copy-start(bf16[768,768]{1,0:T(8,128)(2,1)S(1)} %convolution_convert_fusion.5.k_ref) | copy-start | bytes 3538948
  39.6 19.2 %copy-start.20 = (bf16[1,256,768]{2,1,0:T(8,128)(2,1)S(1)}, bf16[1,256,768]{2,1,0:T(8,128)(2,1)}, u32[]{:S(2)}) copy-start(bf16[1,256,768]{2,1,0:T(8,128)(2,1)} %param.16) | copy-start | bytes 1179652
  39.6 19.2 %copy-start.23 = (bf16[768,768]{1,0:T(8,128)(2,1)S(1)}, bf16[768,768]{1,0:T(8,128)(2,1)}, u32[]{:S(2)}) copy-start(bf16[768,768]{1,0:T(8,128)(2,1)} %param.21) | copy-start | bytes 3538948
  58.8 12.4 %copy-start.9 = (bf16[768,256]{1,0:T(8,128)(2,1)}, bf16[768,256]{1,0:T(8,128)(2,1)S(1)}, u32[]{:S(2)}) copy-start(bf16[768,256]{1,0:T(8,128)(2,1)S(1)} %get-tuple-element.20) | copy-start | bytes 1179652
  58.8 0.9 copy-start.40
  58.8 12.4 %slice-start = ((s8[4718592]{0:T(1024)(128)(4,1)}), s8[524288]{0:T(1024)(128)(4,1)S(1)}, s32[]{:S(2)}) async-start(s8[4718592]{0:T(1024)(128)(4,1)} %bitcast.101), calls=%async_computation.9 | async-start | bytes 1048576
  59.4 11.8 %copy-start.14 = (f32[256,768]{1,0:T(8,128)}, f32[256,768]{1,0:T(8,128)S(1)}, u32[]{:S(2)}) copy-start(f32[256,768]{1,0:T(8,128)S(1)} %get-tuple-element.58) | copy-start | bytes 2359300
  59.6 11.5 %copy-start.46 = (f32[256]{0:T(256)}, f32[256]{0:T(256)S(1)}, u32[]{:S(2)}) copy-start(f32[256]{0:T(256)S(1)} %multiply_reduce_fusion.3) | copy-start | bytes 3076
  59.7 11.5 %copy-start.43 = (f32[256]{0:T(256)}, f32[256]{0:T(256)S(1)}, u32[]{:S(2)}) copy-start(f32[256]{0:T(256)S(1)} %fusion.49) | copy-start | bytes 3076
  59.7 11.5 %slice-start.1 = ((s8[4718592]{0:T(1024)(128)(4,1)}), s8[4194304]{0:T(1024)(128)(4,1)S(1)}, s32[]{:S(2)}) async-start(s8[4718592]{0:T(1024)(128)(4,1)} %bitcast.101), calls=%async_computation.10 | async-start | bytes 8388608
  71.2 1.8 copy-start.25
  71.3 1.8 copy-start.41
  71.3 2.2 copy-start.48
  79.2 239.4 %reduce-scatter.6.cloned.1.call-start = ((), (), s32[]{:S(2)}) async-start(), calls=%async_computation.5 | async-start | bytes 4866048 | tf_op jit(solution)/shard_map/reduce_scatter | solution.py:345
  79.2 7.6 %copy-start.15 = (f32[256,768]{1,0:T(8,128)S(1)}, f32[256,768]{1,0:T(8,128)}, u32[]{:S(2)}) copy-start(f32[256,768]{1,0:T(8,128)} %copy-done.14) | copy-start | bytes 2359300
  79.2 7.6 %copy-start.44 = (f32[256]{0:T(256)S(1)}, f32[256]{0:T(256)}, u32[]{:S(2)}) copy-start(f32[256]{0:T(256)} %copy-done.43) | copy-start | bytes 3076
  85.7 1.1 copy-start.32
  91.3 343.0 %reduce-scatter.4.cloned.1.call-start = ((), (), s32[]{:S(2)}) async-start(), calls=%async_computation.3 | async-start | bytes 5677056 | tf_op jit(solution)/shard_map/reduce_scatter | solution.py:345
  91.9 5.8 copy-start.47
  91.9 5.9 copy-start.16
  92.0 6.2 copy-start.24
  97.8 1.3 copy-start.2
  97.8 1.7 copy-start.5
  97.8 1.9 copy-start.7
  98.2 29.7 %copy-start.17 = (f32[256,768]{1,0:T(8,128)}, f32[256,768]{1,0:T(8,128)S(1)}, u32[]{:S(2)}) copy-start(f32[256,768]{1,0:T(8,128)S(1)} %get-tuple-element.37) | copy-start | bytes 2359300
  127.8 13.4 %copy-start.11 = (bf16[256,768]{1,0:T(8,128)(2,1)}, bf16[256,768]{1,0:T(8,128)(2,1)S(1)}, u32[]{:S(2)}) copy-start(bf16[256,768]{1,0:T(8,128)(2,1)S(1)} %get-tuple-element.22) | copy-start | bytes 1179652
  127.9 2.5 copy-start.30
  130.7 2.2 copy-start.13
  132.9 8.3 %copy-start.21 = (bf16[1,256,768]{2,1,0:T(8,128)(2,1)S(1)}, bf16[1,256,768]{2,1,0:T(8,128)(2,1)}, u32[]{:S(2)}) copy-start(bf16[1,256,768]{2,1,0:T(8,128)(2,1)} %param.16) | copy-start | bytes 1179652
  132.9 8.9 %copy-start.55 = (s32[512]{0:T(512)S(1)}, s32[512]{0:T(512)}, u32[]{:S(2)}) copy-start(s32[512]{0:T(512)} %copy-done.54) | copy-start | bytes 6148
  134.2 40.8 %collective-permute-start.2 = (bf16[256,1536]{1,0:T(8,128)(2,1)}, bf16[256,1536]{1,0:T(8,128)(2,1)}, u32[]{:S(2)}, u32[]{:S(2)}) collective-permute-start(bf16[256,1536]{1,0:T(8,128)(2,1)} %get-tuple-element.54), channel_id=1, source_target_pairs={{0,1},{1,2},{2,3},{3,4},{4,5},{5,6},{6,7},{7,8},{8,9},{9,10},{10,1... | collective-permute-start | bytes 2359304 | tf_op jit(solution)/shard_map/ppermute | solution.py:207
  139.9 37.2 %collective-permute-start.3 = (bf16[256,1536]{1,0:T(8,128)(2,1)}, bf16[256,1536]{1,0:T(8,128)(2,1)}, u32[]{:S(2)}, u32[]{:S(2)}) collective-permute-start(bf16[256,1536]{1,0:T(8,128)(2,1)} %get-tuple-element.55), channel_id=1, source_target_pairs={{1,0},{2,1},{3,2},{4,3},{5,4},{6,5},{7,6},{8,7},{9,8},{10,9},{11,1... | collective-permute-start | bytes 2359304 | tf_op jit(solution)/shard_map/ppermute | solution.py:207
  150.0 29.6 %copy-start.22 = (bf16[1,256,768]{2,1,0:T(8,128)(2,1)S(1)}, bf16[1,256,768]{2,1,0:T(8,128)(2,1)}, u32[]{:S(2)}) copy-start(bf16[1,256,768]{2,1,0:T(8,128)(2,1)} %param.16) | copy-start | bytes 1179652
  179.3 3.8 copy-start.27
  179.3 1.7 copy-start.31
  179.3 1.9 copy-start.37
  181.2 3.4 copy-start.10
  181.2 3.4 copy-start.18
  183.0 3.1 copy-start.53
  190.7 243.6 %copy-start.26 = (bf16[1,256,768]{2,1,0:T(8,128)(2,1)S(1)}, bf16[1,256,768]{2,1,0:T(8,128)(2,1)}, u32[]{:S(2)}) copy-start(bf16[1,256,768]{2,1,0:T(8,128)(2,1)} %param.17) | copy-start | bytes 1179652
  190.7 243.7 %copy-start.49 = (f32[768]{0:T(1024)S(1)}, f32[768]{0:T(1024)}, u32[]{:S(2)}) copy-start(f32[768]{0:T(1024)} %get-tuple-element.27) | copy-start | bytes 9220
  190.7 243.7 %copy-start.50 = (f32[768]{0:T(1024)S(1)}, f32[768]{0:T(1024)}, u32[]{:S(2)}) copy-start(f32[768]{0:T(1024)} %get-tuple-element.31) | copy-start | bytes 9220
  190.7 284.5 %copy-start.12 = (bf16[256,768]{1,0:T(8,128)(2,1)S(1)}, bf16[256,768]{1,0:T(8,128)(2,1)}, u32[]{:S(2)}) copy-start(bf16[256,768]{1,0:T(8,128)(2,1)} %copy-done.11) | copy-start | bytes 1179652
  190.8 309.6 %all-gather.8.cloned.1.call-start = ((), (), s32[]{:S(2)}) async-start(), calls=%async_computation.8 | async-start | bytes 4866048 | tf_op jit(solution)/shard_map/all_gather | solution.py:346
  206.0 359.9 %all-gather.6.cloned.1.call-start = ((), (), s32[]{:S(2)}) async-start(), calls=%async_computation.6 | async-start | bytes 4866048 | tf_op jit(solution)/shard_map/all_gather | solution.py:346
  318.6 315.6 %all-gather.4.cloned.1.call-start = ((), (), s32[]{:S(2)}) async-start(), calls=%async_computation.4 | async-start | bytes 5677056 | tf_op jit(solution)/shard_map/all_gather | solution.py:346
  475.2 1.3 copy-start.34
  475.2 1.8 copy-start.28
  475.2 1.9 copy-start.36
  (5 other events, 3.9 us)
Sparse Core Ops, SparseCore 0:
  79.3 126.6 reduce-scatter.7
  212.4 106.1 reduce-scatter.5
  324.7 109.5 reduce-scatter.3
  437.4 62.9 all-gather.7
  503.5 62.3 all-gather.5
  569.1 64.9 all-gather.3

commit v2 on v1

--- a/solution.py
+++ b/solution.py
@@ -197,6 +197,335 @@
     )(query, key_ext, value_ext, grad, probs, relk, relq)
 
 
+MESH = pl.DeviceIdType.MESH
+PACK = 16
+
+
+def axes_of(seq_count):
+    row, place = lax.axis_index("rows"), lax.axis_index("seq")
+    first, second, third = place % 2, (place // 2) % 2, place // 4
+    near = (first + row * (second - first), 1 + row, 2)
+    cross = (second + row * (first - second), 2 - row, 2)
+    far = (third, 4, seq_count // 4)
+    return row, place, near, cross, far
+
+
+class Line:
+    def __init__(self, at, step, count):
+        self.at, self.step, self.count = at, step, count
+
+    def peers(self, row, place):
+        for ahead in range(1, self.count):
+            there = lax.rem(self.at + ahead, self.count)
+            yield ahead - 1, there, {"rows": row, "seq": place + (there - self.at) * self.step}
+
+
+class CoreLine(Line):
+    def peers(self, row, place):
+        yield 0, 1 - row, {"rows": 1 - row, "seq": place}
+
+
+def add_rows(target, at, sources, rows, out=None, out_at=None):
+    out, out_at = (target, at) if out is None else (out, out_at)
+    step = 48 if rows % 48 == 0 else (32 if rows % 32 == 0 else PACK)
+
+    def body(i, carry):
+        here = pl.multiple_of(i * step, PACK)
+        total = target[pl.ds(pl.multiple_of(at + here, PACK), step), :].astype(jnp.float32)
+        for source in sources:
+            total = total + source[pl.ds(here, step), :].astype(jnp.float32)
+        out[pl.ds(pl.multiple_of(out_at + here, PACK), step), :] = total.astype(out.dtype)
+        return carry
+
+    lax.fori_loop(0, rows // step, body, 0)
+
+
+class Chunk:
+    def __init__(self, index, base, half, take, put, far_first):
+        self.index, self.base, self.half = index, base, half
+        self.take, self.put, self.far_first = take, put, far_first
+
+
+def sum_plan(chunks, seq_count):
+    plan = []
+    for chunk in chunks:
+        far = seq_count // 4
+        counts = (2, far, 2, 2) if chunk.far_first else (2, 2, 2, far)
+        rows, phases = 2 * chunk.half, []
+        for count in counts:
+            rows //= count
+            phases.append((count, rows))
+        plan.append(phases)
+    return plan
+
+
+def sum_kernel(chunks, seq_count, stride, *refs):
+    n_in = len(SOURCES)
+    ins, vec_in = refs[:n_in], refs[n_in]
+    outs, vec_out = refs[n_in + 1 : 2 * n_in + 1], refs[2 * n_in + 1]
+    acc, gat, recv, vec_acc, vec_recv, load_sem, send_sem, recv_sem, vec_send, vec_got, store_sem = refs[
+        2 * n_in + 2 :
+    ]
+    row, place, near, cross, far = axes_of(seq_count)
+    core = CoreLine(row, 0, 2)
+    lines_a = (core, Line(*near), Line(*cross), Line(*far))
+    lines_c = (core, Line(*far), Line(*near), Line(*cross))
+    plan = sum_plan(chunks, seq_count)
+
+    barrier = pltpu.get_barrier_semaphore()
+    greeted = 0
+    for line in lines_a:
+        for _, _, device in line.peers(row, place):
+            pl.semaphore_signal(barrier, inc=1, device_id=device, device_id_type=MESH)
+            greeted += 1
+    pl.semaphore_wait(barrier, greeted)
+
+    def remote(source, target, sems, device):
+        return pltpu.make_async_remote_copy(
+            src_ref=source, dst_ref=target, send_sem=send_sem.at[sems], recv_sem=recv_sem.at[sems],
+            device_id=device, device_id_type=MESH,
+        )
+
+    acc_at, recv_at, sem_at = [], [], []
+    acc_rows = recv_rows = sems = 0
+    for phases in plan:
+        acc_at.append(acc_rows)
+        acc_rows += phases[0][1]
+        recv_at.append([])
+        sem_at.append([])
+        for count, rows in phases:
+            recv_at[-1].append(recv_rows)
+            recv_rows += (count - 1) * rows
+            sem_at[-1].append((sems, sems + count - 1))
+            sems += 2 * (count - 1)
+
+    def lines_of(chunk):
+        return lines_c if chunk.far_first else lines_a
+
+    def offset(chunk, phase):
+        at = 0
+        for line, (count, rows) in list(zip(lines_of(chunk), plan[chunk.index]))[1 : phase + 1]:
+            at = at + line.at * rows
+        return at
+
+    in_flight = {}
+
+    def start_reduce(chunk, phase):
+        c = chunk.index
+        count, rows = plan[c][phase]
+        line = lines_of(chunk)[phase]
+        copies = []
+        for slot, there, device in line.peers(row, place):
+            if phase == 0:
+                source = chunk.take(ins, there)
+            else:
+                at = acc_at[c] + offset(chunk, phase - 1) + there * rows
+                source = acc.at[pl.ds(pl.multiple_of(at, PACK), rows)]
+            target = recv.at[pl.ds(recv_at[c][phase] + slot * rows, rows)]
+            copy = remote(source, target, sem_at[c][phase][0] + slot, device)
+            copy.start()
+            copies.append(copy)
+        if phase == 0:
+            load = pltpu.make_async_copy(
+                chunk.take(ins, row), acc.at[pl.ds(acc_at[c], rows)], load_sem.at[c]
+            )
+            load.start()
+            copies.append(load)
+        in_flight[c] = copies
+
+    def end_reduce(chunk, phase):
+        c = chunk.index
+        count, rows = plan[c][phase]
+        for copy in in_flight.pop(c):
+            copy.wait()
+        sources = [
+            recv.at[pl.ds(recv_at[c][phase] + slot * rows, rows)] for slot in range(count - 1)
+        ]
+        at = acc_at[c] + offset(chunk, phase)
+        if phase == 3:
+            home = chunk.base + row * chunk.half + offset(chunk, 3)
+            add_rows(acc, at, sources, rows, gat, home)
+        else:
+            add_rows(acc, at, sources, rows)
+
+    def start_gather(chunk, phase):
+        c = chunk.index
+        count, rows = plan[c][phase]
+        line = lines_of(chunk)[phase]
+        home = chunk.base + row * chunk.half + offset(chunk, phase)
+        mine = gat.at[pl.ds(pl.multiple_of(home, PACK), rows)]
+        copies = []
+        for slot, there, device in line.peers(row, place):
+            copy = remote(mine, mine, sem_at[c][phase][1] + slot, device)
+            copy.start()
+            copies.append(copy)
+        in_flight[c] = copies
+
+    def end_gather(chunk, phase):
+        for copy in in_flight.pop(chunk.index):
+            copy.wait()
+
+    stores = []
+
+    def store(chunk):
+        for number, (source, target) in enumerate(chunk.put(gat, outs)):
+            copy = pltpu.make_async_copy(source, target, store_sem.at[chunk.index, number])
+            copy.start()
+            stores.append(copy)
+
+    def step(chunk, stage):
+        if stage == 0:
+            start_reduce(chunk, 0)
+        elif stage < 4:
+            end_reduce(chunk, stage - 1)
+            start_reduce(chunk, stage)
+        elif stage == 4:
+            end_reduce(chunk, 3)
+            start_gather(chunk, 3)
+        elif stage < 8:
+            end_gather(chunk, 8 - stage)
+            start_gather(chunk, 7 - stage)
+        else:
+            end_gather(chunk, 0)
+            store(chunk)
+
+    vec_sems = [0]
+
+    def vec_stage(stage):
+        if stage == 0:
+            vec_acc[...] = vec_in[...]
+        else:
+            first = vec_sems[0]
+            copies = []
+            for slot, _, device in lines_a[stage - 1].peers(row, place):
+                copy = pltpu.make_async_remote_copy(
+                    src_ref=vec_acc, dst_ref=vec_recv.at[first + slot], send_sem=vec_send.at[first + slot],
+                    recv_sem=vec_got.at[first + slot], device_id=device, device_id_type=MESH,
+                )
+                copy.start()
+                copies.append(copy)
+            for copy in copies:
+                copy.wait()
+            vec_sems[0] += len(copies)
+            for slot in range(len(copies)):
+                vec_acc[...] += vec_recv[first + slot]
+
+    events = sorted(
+        (stride * chunk.index + stage, -stage, chunk.index) for chunk in chunks for stage in range(9)
+    )
+    vec_stage(0)
+    next_vec = 1
+    for slot, minus, c in events:
+        step(chunks[c], -minus)
+        if c == 0 and next_vec <= 4:
+            vec_stage(next_vec)
+            next_vec += 1
+    vec_out[...] = vec_acc[...]
+    for copy in stores:
+        copy.wait()
+
+
+SOURCES = ("outer", "inner", "rest")
+
+
+def cut_rows(which, start, base, half):
+    def take(refs, side):
+        return refs[which].at[pl.ds(pl.multiple_of(start + side * half, PACK), half)]
+
+    def put(gat, refs):
+        return [(gat.at[pl.ds(base, 2 * half)], refs[which].at[pl.ds(start, 2 * half)])]
+
+    return take, put
+
+
+def cut_cols(which, start, base, half):
+    def take(refs, side):
+        return refs[which].at[:, pl.ds(pl.multiple_of(start + side * half, PAIR), half)]
+
+    def put(gat, refs):
+        return [
+            (gat.at[pl.ds(base + side * half, half)], refs[which].at[:, pl.ds(start + side * half, half)])
+            for side in range(2)
+        ]
+
+    return take, put
+
+
+def chunks_of(outer, inner, rest, devices):
+    unit = PACK * devices
+    chunks, base = [], 0
+
+    def add(cut, which, start, half, far_first=False):
+        nonlocal base
+        chunks.append(Chunk(len(chunks), base, half, *cut(which, start, base, half), far_first))
+        base += 2 * half
+
+    def split(which, total, parts):
+        start, left = 0, total // unit
+        for part in range(parts):
+            units = -(-left // (parts - part))
+            add(cut_rows, which, start, units * unit // 2)
+            start, left = start + units * unit, left - units
+
+    split(0, outer.shape[0], 2)
+    width = inner.shape[0]
+    for start in range(0, inner.shape[1], 2 * width):
+        add(cut_cols, 1, start, width)
+    split(2, rest.shape[0], 3)
+    return chunks, base
+
+
+def sum_over_devices(outer, inner, rest, vectors, seq_count):
+    chunks, total = chunks_of(outer, inner, rest, 2 * seq_count)
+    plan = sum_plan(chunks, seq_count)
+    width = rest.shape[1]
+    recv_rows = sum((count - 1) * rows for phases in plan for count, rows in phases)
+    sems = sum(2 * (count - 1) for phases in plan for count, _ in phases)
+    vec_slots = sum(count - 1 for count, _ in plan[0])
+    any_spec = pl.BlockSpec(memory_space=pl.ANY)
+    vmem = pl.BlockSpec(memory_space=pltpu.VMEM)
+    return pl.pallas_call(
+        functools.partial(sum_kernel, chunks, seq_count, 1),
+        in_specs=[any_spec] * 3 + [vmem],
+        out_specs=[any_spec] * 3 + [vmem],
+        out_shape=[jax.ShapeDtypeStruct(a.shape, a.dtype) for a in (outer, inner, rest, vectors)],
+        scratch_shapes=[
+            pltpu.VMEM((total // 2, width), jnp.bfloat16),
+            pltpu.VMEM((total, width), jnp.bfloat16),
+            pltpu.VMEM((recv_rows, width), jnp.bfloat16),
+            pltpu.VMEM(vectors.shape, jnp.float32),
+            pltpu.VMEM((vec_slots,) + vectors.shape, jnp.float32),
+            pltpu.SemaphoreType.DMA((len(chunks),)),
+            pltpu.SemaphoreType.DMA((sems,)),
+            pltpu.SemaphoreType.DMA((sems,)),
+            pltpu.SemaphoreType.DMA((vec_slots,)),
+            pltpu.SemaphoreType.DMA((vec_slots,)),
+            pltpu.SemaphoreType.DMA((len(chunks), 2)),
+        ],
+        compiler_params=pltpu.CompilerParams(
+            collective_id=0, has_side_effects=True, vmem_limit_bytes=56 * 2**20
+        ),
+        name="sum_over_devices",
+    )(outer, inner, rest, vectors)
+
+
+def total_of(outer, inner, rest, vectors):
+    seq_count, rows_count = lax.axis_size("seq"), lax.axis_size("rows")
+    unit = PACK * seq_count * rows_count
+    if rows_count == 2 and seq_count % 4 == 0 and all(
+        part.shape[0] % unit == 0 for part in (outer, rest)
+    ) and inner.shape[0] % (unit // 2) == 0:
+        return sum_over_devices(outer, inner, rest, vectors, seq_count)
+    both = ("rows", "seq")
+    sums = [
+        lax.all_gather(
+            lax.psum_scatter(part, both, scatter_dimension=0, tiled=True), both, axis=0, tiled=True
+        )
+        for part in (outer, inner, rest)
+    ]
+    return (*sums, lax.psum(vectors, both))
+
+
 norm_eps = 1e-07
 masked_score = -1e30
 
@@ -331,29 +660,17 @@
         + f32dot("td,ed->te", dkey, w_key)
         + f32dot("td,ed->te", dvalue, w_value)
     )
-    norm_parts = lax.psum(
-        (mid_gain_part, mid_bias_part, end_gain_part, end_bias_part), ("rows", "seq")
-    )
-    groups = (
-        (outer_part,),
-        tuple(inner_part[:, at : at + width] for at in range(0, inner_part.shape[1], width)),
-        (query_part, key_part, value_part, output_part, table_part),
-    )
-    outs = []
-    for group in groups:
-        packed = jnp.concatenate(group, axis=0)
-        share = lax.psum_scatter(packed, ("rows", "seq"), scatter_dimension=0, tiled=True)
-        whole = lax.all_gather(share, ("rows", "seq"), axis=0, tiled=True).astype(jnp.float32)
-        pieces, at = [], 0
-        for piece in group:
-            pieces.append(whole[at : at + piece.shape[0]])
-            at += piece.shape[0]
-        outs.append(pieces)
-    (outer_w,), inner_w, (query_w, key_w, value_w, output_w, table_w) = outs
-    inner_w = jnp.concatenate(inner_w, axis=1)
+    vectors = jnp.concatenate(
+        [mid_gain_part, mid_bias_part, end_gain_part, end_bias_part, jnp.zeros_like(mid_gain_part)] * 2
+    ).reshape(-1, width)[:8]
+    rest_part = jnp.concatenate([query_part, key_part, value_part, output_part, table_part], axis=0)
+    outer_w, inner_w, rest_w, norm_parts = total_of(outer_part, inner_part, rest_part, vectors)
+    query_w, key_w, value_w, output_w = (rest_w[at * width : (at + 1) * width] for at in range(4))
+    table_w = rest_w[4 * width :]
     return (
-        layer_out[None], tokens_grad[None], query_w, key_w, value_w, output_w, inner_w, outer_w,
-        table_w, *norm_parts,
+        layer_out[None], tokens_grad[None],
+        *(w.astype(jnp.float32) for w in (query_w, key_w, value_w, output_w, inner_w, outer_w, table_w)),
+        *(norm_parts[at] for at in range(4)),
     )
 
 

time: 653 us -> 359 us (0.55)
  waiting for transfers between devices: 412 us -> 20.7 us
  Pallas kernels: 47.3 us -> 204 us
  blocking collectives: 40.8 us -> 0 us
  between operations: 15.1 us -> 1.46 us
    reduce_scatter x3 -> x0, waiting for transfers between devices: 243 us -> none  [shards(): lax.psum_scatter(packed, ('rows', 'seq'), scatter_dimension=0, tiled=True)]
    pallas_call x0 -> x1, Pallas kernels: none -> 157 us  [sum_over_devices(): pl.pallas_call(functools.partial(sum_kernel, chunks, seq_count, 1), in_sp...]
    all_gather x3 -> x0, waiting for transfers between devices: 142 us -> none  [shards(): lax.all_gather(share, ('rows', 'seq'), axis=0, tiled=True)]
    psum x1 -> x0, blocking collectives: 40.8 us -> none  [shards(): lax.psum((mid_gain_part, mid_bias_part, end_gain_part, end_bias_part), ('...]
    convert_element_type x1 -> x4, other arithmetic: 6.82 us -> 18.4 us  [shards(): w.astype(jnp.float32)]
    slice x4 -> x2, local copies, waits for them, and re-layouts: 12 us -> 1.98 us  [the longest x1 1.35 us: shards(): jnp.concatenate([mid_gain_part, mid_bias_part, end_gain_part, end_bias_pa...]
    concatenate x2 -> x0, other arithmetic: 6.64 us -> none  [the longest x1 4.13 us: shards(): inner_w = jnp.concatenate(inner_w, axis=1)]
    unnamed x121 -> x110, local copies, waits for them, and re-layouts: 11.8 us -> 16.7 us
  transfers between devices with their start and end apart: 10 -> 4, of which waited for: 8 -> 2; matrix products, arithmetic and copies ran while one was open for 12% -> 8% of each run, Pallas kernels for 4% -> 0%
where the time goes in v2:
time: 359 us; the launch traced here: 356 us
  Pallas kernels  204 us (57%)
  matrix products  63 us (18%)
  other arithmetic  27.2 us (8%)
  local copies, waits for them, and re-layouts  24.7 us (7%)
  waiting for transfers between devices  20.7 us (6%)
  starting transfers between devices  14.2 us (4%)
    pallas_call x1, Pallas kernels, sum_over_devices(): pl.pallas_call(functools.partial(sum_kernel, chunks, seq_count, 1), in_sp...  157 us
    dot_general x27, matrix products, f32dot(): return jnp.einsum(spec, left, right, preferred_element_type=jnp.float32)  63 us
    pallas_call x1, Pallas kernels, attend_back(): pl.pallas_call(attend_back_kernel, grid=(pairs,), in_specs=[cols(block_le...  27.9 us
    ppermute x4, waiting for transfers between devices, shifted(): return lax.ppermute(shard, axis, pairs)  20.7 us
    pallas_call x1, Pallas kernels, attend(): pl.pallas_call(attend_kernel, grid=(pairs,), in_specs=[pl.BlockSpec((bloc...  19.2 us
    convert_element_type x4, other arithmetic, shards(): w.astype(jnp.float32)  18.4 us
    unnamed x110, local copies, waits for them, and re-layouts  16.7 us
    ppermute x4, starting transfers between devices, shifted(): return lax.ppermute(shard, axis, pairs)  14.2 us
  transfers between devices with their start and end apart: 4, of which 2 were waited for; matrix products, arithmetic and copies ran while one was open for 8% of the time, Pallas kernels for 0%

profile of v2, /device:TPU:0, one launch (start us, length us, event | category | flops | bytes accessed | tf_op | source)
XLA Modules:
  0.0 355.6 jit_solution(7228298256253546189)
XLA Ops:
  0.7 1.4 collective-permute-start.1
  2.1 6.2 %collective-permute-start = (bf16[256,768]{1,0:T(8,128)(2,1)}, bf16[256,768]{1,0:T(8,128)(2,1)}, u32[]{:S(2)}, u32[]{:S(2)}) collective-permute-start(bf16[256,768]{1,0:T(8,128)(2,1)} %bitcast.93), channel_id=1, source_target_pairs={{0,1},{1,2},{2,3},{3,4},{4,5},{5,6},{6,7},{7,8},{8,9},{9,10},{10,1... | collective-permute-start | bytes 1179656 | tf_op jit(solution)/shard_map/ppermute | solution.py:536
  8.3 1.3 slice.67
  9.6 0.8 slice.68
  10.4 0.8 select_reduce_fusion
  11.5 2.2 convolution_convert_fusion.14.q_ref
  13.7 0.7 fusion.47
  14.5 0.6 copy-done.40
  15.0 2.7 convolution_convert_fusion.11
  17.7 0.6 convolution_convert_fusion.10
  18.4 0.9 copy-done.27
  19.2 0.8 convolution_convert_fusion.8
  20.2 1.6 fusion.28.bias_ref
  21.9 0.7 convert_reduce_fusion
  22.5 3.2 convolution_convert_fusion.9.relk_ref
  25.7 2.2 convolution_convert_fusion.4.v_ref
  27.9 1.5 copy.30.vt_ref
  29.4 2.9 convolution_convert_fusion.5.k_ref
  32.3 19.2 %attend.1 = (bf16[768,256]{1,0:T(8,128)(2,1)S(1)}, bf16[12,2,640,128]{3,2,1,0:T(8,128)(2,1)}) custom-call(bf16[256,768]{1,0:T(8,128)(2,1)S(1)} %copy-done.2, bf16[768,768]{1,0:T(8,128)(2,1)S(1)} %convolution_convert_fusion.5.k_ref, bf16[768,768]{1,0:T(8,128)(2,1)S(1)} %copy-done.1, bf16[512,768]{1,0:T(8,128)(2,1)S(1)} %copy-done.3, ...), custom_call_target="tpu_custom_call" | custom-call | tf_op jit(solution)/shard_map/attend/pallas_call | solution.py:81
  51.5 0.6 fusion.70
  52.4 10.8 %multiply_convert_fusion = (bf16[256,3072]{1,0:T(8,128)(2,1)S(1)}, f32[256,3072]{1,0:T(8,128)S(1)}, f32[256,3072]{1,0:T(8,128)S(1)}) fusion(bf16[768,3072]{1,0:T(8,128)(2,1)} %param.22, f32[256,768]{1,0:T(8,128)S(1)} %get-tuple-element.58, f32[768]{0:T(1024)S(1)} %copy-done.29, f32[768]{0:T(1024)S(1)} %copy-done.28, f32[256]{0:T(256)S(1)} %fusion.49, ...), kind=kOutput, calls=%fused_computation.5 | convolution fusion | flops 1260060672 | bytes 13377536 | tf_op jit(solution)/shard_map/td,df->tf/dot_general | solution.py:546
  63.3 1.5 fusion.71
  65.5 1.1 fusion.67
  66.6 2.1 add_convert_fusion
  68.7 1.8 multiply_reduce_fusion
  71.0 0.5 convolution_convert_fusion.13.grad_ref
  71.5 27.9 %attend_back.1 = (bf16[256,768]{1,0:T(8,128)(2,1)S(1)}, f32[768,768]{1,0:T(8,128)}, f32[768,768]{1,0:T(8,128)}, f32[768,512]{1,0:T(8,128)}, f32[768,768]{1,0:T(8,128)}) custom-call(bf16[256,768]{1,0:T(8,128)(2,1)S(1)} %copy-done.2, bf16[768,768]{1,0:T(8,128)(2,1)S(1)} %convolution_convert_fusion.5.k_ref, ...), custom_call_target="tpu_custom_call" | custom-call | tf_op jit(solution)/shard_map/attend_back/pallas_call | solution.py:179
  99.9 1.9 fusion.56
  101.8 3.7 %convolution_convert_fusion.1.refs_0_ = bf16[3072,768]{1,0:T(8,128)(2,1)} fusion(bf16[256,3072]{1,0:T(8,128)(2,1)S(1)} %get-tuple-element.48, f32[256,768]{1,0:T(8,128)S(1)} %get-tuple-element.47, f32[256]{0:T(256)S(1)} %negate_multiply_fusion.2), kind=kOutput, calls=%fused_computation.1 | convolution fusion | flops 1210712064 | bytes 7078912 | tf_op jit(solution)/shard_map/tf,td->fd/dot_general | solution.py:546
  105.5 1.3 constant_dynamic-update-slice_fusion.2
  106.8 1.3 constant_dynamic-update-slice_fusion.3
  108.1 1.3 constant_dynamic-update-slice_fusion.6
  109.4 1.3 constant_dynamic-update-slice_fusion.5
  110.7 1.3 constant_dynamic-update-slice_fusion.4
  112.0 1.3 constant_dynamic-update-slice_fusion.9
  113.3 1.3 constant_dynamic-update-slice_fusion.8
  114.6 4.2 %fusion.16 = f32[512,768]{1,0:T(8,128)} fusion(bf16[768,768]{1,0:T(8,128)(2,1)} %param.19, s32[512]{0:T(512)} %copy-done.40, f32[768,512]{1,0:T(8,128)S(1)} %copy-done.19), kind=kOutput, calls=%fused_computation.44 | convolution fusion | flops 1007681536 | bytes 4327424 | tf_op jit(solution)/shard_map/mr,me->re/dot_general | solution.py:546
  118.8 2.2 constant_dynamic-update-slice_fusion.1
  121.8 1.9 copy-done.7
  123.7 1.0 fusion.69
  124.7 5.1 %collective-permute-start.2 = (bf16[256,1536]{1,0:T(8,128)(2,1)}, bf16[256,1536]{1,0:T(8,128)(2,1)}, u32[]{:S(2)}, u32[]{:S(2)}) collective-permute-start(bf16[256,1536]{1,0:T(8,128)(2,1)} %get-tuple-element.54), channel_id=1, source_target_pairs={{0,1},{1,2},{2,3},{3,4},{4,5},{5,6},{6,7},{7,8},{8,9},{9,10},{10,1... | collective-permute-start | bytes 2359304 | tf_op jit(solution)/shard_map/ppermute | solution.py:536
  129.8 1.5 collective-permute-start.3
  131.2 1.3 constant_dynamic-update-slice_fusion.7
  132.5 1.3 slice.76.refs_3_
  133.8 4.3 %fusion.10 = bf16[3584,768]{1,0:T(8,128)(2,1)} fusion(bf16[512,768]{1,0:T(8,128)(2,1)} %copy-done.27, f32[768,768]{0,1:T(8,128)} %fusion.56, f32[768,768]{1,0:T(8,128)} %get-tuple-element.29), kind=kOutput, calls=%fused_computation.28 | convolution fusion | flops 605159424 | bytes 5111808 | tf_op jit(solution)/shard_map/me,dm->ed/dot_general | solution.py:546
  138.2 4.5 %convolution_convert_fusion.refs_1_ = bf16[768,3072]{1,0:T(8,128)(2,1)} fusion(bf16[256,3072]{1,0:T(8,128)(2,1)S(1)} %copy-done.22, f32[256,768]{1,0:T(8,128)S(1)} %copy-done.9, f32[768]{0:T(1024)S(1)} %copy-done.29, f32[768]{0:T(1024)S(1)} %copy-done.28, f32[256]{0:T(256)} %copy-done.35, f32[256]{0:T(256)S(1)} %broadcast_multiply_fusion.1), kind=kOutput, calls=%fused_computation | convolution fusion | flops 1211301888 | bytes 7086080 | tf_op jit(solution)/shard_map/td,tf->df/dot_general | solution.py:546
  142.6 19.6 %collective-permute-done.2 = bf16[256,1536]{1,0:T(8,128)(2,1)} collective-permute-done((bf16[256,1536]{1,0:T(8,128)(2,1)}, bf16[256,1536]{1,0:T(8,128)(2,1)}, u32[]{:S(2)}, u32[]{:S(2)}) %collective-permute-start.2) | collective-permute-done | bytes 786464 | tf_op jit(solution)/shard_map/ppermute | solution.py:536
  162.3 1.1 collective-permute-done.3
  163.3 2.1 fusion.9
  165.8 0.5 fusion.54
  166.3 0.6 copy-done.20
  167.1 1.8 fusion.11
  168.9 1.5 fusion.14
  170.4 1.6 fusion.12
  172.0 4.6 %fusion.15.refs_2_ = bf16[3584,768]{1,0:T(8,128)(2,1)} fusion(bf16[3584,768]{1,0:T(8,128)(2,1)} %fusion.12, f32[512,768]{1,0:T(8,128)} %fusion.16, bf16[768,768]{1,0:T(8,128)(2,1)S(1)} %copy-done, s32[512]{0:T(512)S(1)} %copy-done.39, f32[768,768]{1,0:T(8,128)} %get-tuple-element.29), kind=kOutput, calls=%fused_computation.41 | convolution fusion | flops 1008074752 | bytes 4327424 | tf_op jit(solution)/shard_map/mr,me->re/dot_general | solution.py:546
  176.6 157.3 %sum_over_devices.1 = (bf16[3072,768]{1,0:T(8,128)(2,1)}, bf16[768,3072]{1,0:T(8,128)(2,1)}, bf16[3584,768]{1,0:T(8,128)(2,1)}, f32[8,768]{1,0:T(8,128)}) custom-call(bf16[3072,768]{1,0:T(8,128)(2,1)} %convolution_convert_fusion.1.refs_0_, bf16[768,3072]{1,0:T(8,128)(2,1)} %convolution_convert_fusion.refs_1_, bf16[3584,768]{1,0:T(8,128)(2,1)} %fusion.15.refs_2_, ...), custom_call_target="tpu_custom_call" | custom-call | tf_op jit(solution)/shard_map/sum_over_devices/pallas_call | solution.py:487
  333.9 2.5 slice_convert_fusion.5
  336.4 6.3 %slice_convert_fusion.1 = (f32[768,768]{1,0:T(8,128)}, f32[768,768]{1,0:T(8,128)}, f32[768,768]{1,0:T(8,128)}, f32[768,768]{1,0:T(8,128)}) fusion(bf16[3584,768]{1,0:T(8,128)(2,1)} %get-tuple-element.31), kind=kLoop, calls=%fused_computation.59 | loop fusion | flops 2359296 | bytes 14155776 | tf_op jit(solution)/shard_map/convert_element_type | solution.py:672
  342.7 0.5 convolution_add_fusion.1
  343.2 0.7 copy-done.25
  344.0 1.3 fusion.18
  345.2 0.6 slice_reduce_fusion
  345.9 5.0 %convert_element_type.183 = f32[768,3072]{1,0:T(8,128)} convert(bf16[768,3072]{1,0:T(8,128)(2,1)S(1)} %bitcast.99) | non-fusion elementwise | flops 2359296 | bytes 14155776 | tf_op jit(solution)/shard_map/convert_element_type | solution.py:672
  350.9 4.5 %convert_element_type.184 = f32[3072,768]{1,0:T(8,128)} convert(bf16[3072,768]{1,0:T(8,128)(2,1)S(1)} %bitcast.97) | non-fusion elementwise | flops 2359296 | bytes 14155776 | tf_op jit(solution)/shard_map/convert_element_type | solution.py:672
  (128 shorter events, 3.7 us)
Async XLA Ops:
  0.6 10.8 %copy-start = (bf16[768,768]{1,0:T(8,128)(2,1)S(1)}, bf16[768,768]{1,0:T(8,128)(2,1)}, u32[]{:S(2)}) copy-start(bf16[768,768]{1,0:T(8,128)(2,1)} %param.18) | copy-start | bytes 3538948
  0.7 17.0 %copy-start.41 = (bf16[512,768]{1,0:T(8,128)(2,1)S(1)}, bf16[512,768]{1,0:T(8,128)(2,1)}, u32[]{:S(2)}) copy-start(bf16[512,768]{1,0:T(8,128)(2,1)} %param.24) | copy-start | bytes 2359300
  0.7 25.0 %collective-permute-start.1 = (bf16[256,768]{1,0:T(8,128)(2,1)}, bf16[256,768]{1,0:T(8,128)(2,1)}, u32[]{:S(2)}, u32[]{:S(2)}) collective-permute-start(bf16[256,768]{1,0:T(8,128)(2,1)} %bitcast.92), channel_id=1, source_target_pairs={{1,0},{2,1},{3,2},{4,3},{5,4},{6,5},{7,6},{8,7},{9,8},{10,9},{11,1... | collective-permute-start | bytes 1179656 | tf_op jit(solution)/shard_map/ppermute | solution.py:536
  2.1 23.6 %collective-permute-start = (bf16[256,768]{1,0:T(8,128)(2,1)}, bf16[256,768]{1,0:T(8,128)(2,1)}, u32[]{:S(2)}, u32[]{:S(2)}) collective-permute-start(bf16[256,768]{1,0:T(8,128)(2,1)} %bitcast.93), channel_id=1, source_target_pairs={{0,1},{1,2},{2,3},{3,4},{4,5},{5,6},{6,7},{7,8},{8,9},{9,10},{10,1... | collective-permute-start | bytes 1179656 | tf_op jit(solution)/shard_map/ppermute | solution.py:536
  14.4 0.6 copy-start.40
  14.4 3.3 copy-start.38
  17.7 2.3 copy-start.34
  18.3 0.9 copy-start.27
  19.2 2.6 copy-start.16
  20.1 5.6 %copy-start.12 = (bf16[1,256,768]{2,1,0:T(8,128)(2,1)S(1)}, bf16[1,256,768]{2,1,0:T(8,128)(2,1)}, u32[]{:S(2)}) copy-start(bf16[1,256,768]{2,1,0:T(8,128)(2,1)} %param.16) | copy-start | bytes 1179652
  20.1 5.6 %copy-start.24 = (bf16[768,768]{1,0:T(8,128)(2,1)S(1)}, bf16[768,768]{1,0:T(8,128)(2,1)}, u32[]{:S(2)}) copy-start(bf16[768,768]{1,0:T(8,128)(2,1)} %param.20) | copy-start | bytes 3538948
  29.4 2.9 copy-start.1
  29.4 2.9 copy-start.2
  29.4 2.9 copy-start.3
  29.4 2.9 copy-start.4
  32.3 19.2 %copy-start.13 = (bf16[1,256,768]{2,1,0:T(8,128)(2,1)S(1)}, bf16[1,256,768]{2,1,0:T(8,128)(2,1)}, u32[]{:S(2)}) copy-start(bf16[1,256,768]{2,1,0:T(8,128)(2,1)} %param.16) | copy-start | bytes 1179652
  32.3 19.2 %copy-start.15 = (bf16[768,768]{1,0:T(8,128)(2,1)S(1)}, bf16[768,768]{1,0:T(8,128)(2,1)}, u32[]{:S(2)}) copy-start(bf16[768,768]{1,0:T(8,128)(2,1)} %param.21) | copy-start | bytes 3538948
  51.5 11.8 %copy-start.5 = (bf16[768,256]{1,0:T(8,128)(2,1)}, bf16[768,256]{1,0:T(8,128)(2,1)S(1)}, u32[]{:S(2)}) copy-start(bf16[768,256]{1,0:T(8,128)(2,1)S(1)} %get-tuple-element.24) | copy-start | bytes 1179652
  51.5 0.9 copy-start.28
  51.5 0.9 copy-start.29
  51.5 11.7 %slice-start.4 = ((s8[4718592]{0:T(1024)(128)(4,1)}), s8[4194304]{0:T(1024)(128)(4,1)S(1)}, s32[]{:S(2)}) async-start(s8[4718592]{0:T(1024)(128)(4,1)} %bitcast.105), calls=%async_computation.4 | async-start | bytes 8388608
  52.1 18.5 %copy-start.8 = (f32[256,768]{1,0:T(8,128)}, f32[256,768]{1,0:T(8,128)S(1)}, u32[]{:S(2)}) copy-start(f32[256,768]{1,0:T(8,128)S(1)} %get-tuple-element.58) | copy-start | bytes 2359300
  52.4 18.2 %copy-start.35 = (f32[256]{0:T(256)}, f32[256]{0:T(256)S(1)}, u32[]{:S(2)}) copy-start(f32[256]{0:T(256)S(1)} %fusion.49) | copy-start | bytes 3076
  52.4 10.9 %slice-start.5 = ((s8[4718592]{0:T(1024)(128)(4,1)}), s8[524288]{0:T(1024)(128)(4,1)S(1)}, s32[]{:S(2)}) async-start(s8[4718592]{0:T(1024)(128)(4,1)} %bitcast.105), calls=%async_computation.5 | async-start | bytes 1048576
  63.3 1.8 copy-start.17
  63.3 1.8 copy-start.30
  63.3 2.2 copy-start.37
  65.5 3.2 slice-start.6
  66.6 2.1 slice-start.7
  68.7 1.8 copy-start.21
  70.9 28.5 %copy-start.10 = (f32[256,768]{1,0:T(8,128)}, f32[256,768]{1,0:T(8,128)S(1)}, u32[]{:S(2)}) copy-start(f32[256,768]{1,0:T(8,128)S(1)} %get-tuple-element.45) | copy-start | bytes 2359300
  71.0 28.4 %copy-start.31 = (f32[256]{0:T(256)}, f32[256]{0:T(256)S(1)}, u32[]{:S(2)}) copy-start(f32[256]{0:T(256)S(1)} %negate_multiply_fusion.1) | copy-start | bytes 3076
  101.8 7.6 %copy-start.33 = (f32[768]{0:T(1024)S(1)}, f32[768]{0:T(1024)}, u32[]{:S(2)}) copy-start(f32[768]{0:T(1024)} %convert_reduce_fusion) | copy-start | bytes 9220
  101.8 12.7 %copy-start.19 = (f32[768,512]{1,0:T(8,128)S(1)}, f32[768,512]{1,0:T(8,128)}, u32[]{:S(2)}) copy-start(f32[768,512]{1,0:T(8,128)} %get-tuple-element.30) | copy-start | bytes 4718596
  118.8 2.4 copy-start.18
  121.5 2.2 copy-start.7
  124.7 13.5 %copy-start.9 = (f32[256,768]{1,0:T(8,128)S(1)}, f32[256,768]{1,0:T(8,128)}, u32[]{:S(2)}) copy-start(f32[256,768]{1,0:T(8,128)} %copy-done.8) | copy-start | bytes 2359300
  124.7 37.6 %collective-permute-start.2 = (bf16[256,1536]{1,0:T(8,128)(2,1)}, bf16[256,1536]{1,0:T(8,128)(2,1)}, u32[]{:S(2)}, u32[]{:S(2)}) collective-permute-start(bf16[256,1536]{1,0:T(8,128)(2,1)} %get-tuple-element.54), channel_id=1, source_target_pairs={{0,1},{1,2},{2,3},{3,4},{4,5},{5,6},{6,7},{7,8},{8,9},{9,10},{10,1... | collective-permute-start | bytes 2359304 | tf_op jit(solution)/shard_map/ppermute | solution.py:536
  129.8 33.5 %collective-permute-start.3 = (bf16[256,1536]{1,0:T(8,128)(2,1)S(1)}, bf16[256,1536]{1,0:T(8,128)(2,1)}, u32[]{:S(2)}, u32[]{:S(2)}) collective-permute-start(bf16[256,1536]{1,0:T(8,128)(2,1)S(1)} %get-tuple-element.55), channel_id=1, source_target_pairs={{1,0},{2,1},{3,2},{4,3},{5,4},{6,5},{7,6},{8,7},{9,8},{10,9},{11,1... | collective-permute-start | bytes 2359304 | tf_op jit(solution)/shard_map/ppermute | solution.py:536
  133.8 4.3 %copy-start.22 = (bf16[256,3072]{1,0:T(8,128)(2,1)S(1)}, bf16[256,3072]{1,0:T(8,128)(2,1)}, u32[]{:S(2)}) copy-start(bf16[256,3072]{1,0:T(8,128)(2,1)} %copy-done.21) | copy-start | bytes 4718596
  142.6 23.1 %copy-start.14 = (bf16[1,256,768]{2,1,0:T(8,128)(2,1)S(1)}, bf16[1,256,768]{2,1,0:T(8,128)(2,1)}, u32[]{:S(2)}) copy-start(bf16[1,256,768]{2,1,0:T(8,128)(2,1)} %param.16) | copy-start | bytes 1179652
  165.4 1.4 copy-start.20
  165.5 1.6 copy-start.26
  167.1 3.4 copy-start.6
  167.1 3.4 copy-start.11
  167.1 3.4 copy-start.32
  168.9 3.1 copy-start.39
  333.8 12.0 %slice-start.2 = ((s8[4718592]{0:T(1024)(128)(4,1)}), s8[4194304]{0:T(1024)(128)(4,1)S(1)}, s32[]{:S(2)}) async-start(s8[4718592]{0:T(1024)(128)(4,1)} %bitcast.98), calls=%async_computation.2 | async-start | bytes 8388608
  336.4 6.3 %copy-start.23 = (bf16[768,768]{1,0:T(8,128)(2,1)S(1)}, bf16[768,768]{1,0:T(8,128)(2,1)}, u32[]{:S(2)}) copy-start(bf16[768,768]{1,0:T(8,128)(2,1)} %param.19) | copy-start | bytes 3538948
  336.4 9.5 %slice-start.3 = ((s8[4718592]{0:T(1024)(128)(4,1)}), s8[524288]{0:T(1024)(128)(4,1)S(1)}, s32[]{:S(2)}) async-start(s8[4718592]{0:T(1024)(128)(4,1)} %bitcast.98), calls=%async_computation.3 | async-start | bytes 1048576
  342.7 1.3 copy-start.25
  342.7 2.5 copy-start.36
  344.0 7.0 %slice-start = ((s8[4718592]{0:T(1024)(128)(4,1)}), s8[4194304]{0:T(1024)(128)(4,1)S(1)}, s32[]{:S(2)}) async-start(s8[4718592]{0:T(1024)(128)(4,1)} %bitcast.96), calls=%async_computation | async-start | bytes 8388608
  345.9 5.1 %slice-start.1 = ((s8[4718592]{0:T(1024)(128)(4,1)}), s8[524288]{0:T(1024)(128)(4,1)S(1)}, s32[]{:S(2)}) async-start(s8[4718592]{0:T(1024)(128)(4,1)} %bitcast.96), calls=%async_computation.1 | async-start | bytes 1048576

commit v3 on v1

--- a/solution.py
+++ b/solution.py
@@ -197,6 +197,500 @@
     )(query, key_ext, value_ext, grad, probs, relk, relq)
 
 
+MESH = pl.DeviceIdType.MESH
+PACK = 16
+
+
+def axes_of(seq_count):
+    row, place = lax.axis_index("rows"), lax.axis_index("seq")
+    first, second, third = place % 2, (place // 2) % 2, place // 4
+    near = (first + row * (second - first), 1 + row, 2)
+    cross = (second + row * (first - second), 2 - row, 2)
+    far = (third, 4, seq_count // 4)
+    return row, place, near, cross, far
+
+
+class Line:
+    def __init__(self, at, step, count):
+        self.at, self.step, self.count = at, step, count
+
+    def peers(self, row, place):
+        for ahead in range(1, self.count):
+            there = lax.rem(self.at + ahead, self.count)
+            yield ahead - 1, there, {"rows": row, "seq": place + (there - self.at) * self.step}
+
+
+class CoreLine(Line):
+    def peers(self, row, place):
+        yield 0, 1 - row, {"rows": 1 - row, "seq": place}
+
+
+def add_rows(target, at, sources, rows, out, out_at):
+    step = next(s for s in (48, 32, PACK) if rows % s == 0)
+
+    def body(i, carry):
+        here = pl.multiple_of(i * step, PACK)
+        total = target[pl.ds(pl.multiple_of(at + here, PACK), step), :].astype(jnp.float32)
+        for source in sources:
+            total = total + source[pl.ds(here, step), :].astype(jnp.float32)
+        out[pl.ds(pl.multiple_of(out_at + here, PACK), step), :] = total.astype(out.dtype)
+        return carry
+
+    lax.fori_loop(0, rows // step, body, 0)
+
+
+class Chunk:
+    def __init__(self, index, which, start, half, base, width):
+        self.index, self.which, self.start, self.half, self.base, self.width = (
+            index, which, start, half, base, width,
+        )
+
+    def part(self, refs, side):
+        if self.which == "inner":
+            block, low_row = (self.start // 2) // self.width, (self.start // 2) % self.width
+            col = (2 * block + side) * self.width
+            return refs["inner"].at[pl.ds(low_row, self.half), pl.ds(pl.multiple_of(col, PAIR), self.width)]
+        first = pl.multiple_of(self.start + side * self.half, PACK)
+        return refs[self.which].at[pl.ds(first, self.half)]
+
+
+def chunks_of(spec, unit, width):
+    chunks, starts, base = [], {}, 0
+    for which, units in spec:
+        half = units * unit // 2
+        start = starts.get(which, 0)
+        chunks.append(Chunk(len(chunks), which, start, half, base, width))
+        starts[which] = start + 2 * half
+        base += half
+    return chunks, base
+
+
+def phases_of(chunk, seq_count):
+    rows, phases = 2 * chunk.half, []
+    for count in (2, 2, 2, seq_count // 4):
+        rows //= count
+        phases.append((count, rows))
+    return phases
+
+
+class Sum:
+    last = 8
+
+    def __init__(self, chunks, seq_count, ins, outs, acc, gat, recv, own_sem, send_sem, recv_sem):
+        self.chunks, self.ins, self.outs = chunks, ins, outs
+        self.acc, self.gat, self.recv = acc, gat, recv
+        self.own_sem, self.send_sem, self.recv_sem = own_sem, send_sem, recv_sem
+        self.row, self.place, near, cross, far = axes_of(seq_count)
+        self.lines = (CoreLine(self.row, 0, 2), Line(*near), Line(*cross), Line(*far))
+        self.phases = [phases_of(chunk, seq_count) for chunk in chunks]
+        self.recv_at, self.sem_at = [], []
+        recv_rows = sems = 0
+        for phases in self.phases:
+            self.recv_at.append([])
+            self.sem_at.append([])
+            for count, rows in phases:
+                self.recv_at[-1].append(recv_rows)
+                recv_rows += (count - 1) * rows
+                self.sem_at[-1].append((sems, sems + count - 1))
+                sems += 2 * (count - 1)
+
+    def greet(self, more):
+        barrier = pltpu.get_barrier_semaphore()
+        devices = [d for line in self.lines for _, _, d in line.peers(self.row, self.place)] + more
+        for device in devices:
+            pl.semaphore_signal(barrier, inc=1, device_id=device, device_id_type=MESH)
+        pl.semaphore_wait(barrier, len(devices))
+
+    def remote(self, source, target, sem, device):
+        return pltpu.make_async_remote_copy(
+            src_ref=source, dst_ref=target, send_sem=self.send_sem.at[sem], recv_sem=self.recv_sem.at[sem],
+            device_id=device, device_id_type=MESH,
+        )
+
+    def offset(self, c, phase):
+        at = 0
+        for line, (count, rows) in list(zip(self.lines, self.phases[c]))[1 : phase + 1]:
+            at = at + line.at * rows
+        return at
+
+    def received(self, c, phase):
+        count, rows = self.phases[c][phase]
+        return [
+            self.recv.at[pl.ds(self.recv_at[c][phase] + slot * rows, rows)] for slot in range(count - 1)
+        ]
+
+    def reduce_copies(self, chunk, phase):
+        c = chunk.index
+        count, rows = self.phases[c][phase]
+        copies = []
+        for slot, there, device in self.lines[phase].peers(self.row, self.place):
+            if phase == 0:
+                source = chunk.part(self.ins, there)
+            else:
+                at = chunk.base + self.offset(c, phase - 1) + there * rows
+                source = self.acc.at[pl.ds(pl.multiple_of(at, PACK), rows)]
+            copies.append(
+                self.remote(source, self.received(c, phase)[slot], self.sem_at[c][phase][0] + slot, device)
+            )
+        if phase == 0:
+            copies.append(
+                pltpu.make_async_copy(
+                    chunk.part(self.ins, self.row), self.acc.at[pl.ds(chunk.base, rows)], self.own_sem.at[c]
+                )
+            )
+        return copies
+
+    def gather_copies(self, chunk, phase):
+        c = chunk.index
+        home = pl.multiple_of(chunk.base + self.offset(c, phase), PACK)
+        mine = self.gat.at[pl.ds(home, self.phases[c][phase][1])]
+        copies = []
+        for slot, there, device in self.lines[phase].peers(self.row, self.place):
+            target = chunk.part(self.outs, self.row) if phase == 0 else mine
+            copies.append(self.remote(mine, target, self.sem_at[c][phase][1] + slot, device))
+        if phase == 0:
+            copies.append(
+                pltpu.make_async_copy(mine, chunk.part(self.outs, self.row), self.own_sem.at[c])
+            )
+        return copies
+
+    def copies(self, chunk, stage):
+        return self.reduce_copies(chunk, stage) if stage < 4 else self.gather_copies(chunk, 7 - stage)
+
+    def step(self, c, stage):
+        chunk = self.chunks[c]
+        if stage > 0:
+            for copy in self.copies(chunk, stage - 1):
+                copy.wait()
+        if 0 < stage <= 4:
+            at = chunk.base + self.offset(c, stage - 1)
+            add_rows(
+                self.acc, at, self.received(c, stage - 1), self.phases[c][stage - 1][1],
+                self.gat if stage == 4 else self.acc, at,
+            )
+        if stage < self.last:
+            for copy in self.copies(chunk, stage):
+                copy.start()
+
+
+class VectorSum:
+    def __init__(self, total, acc, recv, send_sem, recv_sem):
+        self.total, self.acc, self.recv, self.send_sem, self.recv_sem = total, acc, recv, send_sem, recv_sem
+
+    def copies(self, phase):
+        first = sum(line.count - 1 for line in self.total.lines[:phase])
+        for slot, _, device in self.total.lines[phase].peers(self.total.row, self.total.place):
+            yield first + slot, pltpu.make_async_remote_copy(
+                src_ref=self.acc.at[phase], dst_ref=self.recv.at[first + slot],
+                send_sem=self.send_sem.at[first + slot], recv_sem=self.recv_sem.at[first + slot],
+                device_id=device, device_id_type=MESH,
+            )
+
+    def start(self, phase):
+        for _, copy in self.copies(phase):
+            copy.start()
+
+    def end(self, phase):
+        whole = self.acc[phase]
+        for slot, copy in self.copies(phase):
+            copy.wait()
+            whole = whole + self.recv[slot]
+        self.acc[phase + 1] = whole
+
+
+def back_of_pair(pair, buf, r):
+    swap = unit(True)
+    lanes_at = pl.multiple_of(pair * PAIR, PAIR)
+    lanes_here = pl.ds(lanes_at, PAIR)
+    row = lax.broadcasted_iota(jnp.int32, (TILE, TILE), 0)
+    col = lax.broadcasted_iota(jnp.int32, (TILE, TILE), 1)
+    parts = REACH // TILE
+    block_len, ext_len = r["q"].shape[0], r["k"].shape[0]
+    tiles = block_len // TILE
+    qt_ref, kt_ref, dk_ref, dv_ref, drelk_ref, drelq_ref = (
+        r[name] for name in ("qt", "kt", "dk_pair", "dv_pair", "drelk_t", "drelq_t")
+    )
+    for source, result in ((r["q"], qt_ref), (r["k"], kt_ref)):
+        for at in range(0, source.shape[0], TILE):
+            flipped = nn(swap, source[pl.ds(at, TILE), lanes_here])
+            result[:, pl.ds(at, TILE)] = flipped.T.astype(jnp.bfloat16)
+    dk_ref[...] = jnp.zeros_like(dk_ref)
+    dv_ref[...] = jnp.zeros_like(dv_ref)
+    drelk_ref[...] = jnp.zeros_like(drelk_ref)
+    drelq_ref[...] = jnp.zeros_like(drelq_ref)
+    for tile in range(tiles):
+        first = tile * TILE
+        q_tile = r["q"][pl.ds(first, TILE), lanes_here]
+        grad_tile = r["grad"][pl.ds(first, TILE), lanes_here]
+        v_tile = r["v"][pl.ds(first, REACH), lanes_here]
+        q_heads = [head_lanes(q_tile, head) for head in range(2)]
+        grad_heads = [head_lanes(grad_tile, head) for head in range(2)]
+        dq_heads = []
+        lefts = [[] for _ in range(parts)]
+        for head in range(2):
+            lanes = pl.ds(head * DH, DH)
+            probs = r["probs"][buf, head, tile].astype(jnp.float32)
+            weighted = probs * nt(v_tile, grad_heads[head])
+            delta = jnp.sum(weighted, axis=0, keepdims=True)
+            dscore = ((weighted - probs * delta) * score_scale).astype(jnp.bfloat16)
+            turned = nt(swap, dscore)
+            dband = pltpu.roll(turned, REACH - TILE + 1, 1, stride=1, stride_axis=0)
+            dband = dband[:, : 2 * SPAN].astype(jnp.bfloat16)
+            dq_heads.append(
+                nn(turned.astype(jnp.bfloat16), r["k"][pl.ds(first, REACH), lanes_here])
+                + nn(dband, r["relk"][:, lanes_here])
+            )
+            drelk_ref[lanes, :] += nn(qt_ref[lanes, pl.ds(first, TILE)], dband)
+            for part in range(parts):
+                flipped = nn(swap, dscore[part * TILE : (part + 1) * TILE, :])
+                spun = pltpu.roll(flipped, 0, 1, stride=1, stride_axis=0)
+                near = jnp.where(col >= row, spun, 0.0)
+                dfrom = jnp.concatenate([near, spun - near], axis=1).astype(jnp.bfloat16)
+                window = pl.ds((parts - 1 - part) * TILE, 2 * TILE)
+                drelq_ref[lanes, window] += nn(kt_ref[lanes, pl.ds(first + part * TILE, TILE)], dfrom)
+                lefts[part] += [flipped.astype(jnp.bfloat16), dfrom]
+        dq_turned = jnp.where(col < DH, dq_heads[0], dq_heads[1]).astype(jnp.bfloat16)
+        r["dq"][pl.ds(first, TILE), lanes_here] = nn(swap, dq_turned).astype(jnp.bfloat16)
+        dv_ref[pl.ds(first, REACH), :] += nn(
+            jnp.concatenate([r["probs"][buf, 0, tile], r["probs"][buf, 1, tile]], axis=1),
+            jnp.concatenate(grad_heads, axis=0),
+        )
+        for part in range(parts):
+            window = r["relq"][pl.ds((parts - 1 - part) * TILE, 2 * TILE), lanes_here]
+            right = jnp.concatenate(
+                [q_heads[0], head_lanes(window, 0), q_heads[1], head_lanes(window, 1)], axis=0
+            )
+            dk_ref[pl.ds(first + part * TILE, TILE), :] += nn(
+                jnp.concatenate(lefts[part], axis=1), right
+            )
+    r["dv"][:, lanes_here] = dv_ref[...].astype(jnp.bfloat16)
+    for at in range(0, ext_len, TILE):
+        r["dk"][pl.ds(at, TILE), lanes_here] = nn(
+            swap, dk_ref[pl.ds(at, TILE), :].astype(jnp.bfloat16)
+        ).astype(jnp.bfloat16)
+    r["dk"][pl.ds(ext_len, 2 * SPAN), lanes_here] = drelk_ref[...].T.astype(jnp.bfloat16)
+    r["dq"][pl.ds(block_len, 2 * SPAN), lanes_here] = (
+        drelq_ref[:, pl.ds(TILE, 2 * SPAN)].T.astype(jnp.bfloat16)
+    )
+
+
+def by_rows(rows, step, body):
+    def one(i, carry):
+        body(pl.ds(pl.multiple_of(i * step, step), step))
+        return carry
+
+    lax.fori_loop(0, rows // step, one, 0)
+
+
+FINISH_IN = (
+    "q", "k", "v", "grad", "relk", "relq", "xt_key", "xt_query", "w_query", "w_key", "w_value",
+    "hot", "resid", "vectors", "outer", "inner", "output", "probs_in",
+)
+FINISH_OUT = ("outer", "inner", "rest", "vectors", "tokens_grad")
+FINISH_SCRATCH = (
+    "probs", "qt", "kt", "dk_pair", "dv_pair", "drelk_t", "drelq_t", "dq", "dk", "dv", "rest", "table",
+    "halo", "halo_got", "acc", "gat", "recv", "vec_acc", "vec_recv", "own_sem", "send_sem", "recv_sem",
+    "vec_send", "vec_got", "probs_sem", "halo_send", "halo_recv",
+)
+
+
+def finish_kernel(chunks, seq_count, *refs):
+    r = dict(zip(FINISH_IN, refs))
+    outs = dict(zip(FINISH_OUT, refs[len(FINISH_IN) :]))
+    r.update(zip(FINISH_SCRATCH, refs[len(FINISH_IN) + len(FINISH_OUT) :]))
+    block_len, width = r["q"].shape
+    ext_len = r["k"].shape[0]
+    pairs = width // PAIR
+    total = Sum(
+        chunks, seq_count, r, outs, r["acc"], r["gat"], r["recv"], r["own_sem"], r["send_sem"], r["recv_sem"]
+    )
+    row, place = total.row, total.place
+    before = {"rows": row, "seq": lax.rem(place + seq_count - 1, seq_count)}
+    after = {"rows": row, "seq": lax.rem(place + 1, seq_count)}
+    total.greet([before, after])
+    vec = VectorSum(total, r["vec_acc"], r["vec_recv"], r["vec_send"], r["vec_got"])
+    vec.acc[0] = r["vectors"][...]
+
+    early = [c for c, chunk in enumerate(chunks) if chunk.which != "rest"]
+    late = [c for c, chunk in enumerate(chunks) if chunk.which == "rest"]
+    for c in early:
+        total.step(c, 0)
+
+    def probs_copy(pair, buf):
+        return pltpu.make_async_copy(
+            r["probs_in"].at[pl.ds(2 * pair, 2)], r["probs"].at[buf], r["probs_sem"].at[buf]
+        )
+
+    probs_copy(0, 0).start()
+    done = {c: 0 for c in early}
+
+    def move(*steps):
+        for c, stage in steps:
+            total.step(c, stage)
+            done[c] = stage
+
+    def between(pair):
+        if pair == 0:
+            move((0, 1), (1, 1))
+            vec.start(0)
+        elif pair == 1:
+            move((2, 1), (3, 1))
+            vec.end(0)
+            vec.start(1)
+        elif pair == 2:
+            move((0, 2))
+            vec.end(1)
+            vec.start(2)
+        elif pair == 3:
+            move((1, 2), (0, 3))
+            vec.end(2)
+            vec.start(3)
+        elif pair == 4:
+            move((1, 3), (0, 4))
+            vec.end(3)
+        else:
+            move((2, 2), (1, 4), (0, 5))
+
+    def one_pair(pair, carry):
+        buf = lax.rem(pair, 2)
+
+        @pl.when(pair + 1 < pairs)
+        def _():
+            probs_copy(pair + 1, 1 - buf).start()
+
+        probs_copy(pair, buf).wait()
+        back_of_pair(pair, buf, r)
+        for at in range(pairs):
+            pl.when(pair == at)(functools.partial(between, at))
+        return carry
+
+    lax.fori_loop(0, pairs, one_pair, 0)
+
+    def query_rows(rows):
+        r["rest"][rows, :] = nn(r["xt_query"][rows, :], r["dq"][...]).astype(jnp.bfloat16)
+
+    def key_rows(rows):
+        at = pl.ds(pl.multiple_of(width + rows.start, PACK), rows.size)
+        r["rest"][at, :] = nn(r["xt_key"][rows, :], r["dk"][...]).astype(jnp.bfloat16)
+
+    def value_rows(rows):
+        at = pl.ds(pl.multiple_of(2 * width + rows.start, PACK), rows.size)
+        r["rest"][at, :] = nn(r["xt_key"][rows, pl.ds(0, ext_len)], r["dv"][...]).astype(jnp.bfloat16)
+
+    def table_rows(rows):
+        key_at = pl.ds(pl.multiple_of(ext_len + rows.start, PACK), rows.size)
+        query_at = pl.ds(pl.multiple_of(block_len + rows.start, PACK), rows.size)
+        other = pl.ds(pl.multiple_of(2 * SPAN + rows.start, PACK), rows.size)
+        r["table"][rows, :] = nt(r["dk"][key_at, :], r["w_key"][...]).astype(jnp.bfloat16)
+        r["table"][other, :] = nt(r["dq"][query_at, :], r["w_query"][...]).astype(jnp.bfloat16)
+
+    def bucket_rows(rows):
+        at = pl.ds(pl.multiple_of(4 * width + rows.start, PACK), rows.size)
+        r["rest"][at, :] = nn(r["hot"][rows, :], r["table"][...]).astype(jnp.bfloat16)
+
+    def token_rows(rows):
+        grad = nt(r["dk"][rows, :], r["w_key"][...]) + nt(r["dv"][rows, :], r["w_value"][...])
+        r["halo"][rows, :] = grad.astype(jnp.bfloat16)
+
+    output_copy = pltpu.make_async_copy(
+        r["output"], r["rest"].at[pl.ds(3 * width, width)], r["own_sem"].at[len(chunks)]
+    )
+    output_copy.start()
+    by_rows(width, 128, query_rows)
+    move((3, 2))
+    by_rows(width, 128, key_rows)
+    move((late[0], 0), (2, 3), (0, 6))
+    by_rows(width, 128, value_rows)
+    output_copy.wait()
+    move((late[1], 0), (late[0], 1), (3, 3), (2, 4), (1, 5))
+    by_rows(2 * SPAN, 128, table_rows)
+    by_rows(2 * SPAN, 128, bucket_rows)
+    move((late[2], 0), (late[1], 1), (late[0], 2), (3, 4), (2, 5), (1, 6), (0, 7))
+    by_rows(ext_len, 128, token_rows)
+    halos = []
+    for number, (at, device) in enumerate(((0, before), (ext_len - SPAN, after))):
+        copy = pltpu.make_async_remote_copy(
+            src_ref=r["halo"].at[pl.ds(at, SPAN)], dst_ref=r["halo_got"].at[number],
+            send_sem=r["halo_send"].at[number], recv_sem=r["halo_recv"].at[number],
+            device_id=device, device_id_type=MESH,
+        )
+        copy.start()
+        halos.append(copy)
+
+    def finish_tokens():
+        for copy in halos:
+            copy.wait()
+
+        def own_rows(rows):
+            mid = pl.ds(pl.multiple_of(SPAN + rows.start, PACK), rows.size)
+            grad = r["resid"][rows, :] + nt(r["dq"][rows, :], r["w_query"][...])
+            grad = grad + nt(r["dk"][mid, :], r["w_key"][...]) + nt(r["dv"][mid, :], r["w_value"][...])
+            for number in range(2):
+                grad = grad + r["halo_got"][number, rows, :].astype(jnp.float32)
+            outs["tokens_grad"][rows, :] = grad.astype(jnp.bfloat16)
+
+        by_rows(block_len, 128, own_rows)
+
+    left = [c for c in done if done[c] < total.last]
+    order = sorted(
+        (stage - done[c], stage, c) for c in left for stage in range(done[c] + 1, total.last + 1)
+    )
+    last_slot = 0
+    tokens_done = False
+    for slot, stage, c in order:
+        if slot == 3 and not tokens_done:
+            finish_tokens()
+            tokens_done = True
+        total.step(c, stage)
+    outs["vectors"][...] = vec.acc[len(total.lines)]
+
+
+def finish(inputs, seq_count):
+    unit_rows = PACK * 2 * seq_count
+    width = inputs["q"].shape[1]
+    block_len, ext_len = inputs["q"].shape[0], inputs["k"].shape[0]
+    spec = (("outer", 3), ("outer", 3), ("inner", 3), ("inner", 3), ("rest", 3), ("rest", 2), ("rest", 2))
+    chunks, rows = chunks_of(spec, unit_rows, width)
+    phases = [phases_of(chunk, seq_count) for chunk in chunks]
+    recv_rows = sum((count - 1) * high for chunk in phases for count, high in chunk)
+    sems = sum(2 * (count - 1) for chunk in phases for count, _ in chunk)
+    vec_slots = sum(count - 1 for count, _ in phases[0])
+    rest_rows = 4 * width + 2 * SPAN
+    bf = lambda *shape: pltpu.VMEM(shape, jnp.bfloat16)
+    f32 = lambda *shape: pltpu.VMEM(shape, jnp.float32)
+    dma = pltpu.SemaphoreType.DMA
+    vec_shape = inputs["vectors"].shape
+    in_hbm = ("outer", "inner", "output", "probs_in")
+    any_spec = pl.BlockSpec(memory_space=pl.ANY)
+    vmem = pl.BlockSpec(memory_space=pltpu.VMEM)
+    tiles = block_len // TILE
+    return pl.pallas_call(
+        functools.partial(finish_kernel, chunks, seq_count),
+        in_specs=[any_spec if name in in_hbm else vmem for name in FINISH_IN],
+        out_specs=[any_spec] * 3 + [vmem] * 2,
+        out_shape=[
+            jax.ShapeDtypeStruct(inputs["outer"].shape, jnp.bfloat16),
+            jax.ShapeDtypeStruct(inputs["inner"].shape, jnp.bfloat16),
+            jax.ShapeDtypeStruct((rest_rows, width), jnp.bfloat16),
+            jax.ShapeDtypeStruct(vec_shape, jnp.float32),
+            jax.ShapeDtypeStruct((block_len, width), jnp.bfloat16),
+        ],
+        scratch_shapes=[
+            bf(2, 2, tiles, REACH, TILE), bf(PAIR, block_len), bf(PAIR, ext_len),
+            f32(ext_len, PAIR), f32(ext_len, PAIR), f32(PAIR, 2 * SPAN), f32(PAIR, 2 * SPAN + 2 * TILE),
+            bf(block_len + 2 * SPAN, width), bf(ext_len + 2 * SPAN, width), bf(ext_len, width),
+            bf(rest_rows, width), bf(4 * SPAN, width), bf(ext_len, width), bf(2, SPAN, width),
+            bf(rows, width), bf(rows, width), bf(recv_rows, width),
+            f32(5, *vec_shape), f32(vec_slots, *vec_shape),
+            dma((len(chunks) + 1,)), dma((sems,)), dma((sems,)), dma((vec_slots,)), dma((vec_slots,)),
+            dma((2,)), dma((2,)), dma((2,)),
+        ],
+        compiler_params=pltpu.CompilerParams(
+            collective_id=0, has_side_effects=True, vmem_limit_bytes=60 * 2**20
+        ),
+        name="finish",
+    )(*(inputs[name] for name in FINISH_IN))
+
 norm_eps = 1e-07
 masked_score = -1e30
 
@@ -260,6 +754,51 @@
 
 def low(values):
     return values.astype(jnp.bfloat16)
+
+def finish_plain(inputs):
+    query, key_ext, value_ext = inputs["q"], inputs["k"], inputs["v"]
+    block_len, width = query.shape
+    w_query, w_key, w_value, hot = (inputs[name] for name in ("w_query", "w_key", "w_value", "hot"))
+    dquery, dkey, dvalue, drelk, drelq = attend_back(
+        query, key_ext, value_ext, inputs["grad"], inputs["probs_in"], inputs["relk"], inputs["relq"]
+    )
+    dkey = low(f32dot("ab,nbd->nad", unit(True), low(dkey).reshape(-1, TILE, width))).reshape(-1, width)
+    dvalue = low(dvalue)
+    drelk = low(drelk).T
+    drelq = low(drelq[:, TILE : TILE + 2 * SPAN]).T
+    query_part = f32dot("em,md->ed", inputs["xt_query"], jnp.concatenate([dquery, drelq]))
+    key_part = f32dot("em,md->ed", inputs["xt_key"], jnp.concatenate([dkey, drelk]))
+    value_part = f32dot("em,md->ed", inputs["xt_key"][:, : key_ext.shape[0]], dvalue)
+    table = jnp.concatenate(
+        [low(f32dot("md,ed->me", drelk, w_key)), low(f32dot("md,ed->me", drelq, w_query))]
+    )
+    table_part = f32dot("rm,me->re", hot, table)
+    rest = jnp.concatenate(
+        [low(query_part), low(key_part), low(value_part), inputs["output"], low(table_part)]
+    )
+    ext_grad = f32dot("td,ed->te", dkey, w_key) + f32dot("td,ed->te", dvalue, w_value)
+    tokens_grad = (
+        inputs["resid"]
+        + f32dot("td,ed->te", dquery, w_query)
+        + ext_grad[SPAN : SPAN + block_len]
+        + shifted(low(ext_grad[:SPAN]), "seq", -1).astype(jnp.float32)
+        + shifted(low(ext_grad[SPAN + block_len :]), "seq", 1).astype(jnp.float32)
+    )
+    both = ("rows", "seq")
+    sums = [
+        lax.all_gather(
+            lax.psum_scatter(part, both, scatter_dimension=0, tiled=True), both, axis=0, tiled=True
+        )
+        for part in (inputs["outer"], inputs["inner"], rest)
+    ]
+    return (*sums, lax.psum(inputs["vectors"], both), low(tokens_grad))
+
+
+def finish_of(inputs):
+    seq_count, rows_count = lax.axis_size("seq"), lax.axis_size("rows")
+    if rows_count == 2 and seq_count == 16:
+        return finish(inputs, seq_count)
+    return finish_plain(inputs)
 
 
 def shards(
@@ -275,6 +814,8 @@
     to_hot, from_hot = band_tables(rel_buckets)
     to_table = low(f32dot("mr,re->me", to_hot, rel_table))
     from_table = low(f32dot("mr,re->me", from_hot, rel_table))
+    to_table_t = low(f32dot("mr,re->em", to_hot, rel_table))
+    from_table_t = low(f32dot("mr,re->em", from_hot, rel_table))
     relk = low(f32dot("me,ed->md", to_table, w_key))
     relq = low(f32dot("me,ed->md", from_table, w_query))
     relq = jnp.pad(relq, ((TILE, TILE), (0, 0)))
@@ -304,56 +845,24 @@
     output_part = low(f32dot("dt,te->de", attn_t, mixed_low))
     attn_grad = low(f32dot("te,de->td", mixed_low, w_output))
 
-    dquery, dkey, dvalue, drelk, drelq = attend_back(
-        query, key_ext, value_ext, attn_grad, probs, relk, relq
-    )
-    pair = jnp.concatenate([dkey, dvalue], axis=1)
-    from_next = shifted(low(pair[:SPAN]), "seq", -1).astype(jnp.float32)
-    from_prev = shifted(low(pair[SPAN + block_len :]), "seq", 1).astype(jnp.float32)
-    pair = low(pair[SPAN : SPAN + block_len] + from_prev + from_next)
-    swap = unit(True)
-    dkey = low(
-        f32dot("ab,nbd->nad", swap, pair[:, :width].reshape(-1, TILE, width))
-    ).reshape(block_len, width)
-    dvalue = pair[:, width:]
-    drelk = low(drelk)
-    drelq = low(drelq[:, TILE : TILE + 2 * SPAN])
-    query_part = low(f32dot("te,td->ed", tokens, dquery) + f32dot("me,dm->ed", from_table, drelq))
-    key_part = low(f32dot("te,td->ed", tokens, dkey) + f32dot("me,dm->ed", to_table, drelk))
-    value_part = low(f32dot("te,td->ed", tokens, dvalue))
-    table_part = low(
-        f32dot("mr,me->re", to_hot, low(f32dot("dm,ed->me", drelk, w_key)))
-        + f32dot("mr,me->re", from_hot, low(f32dot("dm,ed->me", drelq, w_query)))
-    )
-    tokens_grad = low(
-        resid_grad
-        + f32dot("td,ed->te", dquery, w_query)
-        + f32dot("td,ed->te", dkey, w_key)
-        + f32dot("td,ed->te", dvalue, w_value)
-    )
-    norm_parts = lax.psum(
-        (mid_gain_part, mid_bias_part, end_gain_part, end_bias_part), ("rows", "seq")
-    )
-    groups = (
-        (outer_part,),
-        tuple(inner_part[:, at : at + width] for at in range(0, inner_part.shape[1], width)),
-        (query_part, key_part, value_part, output_part, table_part),
-    )
-    outs = []
-    for group in groups:
-        packed = jnp.concatenate(group, axis=0)
-        share = lax.psum_scatter(packed, ("rows", "seq"), scatter_dimension=0, tiled=True)
-        whole = lax.all_gather(share, ("rows", "seq"), axis=0, tiled=True).astype(jnp.float32)
-        pieces, at = [], 0
-        for piece in group:
-            pieces.append(whole[at : at + piece.shape[0]])
-            at += piece.shape[0]
-        outs.append(pieces)
-    (outer_w,), inner_w, (query_w, key_w, value_w, output_w, table_w) = outs
-    inner_w = jnp.concatenate(inner_w, axis=1)
+    inputs = {
+        "q": query, "k": key_ext, "v": value_ext, "grad": attn_grad, "relk": relk, "relq": relq,
+        "xt_key": jnp.concatenate([tokens_ext.T, to_table_t], axis=1),
+        "xt_query": jnp.concatenate([tokens.T, from_table_t], axis=1),
+        "w_query": w_query, "w_key": w_key, "w_value": w_value,
+        "hot": jnp.concatenate([to_hot.T, from_hot.T], axis=1), "resid": resid_grad,
+        "vectors": jnp.concatenate(
+            [mid_gain_part, mid_bias_part, end_gain_part, end_bias_part] * 2
+        ).reshape(8, width),
+        "outer": outer_part, "inner": inner_part, "output": output_part, "probs_in": probs,
+    }
+    outer_w, inner_w, rest_w, norm_parts, tokens_grad = finish_of(inputs)
+    query_w, key_w, value_w, output_w = (rest_w[at * width : (at + 1) * width] for at in range(4))
+    table_w = rest_w[4 * width :]
     return (
-        layer_out[None], tokens_grad[None], query_w, key_w, value_w, output_w, inner_w, outer_w,
-        table_w, *norm_parts,
+        layer_out[None], tokens_grad[None],
+        *(w.astype(jnp.float32) for w in (query_w, key_w, value_w, output_w, inner_w, outer_w, table_w)),
+        *(norm_parts[at] for at in range(4)),
     )
 
 

time: 653 us -> 304 us (0.47)
  waiting for transfers between devices: 412 us -> 0.01 us
  Pallas kernels: 47.3 us -> 212 us
  blocking collectives: 40.8 us -> 0 us
  matrix products: 67.9 us -> 43.7 us
  local copies, waits for them, and re-layouts: 30.1 us -> 9.24 us
  between operations: 15.1 us -> 1.15 us
  other arithmetic: 22.1 us -> 30.6 us
  starting transfers between devices: 14.3 us -> 7.17 us
    reduce_scatter x3 -> x0, waiting for transfers between devices: 243 us -> none  [shards(): lax.psum_scatter(packed, ('rows', 'seq'), scatter_dimension=0, tiled=True)]
    pallas_call x1, Pallas kernels: 28.1 us -> 192 us  [finish(): pl.pallas_call(functools.partial(finish_kernel, chunks, seq_count), in_sp...]
    all_gather x3 -> x0, waiting for transfers between devices: 142 us -> none  [shards(): lax.all_gather(share, ('rows', 'seq'), axis=0, tiled=True)]
    psum x1 -> x0, blocking collectives: 40.8 us -> none  [shards(): lax.psum((mid_gain_part, mid_bias_part, end_gain_part, end_bias_part), ('...]
    ppermute x4 -> x2, waiting for transfers between devices: 27.2 us -> 0.01 us  [shifted(): return lax.ppermute(shard, axis, pairs)]
    dot_general x27 -> x16, matrix products: 67.9 us -> 43.7 us  [f32dot(): return jnp.einsum(spec, left, right, preferred_element_type=jnp.float32)]
    slice x6 -> x1, local copies, waits for them, and re-layouts: 13.3 us -> 0.63 us  [shards(): norm_parts[at]]
    unnamed x121 -> x74, local copies, waits for them, and re-layouts: 11.8 us -> 1.11 us
  transfers between devices with their start and end apart: 10 -> 2, of which waited for: 8 -> 0; matrix products, arithmetic and copies ran while one was open for 12% -> 7% of each run, Pallas kernels for 4% -> 0%
where the time goes in v3:
time: 304 us; the launch traced here: 303 us
  Pallas kernels  212 us (70%)
  matrix products  43.7 us (14%)
  other arithmetic  30.6 us (10%)
  local copies, waits for them, and re-layouts  9.24 us (3%)
  starting transfers between devices  7.17 us (2%)
    pallas_call x1, Pallas kernels, finish(): pl.pallas_call(functools.partial(finish_kernel, chunks, seq_count), in_sp...  192 us
    dot_general x16, matrix products, f32dot(): return jnp.einsum(spec, left, right, preferred_element_type=jnp.float32)  43.7 us
    pallas_call x1, Pallas kernels, attend(): pl.pallas_call(attend_kernel, grid=(pairs,), in_specs=[pl.BlockSpec((bloc...  19.2 us
    convert_element_type x4, other arithmetic, shards(): w.astype(jnp.float32)  18.4 us
    ppermute x2, starting transfers between devices, shifted(): return lax.ppermute(shard, axis, pairs)  7.17 us
  transfers between devices with their start and end apart: 2, of which 0 were waited for; matrix products, arithmetic and copies ran while one was open for 7% of the time, Pallas kernels for 0%

profile of v3, /device:TPU:0, one launch (start us, length us, event | category | flops | bytes accessed | tf_op | source)
XLA Modules:
  0.0 303.4 jit_solution(9339434426945421114)
XLA Ops:
  0.6 0.0 copy-start
  0.7 0.0 copy-start.9
  0.7 5.9 %collective-permute-start = (bf16[256,768]{1,0:T(8,128)(2,1)}, bf16[256,768]{1,0:T(8,128)(2,1)}, u32[]{:S(2)}, u32[]{:S(2)}) collective-permute-start(bf16[256,768]{1,0:T(8,128)(2,1)} %bitcast.55), channel_id=1, source_target_pairs={{0,1},{1,2},{2,3},{3,4},{4,5},{5,6},{6,7},{7,8},{8,9},{9,10},{10,1... | collective-permute-start | bytes 1179656 | tf_op jit(solution)/shard_map/ppermute | solution.py:701
  6.6 1.3 collective-permute-start.1
  7.9 1.3 slice.39
  9.1 0.8 slice.40
  9.9 0.1 reverse.2
  10.0 0.1 slice.60
  10.1 0.7 fusion.24
  10.8 0.2 iota_compare_fusion.1
  10.9 0.9 iota_compare_fusion
  11.8 2.8 convolution_convert_fusion.7
  14.6 2.6 convolution_convert_fusion.8
  17.3 0.1 select_reduce_fusion
  17.4 0.1 convert_reduce_fusion.2
  17.5 0.1 convert_reduce_fusion.1
  17.6 0.0 copy-start.20
  17.6 1.2 convolution_convert_fusion.10.q_ref.refs_0_
  18.8 0.2 copy.35
  19.0 2.8 convolution_convert_fusion.5
  21.8 0.1 fusion.23
  21.9 2.2 add_convert_fusion.1.refs_11_
  24.1 2.4 pad_maximum_fusion.2.refs_7_
  26.5 0.1 pad.8.relq_ref.refs_5_
  26.6 0.0 copy-start.1
  26.6 1.6 fusion.15.bias_ref
  28.2 0.1 convert_reduce_fusion
  28.3 1.7 convolution_convert_fusion.6.relk_ref.refs_4_
  30.0 0.0 collective-permute-done
  30.0 3.2 %convolution_convert_fusion.3.refs_2_ = bf16[768,768]{1,0:T(8,128)(2,1)} fusion(bf16[768,768]{1,0:T(8,128)(2,1)S(1)} %copy-done.12, bf16[256,768]{1,0:T(8,128)(2,1)} %collective-permute-done.1, bf16[256,768]{1,0:T(8,128)(2,1)S(1)} %bitcast.58, bf16[256,768]{1,0:T(8,128)(2,1)} %collective-permute-done), kind=kOutput, calls=%fused_computation.22 | convolution fusion | flops 910098432 | bytes 3538944 | tf_op jit(solution)/shard_map/te,ed->td/dot_general | solution.py:711
  33.2 2.4 copy.34.vt_ref
  35.6 2.7 convolution_convert_fusion.4.k_ref.refs_1_
  38.4 0.0 copy-start.2
  38.4 19.2 %attend.1 = (bf16[768,256]{1,0:T(8,128)(2,1)S(1)}, bf16[12,2,640,128]{3,2,1,0:T(8,128)(2,1)}) custom-call(bf16[256,768]{1,0:T(8,128)(2,1)S(1)} %copy-done.4, bf16[768,768]{1,0:T(8,128)(2,1)S(1)} %convolution_convert_fusion.4.k_ref.refs_1_, bf16[768,768]{1,0:T(8,128)(2,1)S(1)} %copy-done.3, bf16[512,768]{1,0:T(8,128)(2,1)S(1)} %copy-done.5, ...), custom_call_target="tpu_custom_call" | custom-call | tf_op jit(solution)/shard_map/attend/pallas_call | solution.py:81
  57.7 0.6 fusion.37
  58.3 0.2 multiply_reduce_fusion.3
  58.5 0.0 slice-start.5
  58.5 10.2 %multiply_convert_fusion = (bf16[256,3072]{1,0:T(8,128)(2,1)S(1)}, f32[256,3072]{1,0:T(8,128)S(1)}, f32[256,3072]{1,0:T(8,128)S(1)}) fusion(bf16[768,3072]{1,0:T(8,128)(2,1)} %param.22, f32[256,768]{1,0:T(8,128)S(1)} %get-tuple-element.48, f32[768]{0:T(1024)S(1)} %copy-done.18, f32[768]{0:T(1024)S(1)} %copy-done.17, f32[256]{0:T(256)S(1)} %fusion.26, ...), kind=kOutput, calls=%fused_computation.5 | convolution fusion | flops 1260060672 | bytes 13377536 | tf_op jit(solution)/shard_map/td,df->tf/dot_general | solution.py:711
  68.8 0.0 copy-start.19
  68.8 0.0 copy-start.22
  68.8 1.5 fusion.38
  70.4 0.2 multiply_reduce_fusion.2
  70.6 0.4 fusion.11
  71.0 0.0 slice-start.6
  71.0 1.1 fusion.35
  72.2 2.1 add_convert_fusion
  74.3 1.8 multiply_reduce_fusion
  76.2 0.3 fusion.34
  76.5 0.1 broadcast_add_fusion.refs_12_
  76.6 1.3 convolution_convert_fusion.9.refs_3_
  77.9 1.5 convolution_convert_fusion.2.refs_16_
  79.4 3.8 %convolution_convert_fusion.refs_15_ = bf16[768,3072]{1,0:T(8,128)(2,1)} fusion(bf16[256,3072]{1,0:T(8,128)(2,1)S(1)} %add_convert_fusion, f32[256,768]{1,0:T(8,128)S(1)} %get-tuple-element.48, f32[768]{0:T(1024)S(1)} %copy-done.18, f32[768]{0:T(1024)S(1)} %copy-done.17, f32[256]{0:T(256)S(1)} %fusion.26, f32[256]{0:T(256)S(1)} %broadcast_multiply_fusion.1), kind=kOutput, calls=%fused_computation | convolution fusion | flops 1211301888 | bytes 7086080 | tf_op jit(solution)/shard_map/td,tf->df/dot_general | solution.py:711
  83.2 3.7 %convolution_convert_fusion.1.refs_14_ = bf16[3072,768]{1,0:T(8,128)(2,1)} fusion(bf16[256,3072]{1,0:T(8,128)(2,1)S(1)} %get-tuple-element.40, f32[256,768]{1,0:T(8,128)S(1)} %get-tuple-element.39, f32[256]{0:T(256)S(1)} %negate_multiply_fusion.2), kind=kOutput, calls=%fused_computation.1 | convolution fusion | flops 1210712064 | bytes 7078912 | tf_op jit(solution)/shard_map/tf,td->fd/dot_general | solution.py:711
  86.9 1.2 fusion.30
  88.1 0.1 pad_maximum_fusion
  88.2 2.3 copy.36.refs_6_
  90.6 0.6 reshape.150.refs_13_
  91.2 192.4 %finish.1 = (bf16[3072,768]{1,0:T(8,128)(2,1)}, bf16[768,3072]{1,0:T(8,128)(2,1)}, bf16[3584,768]{1,0:T(8,128)(2,1)}, f32[8,768]{1,0:T(8,128)}, bf16[256,768]{1,0:T(8,128)(2,1)}) custom-call(bf16[256,768]{1,0:T(8,128)(2,1)} %convolution_convert_fusion.10.q_ref.refs_0_, bf16[768,768]{1,0:T(8,128)(2,1)} %copy-done.2, ...), custom_call_target="tpu_custom_call" | custom-call | tf_op jit(solution)/shard_map/finish/pallas_call | solution.py:667
  283.6 2.5 slice_convert_fusion.4
  286.1 6.3 %slice_convert_fusion = (f32[768,768]{1,0:T(8,128)}, f32[768,768]{1,0:T(8,128)}, f32[768,768]{1,0:T(8,128)}, f32[768,768]{1,0:T(8,128)}) fusion(bf16[3584,768]{1,0:T(8,128)(2,1)} %get-tuple-element.23), kind=kLoop, calls=%fused_computation.37 | loop fusion | flops 2359296 | bytes 14155776 | tf_op jit(solution)/shard_map/convert_element_type | solution.py:864
  292.4 0.6 slice_reduce_fusion
  293.1 5.0 %convert_element_type.132 = f32[768,3072]{1,0:T(8,128)} convert(bf16[768,3072]{1,0:T(8,128)(2,1)S(1)} %bitcast.65) | non-fusion elementwise | flops 2359296 | bytes 14155776 | tf_op jit(solution)/shard_map/convert_element_type | solution.py:864
  298.1 4.5 %convert_element_type.133 = f32[3072,768]{1,0:T(8,128)} convert(bf16[3072,768]{1,0:T(8,128)(2,1)S(1)} %bitcast.63) | non-fusion elementwise | flops 2359296 | bytes 14155776 | tf_op jit(solution)/shard_map/convert_element_type | solution.py:864
  302.6 0.7 copy.47
  (80 shorter events, 0.2 us)
Async XLA Ops:
  0.6 57.0 %copy-start = (bf16[768,768]{1,0:T(8,128)(2,1)S(1)}, bf16[768,768]{1,0:T(8,128)(2,1)}, u32[]{:S(2)}) copy-start(bf16[768,768]{1,0:T(8,128)(2,1)} %param.21) | copy-start | bytes 3538948
  0.7 16.9 %copy-start.8 = (bf16[1,256,768]{2,1,0:T(8,128)(2,1)S(1)}, bf16[1,256,768]{2,1,0:T(8,128)(2,1)}, u32[]{:S(2)}) copy-start(bf16[1,256,768]{2,1,0:T(8,128)(2,1)} %param.16) | copy-start | bytes 1179652
  0.7 16.6 %copy-start.23 = (s32[1,4]{1,0:T(1,128)S(1)}, s32[1,4]{1,0:T(1,128)}, u32[]{:S(2)}) copy-start(s32[1,4]{1,0:T(1,128)} %param.29) | copy-start | bytes 52
  0.7 16.9 %copy-start.9 = (bf16[768,768]{1,0:T(8,128)(2,1)S(1)}, bf16[768,768]{1,0:T(8,128)(2,1)}, u32[]{:S(2)}) copy-start(bf16[768,768]{1,0:T(8,128)(2,1)} %refs_8_.1) | copy-start | bytes 3538948
  0.7 29.3 %collective-permute-start = (bf16[256,768]{1,0:T(8,128)(2,1)}, bf16[256,768]{1,0:T(8,128)(2,1)}, u32[]{:S(2)}, u32[]{:S(2)}) collective-permute-start(bf16[256,768]{1,0:T(8,128)(2,1)} %bitcast.55), channel_id=1, source_target_pairs={{0,1},{1,2},{2,3},{3,4},{4,5},{5,6},{6,7},{7,8},{8,9},{9,10},{10,1... | collective-permute-start | bytes 1179656 | tf_op jit(solution)/shard_map/ppermute | solution.py:701
  6.6 23.4 %collective-permute-start.1 = (bf16[256,768]{1,0:T(8,128)(2,1)}, bf16[256,768]{1,0:T(8,128)(2,1)}, u32[]{:S(2)}, u32[]{:S(2)}) collective-permute-start(bf16[256,768]{1,0:T(8,128)(2,1)} %bitcast.56), channel_id=1, source_target_pairs={{1,0},{2,1},{3,2},{4,3},{5,4},{6,5},{7,6},{8,7},{9,8},{10,9},{11,1... | collective-permute-start | bytes 1179656 | tf_op jit(solution)/shard_map/ppermute | solution.py:701
  17.6 4.3 %copy-start.20 = (s32[1,4096]{1,0:T(1,128)S(1)}, s32[1,4096]{1,0:T(1,128)}, u32[]{:S(2)}) copy-start(s32[1,4096]{1,0:T(1,128)} %param.30) | copy-start | bytes 49156
  21.8 4.7 %copy-start.13 = (bf16[512,768]{1,0:T(8,128)(2,1)S(1)}, bf16[512,768]{1,0:T(8,128)(2,1)}, u32[]{:S(2)}) copy-start(bf16[512,768]{1,0:T(8,128)(2,1)} %convolution_convert_fusion.5) | copy-start | bytes 2359300
  21.9 6.3 %copy-start.10 = (bf16[1,256,768]{2,1,0:T(8,128)(2,1)S(1)}, bf16[1,256,768]{2,1,0:T(8,128)(2,1)}, u32[]{:S(2)}) copy-start(bf16[1,256,768]{2,1,0:T(8,128)(2,1)} %param.17) | copy-start | bytes 1179652
  24.1 4.2 %copy-start.11 = (bf16[768,768]{1,0:T(8,128)(2,1)S(1)}, bf16[768,768]{1,0:T(8,128)(2,1)}, u32[]{:S(2)}) copy-start(bf16[768,768]{1,0:T(8,128)(2,1)} %refs_9_.1) | copy-start | bytes 3538948
  24.1 4.2 %copy-start.14 = (bf16[512,768]{1,0:T(8,128)(2,1)S(1)}, bf16[512,768]{1,0:T(8,128)(2,1)}, u32[]{:S(2)}) copy-start(bf16[512,768]{1,0:T(8,128)(2,1)} %convolution_convert_fusion.8) | copy-start | bytes 2359300
  26.5 3.5 %copy-start.12 = (bf16[768,768]{1,0:T(8,128)(2,1)S(1)}, bf16[768,768]{1,0:T(8,128)(2,1)}, u32[]{:S(2)}) copy-start(bf16[768,768]{1,0:T(8,128)(2,1)} %refs_10_.1) | copy-start | bytes 3538948
  26.6 11.8 %copy-start.1 = (bf16[768,768]{1,0:T(8,128)(2,1)}, bf16[768,768]{1,0:T(8,128)(2,1)S(1)}, u32[]{:S(2)}) copy-start(bf16[768,768]{1,0:T(8,128)(2,1)S(1)} %pad.8.relq_ref.refs_5_) | copy-start | bytes 3538948
  35.6 2.8 copy-start.3
  35.6 2.8 copy-start.4
  35.6 2.8 copy-start.5
  35.6 2.8 copy-start.6
  38.4 19.8 %copy-start.2 = (bf16[768,768]{1,0:T(8,128)(2,1)}, bf16[768,768]{1,0:T(8,128)(2,1)S(1)}, u32[]{:S(2)}) copy-start(bf16[768,768]{1,0:T(8,128)(2,1)S(1)} %convolution_convert_fusion.4.k_ref.refs_1_) | copy-start | bytes 3538948
  57.6 0.9 copy-start.17
  57.6 0.9 copy-start.18
  57.7 11.1 %slice-start.4 = ((s8[4718592]{0:T(1024)(128)(4,1)}), s8[4194304]{0:T(1024)(128)(4,1)S(1)}, s32[]{:S(2)}) async-start(s8[4718592]{0:T(1024)(128)(4,1)} %bitcast.71), calls=%async_computation.4 | async-start | bytes 8388608
  58.5 10.3 %slice-start.5 = ((s8[4718592]{0:T(1024)(128)(4,1)}), s8[524288]{0:T(1024)(128)(4,1)S(1)}, s32[]{:S(2)}) async-start(s8[4718592]{0:T(1024)(128)(4,1)} %bitcast.71), calls=%async_computation.5 | async-start | bytes 1048576
  68.8 1.8 copy-start.19
  68.8 2.2 copy-start.22
  71.0 3.3 %slice-start.6 = ((s8[4718592]{0:T(1024)(128)(4,1)}), s8[4194304]{0:T(1024)(128)(4,1)S(1)}, s32[]{:S(2)}) async-start(s8[4718592]{0:T(1024)(128)(4,1)} %bitcast.73), calls=%async_computation.6 | async-start | bytes 8388608
  72.2 2.1 slice-start.7
  76.6 6.5 %copy-start.7 = (f32[256,768]{1,0:T(8,128)}, f32[256,768]{1,0:T(8,128)S(1)}, u32[]{:S(2)}) copy-start(f32[256,768]{1,0:T(8,128)S(1)} %broadcast_add_fusion.refs_12_) | copy-start | bytes 2359300
  83.2 4.9 %copy-start.15 = (bf16[512,768]{1,0:T(8,128)(2,1)S(1)}, bf16[512,768]{1,0:T(8,128)(2,1)}, u32[]{:S(2)}) copy-start(bf16[512,768]{1,0:T(8,128)(2,1)} %convolution_convert_fusion.8) | copy-start | bytes 2359300
  283.6 9.5 %slice-start.2 = ((s8[4718592]{0:T(1024)(128)(4,1)}), s8[4194304]{0:T(1024)(128)(4,1)S(1)}, s32[]{:S(2)}) async-start(s8[4718592]{0:T(1024)(128)(4,1)} %bitcast.64), calls=%async_computation.2 | async-start | bytes 8388608
  286.1 6.3 %copy-start.21 = (f32[8,768]{1,0:T(8,128)S(1)}, f32[8,768]{1,0:T(8,128)}, u32[]{:S(2)}) copy-start(f32[8,768]{1,0:T(8,128)} %get-tuple-element.26) | copy-start | bytes 73732
  286.1 7.0 %slice-start.3 = ((s8[4718592]{0:T(1024)(128)(4,1)}), s8[524288]{0:T(1024)(128)(4,1)S(1)}, s32[]{:S(2)}) async-start(s8[4718592]{0:T(1024)(128)(4,1)} %bitcast.64), calls=%async_computation.3 | async-start | bytes 1048576
  286.1 12.0 %slice-start = ((s8[4718592]{0:T(1024)(128)(4,1)}), s8[4194304]{0:T(1024)(128)(4,1)S(1)}, s32[]{:S(2)}) async-start(s8[4718592]{0:T(1024)(128)(4,1)} %bitcast.62), calls=%async_computation | async-start | bytes 8388608
  292.4 5.7 %slice-start.1 = ((s8[4718592]{0:T(1024)(128)(4,1)}), s8[524288]{0:T(1024)(128)(4,1)S(1)}, s32[]{:S(2)}) async-start(s8[4718592]{0:T(1024)(128)(4,1)} %bitcast.62), calls=%async_computation.1 | async-start | bytes 1048576
  298.1 4.5 %copy-start.16 = (bf16[256,768]{1,0:T(8,128)(2,1)S(1)}, bf16[256,768]{1,0:T(8,128)(2,1)}, u32[]{:S(2)}) copy-start(bf16[256,768]{1,0:T(8,128)(2,1)} %get-tuple-element.22) | copy-start | bytes 1179652

commit v4 on v3

v4 whole, which is shorter than its diff:
```python
import functools
import math

import jax
import jax.numpy as jnp
from jax import lax
from jax.experimental import pallas as pl
from jax.experimental.pallas import tpu as pltpu
from jax.sharding import PartitionSpec as P

H = 12
DH = 64
SPAN = 256
TILE = 128
REACH = 640
PAIR = 128
score_scale = 1.0 / math.sqrt(3 * DH)


def nt(left, right):
    return lax.dot_general(left, right, (((1,), (1,)), ((), ())), preferred_element_type=jnp.float32)


def nn(left, right):
    return lax.dot_general(left, right, (((1,), (0,)), ((), ())), preferred_element_type=jnp.float32)


def head_lanes(values, head):
    lane = lax.broadcasted_iota(jnp.int32, values.shape, 1)
    mine = (lane < DH) if head == 0 else (lane >= DH)
    return jnp.where(mine, values, jnp.zeros_like(values))


def unit(reverse):
    row = lax.broadcasted_iota(jnp.int32, (TILE, TILE), 0)
    col = lax.broadcasted_iota(jnp.int32, (TILE, TILE), 1)
    hit = (row + col == TILE - 1) if reverse else (row == col)
    return jnp.where(hit, 1.0, 0.0).astype(jnp.bfloat16)


def attend_back_kernel(
    q_ref, k_ref, v_ref, grad_ref, prob_ref, relk_ref, relq_ref,
    dq_ref, dk_ref, dv_ref, drelk_ref, drelq_ref, qt_ref, kt_ref,
):
    swap = unit(True)
    for source, result in ((q_ref, qt_ref), (k_ref, kt_ref)):
        for at in range(0, source.shape[0], TILE):
            flipped = nn(swap, source[pl.ds(at, TILE), :])
            result[:, pl.ds(at, TILE)] = flipped.T.astype(jnp.bfloat16)
    row = lax.broadcasted_iota(jnp.int32, (TILE, TILE), 0)
    col = lax.broadcasted_iota(jnp.int32, (TILE, TILE), 1)
    parts = REACH // TILE
    tiles = q_ref.shape[0] // TILE
    dk_ref[...] = jnp.zeros_like(dk_ref)
    dv_ref[...] = jnp.zeros_like(dv_ref)
    drelk_ref[...] = jnp.zeros_like(drelk_ref)
    drelq_ref[...] = jnp.zeros_like(drelq_ref)
    for tile in range(tiles):
        first = tile * TILE
        q_tile = q_ref[pl.ds(first, TILE), :]
        grad_tile = grad_ref[pl.ds(first, TILE), :]
        v_tile = v_ref[pl.ds(first, REACH), :]
        q_heads = [head_lanes(q_tile, head) for head in range(2)]
        grad_heads = [head_lanes(grad_tile, head) for head in range(2)]
        dq_heads = []
        lefts = [[] for _ in range(parts)]
        for head in range(2):
            lanes = pl.ds(head * DH, DH)
            probs = prob_ref[head, tile].astype(jnp.float32)
            weighted = probs * nt(v_tile, grad_heads[head])
            delta = jnp.sum(weighted, axis=0, keepdims=True)
            dscore = ((weighted - probs * delta) * score_scale).astype(jnp.bfloat16)
            turned = nt(swap, dscore)
            dband = pltpu.roll(turned, REACH - TILE + 1, 1, stride=1, stride_axis=0)
            dband = dband[:, : 2 * SPAN].astype(jnp.bfloat16)
            dq_heads.append(
                nn(turned.astype(jnp.bfloat16), k_ref[pl.ds(first, REACH), :])
                + nn(dband, relk_ref[...])
            )
            drelk_ref[lanes, :] += nn(qt_ref[lanes, pl.ds(first, TILE)], dband)
            for part in range(parts):
                flipped = nn(swap, dscore[part * TILE : (part + 1) * TILE, :])
                spun = pltpu.roll(flipped, 0, 1, stride=1, stride_axis=0)
                low = jnp.where(col >= row, spun, 0.0)
                dfrom = jnp.concatenate([low, spun - low], axis=1).astype(jnp.bfloat16)
                window = pl.ds((parts - 1 - part) * TILE, 2 * TILE)
                drelq_ref[lanes, window] += nn(kt_ref[lanes, pl.ds(first + part * TILE, TILE)], dfrom)
                lefts[part] += [flipped.astype(jnp.bfloat16), dfrom]
        dq_turned = jnp.where(col < DH, dq_heads[0], dq_heads[1]).astype(jnp.bfloat16)
        dq_ref[pl.ds(first, TILE), :] = nn(swap, dq_turned).astype(dq_ref.dtype)
        dv_ref[pl.ds(first, REACH), :] += nn(
            jnp.concatenate([prob_ref[0, tile], prob_ref[1, tile]], axis=1),
            jnp.concatenate(grad_heads, axis=0),
        )
        for part in range(parts):
            window = relq_ref[pl.ds((parts - 1 - part) * TILE, 2 * TILE), :]
            right = jnp.concatenate(
                [q_heads[0], head_lanes(window, 0), q_heads[1], head_lanes(window, 1)], axis=0
            )
            dk_ref[pl.ds(first + part * TILE, TILE), :] += nn(
                jnp.concatenate(lefts[part], axis=1), right
            )


def attend_back(query, key_ext, value_ext, grad, probs, relk, relq):
    block_len, width = query.shape
    ext_len = key_ext.shape[0]
    tiles = block_len // TILE
    pairs = width // PAIR
    table = 2 * SPAN
    cols = lambda n: pl.BlockSpec((n, PAIR), lambda p: (0, p))
    rows = lambda n: pl.BlockSpec((PAIR, n), lambda p: (p, 0))
    f32 = lambda *s: jax.ShapeDtypeStruct(s, jnp.float32)
    return pl.pallas_call(
        attend_back_kernel,
        grid=(pairs,),
        in_specs=[
            cols(block_len), cols(ext_len), cols(ext_len), cols(block_len),
            pl.BlockSpec((2, tiles, REACH, TILE), lambda p: (p, 0, 0, 0)),
            cols(table), cols(table + 2 * TILE),
        ],
        out_specs=[cols(block_len), cols(ext_len), cols(ext_len), rows(table), rows(table + 2 * TILE)],
        out_shape=[
            jax.ShapeDtypeStruct((block_len, width), jnp.bfloat16),
            f32(ext_len, width), f32(ext_len, width), f32(width, table), f32(width, table + 2 * TILE),
        ],
        scratch_shapes=[
            pltpu.VMEM((PAIR, block_len), jnp.bfloat16), pltpu.VMEM((PAIR, ext_len), jnp.bfloat16),
        ],
        compiler_params=pltpu.CompilerParams(vmem_limit_bytes=48 * 2**20),
        name="attend_back",
    )(query, key_ext, value_ext, grad, probs, relk, relq)


MESH = pl.DeviceIdType.MESH
PACK = 16


norm_eps = 1e-07
masked_score = -1e30
inverse_root_two = math.sqrt(0.5)
density_at_zero = 1.0 / math.sqrt(2.0 * math.pi)


def gelu_both(values):
    size = jnp.abs(values) * inverse_root_two
    t = 1.0 / (1.0 + 0.3275911 * size)
    poly = 1.061405429 * t - 1.453152027
    poly = poly * t + 1.421413741
    poly = poly * t - 0.284496736
    poly = poly * t + 0.254829592
    bell = jnp.exp(-size * size)
    tail = 0.5 * poly * t * bell
    share = jnp.where(values >= 0.0, 1.0 - tail, tail)
    return values * share, share + values * bell * density_at_zero


def mean_of(values):
    return jnp.mean(values, axis=-1, keepdims=True)


def by_blocks(width, body, step=256):
    def one(i, carry):
        body(pl.ds(pl.multiple_of(i * step, step), step))
        return carry

    lax.fori_loop(0, width // step, one, 0)


def column_of(row_values):
    row = lax.broadcasted_iota(jnp.int32, (TILE, TILE), 0)
    col = lax.broadcasted_iota(jnp.int32, (TILE, TILE), 1)
    return jnp.sum(jnp.where(row == col, row_values, 0), axis=1, keepdims=True)


def mask_of(r, seq_count):
    ext_len, block_len = r["bias"].shape
    place = lax.axis_index("seq")
    row_len = block_len * seq_count
    ends, end = [], 0
    for number in range(r["lengths"].shape[1]):
        end = end + r["lengths"][0, number]
        ends.append(end)

    def segment(slots):
        return sum((slots >= end).astype(jnp.int32) for end in ends)

    query = place * block_len + lax.broadcasted_iota(jnp.int32, (1, block_len), 1)
    query_segment = segment(query)
    for block in range(ext_len // TILE):
        first = place * block_len - SPAN + block * TILE
        line = lax.clamp(0, place * (block_len // TILE) - SPAN // TILE + block, row_len // TILE - 1)
        keep = column_of(r["keep"][pl.ds(line, 1), :])
        key = first + lax.broadcasted_iota(jnp.int32, (TILE, 1), 0)
        key_segment = jnp.where((key >= 0) & (key < row_len), segment(key), -1)
        apart = key - query
        seen = (key_segment == query_segment) & (jnp.abs(apart) < SPAN)
        seen = seen & ((keep == 1) | (apart == 0))
        r["bias"][pl.ds(block * TILE, TILE), :] = jnp.where(seen, 0.0, masked_score)


def attend_pair(pair, buf, r):
    eye = unit(False)
    log_two = score_scale * math.log2(math.e)
    lanes = pl.ds(pl.multiple_of(pair * PAIR, PAIR), PAIR)
    tiles = r["q"].shape[0] // TILE
    parts = REACH // TILE
    for at in range(0, r["v"].shape[0], TILE):
        r["vt"][:, pl.ds(at, TILE)] = r["v"][pl.ds(at, TILE), lanes].T
    for tile in range(tiles):
        first = tile * TILE
        q_tile = r["q"][pl.ds(first, TILE), lanes]
        outs = []
        for head in range(2):
            score_ref = r["scores"].at[head]
            q_head = head_lanes(q_tile, head)
            band = nt(q_head, r["relk"][:, lanes])
            band = jnp.concatenate([band, jnp.zeros((TILE, REACH - 2 * SPAN), jnp.float32)], axis=1)
            to_term = pltpu.roll(band, 0, 1, stride=1, stride_axis=0).astype(jnp.bfloat16)
            for part in range(parts):
                at = first + part * TILE
                k_part = r["k"][pl.ds(at, TILE), lanes]
                window = r["relq"][pl.ds((parts - 1 - part) * TILE, 2 * TILE), lanes]
                from_band = nt(head_lanes(k_part, head), window)
                from_term = pltpu.roll(from_band, TILE + 1, 1, stride=1, stride_axis=0)[:, :TILE]
                left = jnp.concatenate([k_part, eye], axis=1)
                right = jnp.concatenate([q_head, to_term[:, part * TILE : (part + 1) * TILE]], axis=1)
                score_ref[pl.ds(part * TILE, TILE), :] = (
                    nt(left, right) + from_term + r["bias"][pl.ds(at, TILE), pl.ds(first, TILE)]
                )
            scores = score_ref[...]
            top = jnp.max(scores, axis=0, keepdims=True)
            weights = jnp.exp2((scores - top) * log_two)
            total = jnp.sum(weights, axis=0, keepdims=True)
            probs = (weights * (1.0 / total)).astype(jnp.bfloat16)
            r["probs"][buf, head, tile] = probs
            outs.append(nn(r["vt"][pl.ds(head * DH, DH), pl.ds(first, REACH)], probs))
        both = jnp.concatenate(outs, axis=0)
        r["attn_t"][lanes, pl.ds(first, TILE)] = both.astype(jnp.bfloat16)
        r["attn"][pl.ds(first, TILE), lanes] = both.T.astype(jnp.bfloat16)


START_HBM = (
    "tokens", "rel_table", "w_query", "w_key", "w_value", "w_output", "w_inner", "w_outer", "cotangent",
)
START_VMEM = ("rel_buckets", "mid_gain", "mid_bias", "end_gain", "end_bias", "keep")
START_IN = START_HBM + START_VMEM + ("lengths",)
START_KEPT = (
    "x", "q", "k", "v", "relk", "relq", "to_table", "from_table", "hot", "grad", "resid",
    "outer", "inner", "output",
)
START_OUT = START_KEPT + ("probs_out", "layer_out", "vectors")
START_SCRATCH = START_KEPT + (
    "rel_table", "w_query", "w_key", "w_value", "w_output", "w_inner", "w_outer", "cotangent",
    "bias", "vt", "scores", "probs", "attn", "attn_t", "mixed", "hidden", "z_mid", "root_mid", "hidden_low",
    "active", "slope", "inner_low", "sum_grad", "outer_low",
    "load_sem", "keep_sem", "probs_sem", "send_sem", "recv_sem",
)


def start_kernel(seq_count, *refs):
    given = dict(zip(START_IN, refs))
    outs = dict(zip(START_OUT, refs[len(START_IN) :]))
    r = dict(zip(START_SCRATCH, refs[len(START_IN) + len(START_OUT) :]))
    r.update((name, given[name]) for name in START_VMEM + ("lengths",))
    block_len, width = r["q"].shape
    ext_len, table_len = r["x"].shape[0], r["to_table"].shape[0]
    inner_width = r["w_inner"].shape[1]
    pairs = width // PAIR
    own = pl.ds(SPAN, block_len)

    loads = {}
    for number, name in enumerate(START_HBM):
        target = r["x"].at[own] if name == "tokens" else r[name]
        loads[name] = pltpu.make_async_copy(given[name], target, r["load_sem"].at[number])
        loads[name].start()
    row, place = lax.axis_index("rows"), lax.axis_index("seq")
    before = {"rows": row, "seq": lax.rem(place + seq_count - 1, seq_count)}
    after = {"rows": row, "seq": lax.rem(place + 1, seq_count)}
    barrier = pltpu.get_barrier_semaphore()
    for device in (before, after):
        pl.semaphore_signal(barrier, inc=1, device_id=device, device_id_type=MESH)
    pl.semaphore_wait(barrier, 2)
    halos = [
        pltpu.make_async_remote_copy(
            src_ref=given["tokens"], dst_ref=r["x"].at[pl.ds(at, SPAN)], send_sem=r["send_sem"].at[number],
            recv_sem=r["recv_sem"].at[number], device_id=device, device_id_type=MESH,
        )
        for number, (at, device) in enumerate(((0, after), (SPAN + block_len, before)))
    ]
    for copy in halos:
        copy.start()

    def keep(name):
        pltpu.make_async_copy(r[name], outs[name], r["keep_sem"].at[START_KEPT.index(name)]).start()

    def low(values):
        return values.astype(jnp.bfloat16)

    place_of = lax.broadcasted_iota(jnp.int32, (table_len, table_len), 0)
    turned_bucket = pltpu.roll(r["rel_buckets"][...].reshape(1, table_len), table_len - 1, 1)
    to_pos = jnp.clip(turned_bucket + SPAN, 0, table_len - 1)
    from_pos = jnp.clip(SPAN - turned_bucket, 0, table_len - 1)
    r["hot"][:, pl.ds(table_len, table_len)] = low(jnp.where(place_of == from_pos, 1.0, 0.0))
    to_turned = low(jnp.where(place_of == to_pos, 1.0, 0.0))
    for at in range(0, table_len, TILE):
        r["hot"][:, pl.ds(at, TILE)] = low(
            nn(to_turned[:, table_len - TILE - at : table_len - at], unit(True))
        )
    keep("hot")
    mask_of(r, seq_count)
    loads["rel_table"].wait()
    for number, name in enumerate(("to", "from")):
        hot = r["hot"][:, pl.ds(number * table_len, table_len)].T

        def table_cols(cols, hot=hot, name=name):
            r[name + "_table"][:, cols] = low(nn(hot, r["rel_table"][:, cols]))

        by_blocks(width, table_cols)
        keep(name + "_table")
    loads["w_query"].wait()
    loads["tokens"].wait()
    r["relq"][pl.ds(0, TILE), :] = jnp.zeros((TILE, width), jnp.bfloat16)
    r["relq"][pl.ds(TILE + table_len, TILE), :] = jnp.zeros((TILE, width), jnp.bfloat16)

    def query_cols(cols):
        r["q"][:, cols] = low(nn(r["x"][own, :], r["w_query"][:, cols]))
        r["relq"][pl.ds(TILE, table_len), cols] = low(nn(r["from_table"][...], r["w_query"][:, cols]))

    by_blocks(width, query_cols)
    keep("q")
    keep("relq")
    loads["w_key"].wait()

    def relk_cols(cols):
        r["relk"][:, cols] = low(nn(r["to_table"][...], r["w_key"][:, cols]))

    by_blocks(width, relk_cols)
    keep("relk")
    loads["w_value"].wait()
    for copy in halos:
        copy.wait()
    keep("x")

    def pair_cols(cols):
        r["k"][:, cols] = low(nn(r["x"][...], r["w_key"][:, cols]))
        r["v"][:, cols] = low(nn(r["x"][...], r["w_value"][:, cols]))

    by_blocks(width, pair_cols)
    keep("k")
    keep("v")

    def probs_copy(pair, buf):
        return pltpu.make_async_copy(
            r["probs"].at[buf], outs["probs_out"].at[pl.ds(2 * pair, 2)], r["probs_sem"].at[buf]
        )

    def one_pair(pair, carry):
        buf = lax.rem(pair, 2)

        @pl.when(pair >= 2)
        def _():
            probs_copy(pair - 2, buf).wait()

        attend_pair(pair, buf, r)
        probs_copy(pair, buf).start()
        return carry

    lax.fori_loop(0, pairs, one_pair, 0)

    for name in ("w_output", "w_inner", "w_outer", "cotangent"):
        loads[name].wait()

    def mixed_cols(cols):
        r["mixed"][:, cols] = nn(r["attn"][...], r["w_output"][:, cols])

    by_blocks(width, mixed_cols)
    high = 64
    mid_gain, mid_bias, end_gain, end_bias = (
        r[name][...].reshape(1, width) for name in ("mid_gain", "mid_bias", "end_gain", "end_bias")
    )

    def mid_rows(rows):
        mine = pl.ds(pl.multiple_of(SPAN + rows.start, high), high)
        values = r["x"][mine, :].astype(jnp.float32) + r["mixed"][rows, :]
        centre = values - mean_of(values)
        root = lax.rsqrt(mean_of(centre * centre) + norm_eps)
        z = centre * root
        hidden = z * mid_gain + mid_bias
        r["z_mid"][rows, :] = z
        r["root_mid"][rows, :] = jnp.broadcast_to(root, (high, TILE))
        r["hidden"][rows, :] = hidden
        r["hidden_low"][rows, :] = low(hidden)

    by_blocks(block_len, mid_rows, high)

    def active_cols(cols):
        active, slope = gelu_both(nn(r["hidden_low"][...], r["w_inner"][:, cols]))
        r["active"][:, cols] = low(active)
        r["slope"][:, cols] = low(slope)

    by_blocks(inner_width, active_cols)

    def outer_cols(cols):
        r["mixed"][:, cols] = nn(r["active"][...], r["w_outer"][:, cols])

    by_blocks(width, outer_cols)
    outs["vectors"][...] = jnp.zeros_like(outs["vectors"])

    def end_rows(rows):
        values = r["hidden"][rows, :] + r["mixed"][rows, :]
        centre = values - mean_of(values)
        root = lax.rsqrt(mean_of(centre * centre) + norm_eps)
        z = centre * root
        outs["layer_out"][rows, :] = low(z * end_gain + end_bias)
        cotangent = r["cotangent"][rows, :].astype(jnp.float32)
        outs["vectors"][pl.ds(2, 1), :] += jnp.sum(cotangent * z, axis=0, keepdims=True)
        outs["vectors"][pl.ds(3, 1), :] += jnp.sum(cotangent, axis=0, keepdims=True)
        grad = cotangent * end_gain
        sum_grad = root * (grad - mean_of(grad) - z * mean_of(grad * z))
        r["sum_grad"][rows, :] = sum_grad
        r["outer_low"][rows, :] = low(sum_grad)

    by_blocks(block_len, end_rows, high)

    def inner_cols(cols):
        grad = nt(r["outer_low"][...], r["w_outer"][cols, :])
        r["inner_low"][:, cols] = low(grad * r["slope"][:, cols].astype(jnp.float32))

    by_blocks(inner_width, inner_cols)

    def outer_part(rows):
        r["outer"][rows, :] = low(nn(r["active"][:, rows].T, r["outer_low"][...]))

    by_blocks(inner_width, outer_part)
    keep("outer")

    def hidden_cols(cols):
        r["mixed"][:, cols] = r["sum_grad"][:, cols] + nt(r["inner_low"][...], r["w_inner"][cols, :])

    by_blocks(width, hidden_cols)
    hidden_t = r["hidden_low"][...].T

    def inner_part(cols):
        r["inner"][:, cols] = low(nn(hidden_t, r["inner_low"][:, cols]))

    by_blocks(inner_width, inner_part)
    keep("inner")

    def resid_rows(rows):
        hidden_grad, z = r["mixed"][rows, :], r["z_mid"][rows, :]
        outs["vectors"][pl.ds(0, 1), :] += jnp.sum(hidden_grad * z, axis=0, keepdims=True)
        outs["vectors"][pl.ds(1, 1), :] += jnp.sum(hidden_grad, axis=0, keepdims=True)
        grad = hidden_grad * mid_gain
        root = r["root_mid"][rows, pl.ds(0, 1)]
        resid = root * (grad - mean_of(grad) - z * mean_of(grad * z))
        r["resid"][rows, :] = resid
        r["outer_low"][rows, :] = low(resid)

    by_blocks(block_len, resid_rows, high)
    keep("resid")

    def grad_cols(cols):
        r["grad"][:, cols] = low(nt(r["outer_low"][...], r["w_output"][cols, :]))
        r["output"][:, cols] = low(nn(r["attn_t"][...], r["outer_low"][:, cols]))

    by_blocks(width, grad_cols)
    keep("grad")
    keep("output")
    for pair in (pairs - 2, pairs - 1):
        probs_copy(pair, pair % 2).wait()
    for number, name in enumerate(START_KEPT):
        pltpu.make_async_copy(r[name], outs[name], r["keep_sem"].at[number]).wait()


def start(inputs, seq_count):
    block_len, width = inputs["tokens"].shape
    table_len = inputs["rel_table"].shape[0]
    inner_width = inputs["w_inner"].shape[1]
    ext_len = block_len + 2 * SPAN
    tiles = block_len // TILE
    heads = 2 * (width // PAIR)
    sizes = {
        "x": (ext_len, width), "q": (block_len, width), "k": (ext_len, width), "v": (ext_len, width),
        "relk": (table_len, width), "relq": (table_len + 2 * TILE, width), "to_table": (table_len, width),
        "from_table": (table_len, width), "hot": (table_len, 2 * table_len), "grad": (block_len, width),
        "resid": (block_len, width), "outer": (inner_width, width), "inner": (width, inner_width),
        "output": (width, width),
    }
    kinds = {name: jnp.float32 if name == "resid" else jnp.bfloat16 for name in START_KEPT}
    bf = lambda *shape: pltpu.VMEM(shape, jnp.bfloat16)
    f32 = lambda *shape: pltpu.VMEM(shape, jnp.float32)
    dma = pltpu.SemaphoreType.DMA
    any_spec = pl.BlockSpec(memory_space=pl.ANY)
    vmem = pl.BlockSpec(memory_space=pltpu.VMEM)
    smem = pl.BlockSpec(memory_space=pltpu.SMEM)
    values = pl.pallas_call(
        functools.partial(start_kernel, seq_count),
        in_specs=[any_spec] * len(START_HBM) + [vmem] * len(START_VMEM) + [smem],
        out_specs=[any_spec] * (len(START_KEPT) + 1) + [vmem] * 2,
        out_shape=[
            *(jax.ShapeDtypeStruct(sizes[name], kinds[name]) for name in START_KEPT),
            jax.ShapeDtypeStruct((heads, tiles, REACH, TILE), jnp.bfloat16),
            jax.ShapeDtypeStruct((block_len, width), jnp.bfloat16),
            jax.ShapeDtypeStruct((8, width), jnp.float32),
        ],
        scratch_shapes=[
            *(pltpu.VMEM(sizes[name], kinds[name]) for name in START_KEPT),
            *(pltpu.VMEM(inputs[name].shape, inputs[name].dtype) for name in START_HBM[1:]),
            f32(ext_len, block_len), bf(PAIR, ext_len), f32(2, REACH, TILE), bf(2, 2, tiles, REACH, TILE),
            bf(block_len, width), bf(width, block_len), f32(block_len, width), f32(block_len, width),
            f32(block_len, width), f32(block_len, TILE), bf(block_len, width),
            bf(block_len, inner_width), bf(block_len, inner_width), bf(block_len, inner_width),
            f32(block_len, width), bf(block_len, width),
            dma((len(START_HBM),)), dma((len(START_KEPT),)), dma((2,)), dma((2,)), dma((2,)),
        ],
        compiler_params=pltpu.CompilerParams(
            collective_id=1, has_side_effects=True, vmem_limit_bytes=60 * 2**20
        ),
        name="start",
    )(*(inputs[name] for name in START_IN))
    return dict(zip(START_OUT, values))


class Line:
    def __init__(self, side, row_step, seq_step):
        self.side = side
        row, place = lax.axis_index("rows"), lax.axis_index("seq")
        away = 1 - 2 * side
        self.device = {"rows": row + away * row_step, "seq": place + away * seq_step}


def lines_of():
    row, place = lax.axis_index("rows"), lax.axis_index("seq")
    first, second, third, fourth = (place // step % 2 for step in (1, 2, 4, 8))
    core = Line(row, 1, 0)
    near = Line(first + row * (second - first), 0, 1 + row)
    cross = Line(second + row * (first - second), 0, 2 - row)
    low_z, high_z = Line(third, 0, 4), Line(fourth, 0, 8)
    return (core, near, cross, low_z, high_z), (core, low_z, high_z, near, cross)


def add_rows(target, at, source, rows, out, out_at):
    step = next(s for s in (48, 32, PACK) if rows % s == 0)

    def body(i, carry):
        here = pl.multiple_of(i * step, PACK)
        mine = pl.ds(pl.multiple_of(at + here, PACK), step)
        goal = pl.ds(pl.multiple_of(out_at + here, PACK), step)
        out[goal, :] = target[mine, :] + source[pl.ds(here, step), :]
        return carry

    lax.fori_loop(0, rows // step, body, 0)


class Chunk:
    def __init__(self, index, which, start, half, base, width, z_first):
        self.index, self.which, self.start, self.half = index, which, start, half
        self.base, self.width, self.z_first = base, width, z_first

    def part(self, refs, side):
        if self.which == "inner":
            block, low_row = (self.start // 2) // self.width, (self.start // 2) % self.width
            col = (2 * block + side) * self.width
            return refs["inner"].at[pl.ds(low_row, self.half), pl.ds(pl.multiple_of(col, PAIR), self.width)]
        first = pl.multiple_of(self.start + side * self.half, PACK)
        return refs[self.which].at[pl.ds(first, self.half)]


def chunks_of(spec, unit, width):
    chunks, starts, base = [], {}, 0
    for which, units, z_first in spec:
        half = units * unit // 2
        start = starts.get(which, 0)
        chunks.append(Chunk(len(chunks), which, start, half, base, width, z_first))
        starts[which] = start + 2 * half
        base += half
    return chunks, base


class Sum:
    phases = 5
    last = 2 * phases

    def __init__(self, chunks, ins, outs, acc, recv, own_sem, send_sem, recv_sem):
        self.chunks, self.ins, self.outs = chunks, ins, outs
        self.acc, self.recv = acc, recv
        self.own_sem, self.send_sem, self.recv_sem = own_sem, send_sem, recv_sem
        self.row = lax.axis_index("rows")
        self.plane_first, self.z_first = lines_of()
        self.recv_at = [2 * chunk.base for chunk in chunks]

    def greet(self, more):
        barrier = pltpu.get_barrier_semaphore()
        devices = [line.device for line in self.plane_first] + more
        for device in devices:
            pl.semaphore_signal(barrier, inc=1, device_id=device, device_id_type=MESH)
        pl.semaphore_wait(barrier, len(devices))

    def lines(self, chunk):
        return self.z_first if chunk.z_first else self.plane_first

    def offset(self, chunk, phase):
        at, rows = chunk.base, chunk.half
        for line in self.lines(chunk)[1 : phase + 1]:
            rows //= 2
            at = at + line.side * rows
        return at

    def received(self, chunk, phase):
        at = self.recv_at[chunk.index] + sum(chunk.half >> p for p in range(phase))
        return self.recv.at[pl.ds(at, chunk.half >> phase)]

    def copies(self, chunk, stage):
        gather = stage >= self.phases
        phase = self.last - 1 - stage if gather else stage
        line, rows = self.lines(chunk)[phase], chunk.half >> phase
        local = None
        if gather:
            at = chunk.base + self.offset(chunk, phase)
            source = self.recv.at[pl.ds(pl.multiple_of(at, PACK), rows)]
            target = source
            if phase == 0:
                target = chunk.part(self.outs, self.row)
                local = (source, target)
        elif phase == 0:
            source, target = chunk.part(self.ins, 1 - self.row), self.received(chunk, 0)
            local = (chunk.part(self.ins, self.row), self.acc.at[pl.ds(chunk.base, rows)])
        else:
            at = self.offset(chunk, phase - 1) + (1 - line.side) * rows
            source = self.acc.at[pl.ds(pl.multiple_of(at, PACK), rows)]
            target = self.received(chunk, phase)
        sem = chunk.index * self.last + stage
        copies = [
            pltpu.make_async_remote_copy(
                src_ref=source, dst_ref=target, send_sem=self.send_sem.at[sem],
                recv_sem=self.recv_sem.at[sem], device_id=line.device, device_id_type=MESH,
            )
        ]
        if local is not None:
            copies.append(pltpu.make_async_copy(*local, self.own_sem.at[chunk.index]))
        return copies

    def step(self, c, stage):
        chunk = self.chunks[c]
        if stage > 0:
            for copy in self.copies(chunk, stage - 1):
                copy.wait()
        if 0 < stage <= self.phases:
            phase = stage - 1
            at, rows = self.offset(chunk, phase), chunk.half >> phase
            if stage == self.phases:
                add_rows(self.acc, at, self.received(chunk, phase), rows, self.recv, chunk.base + at)
            else:
                add_rows(self.acc, at, self.received(chunk, phase), rows, self.acc, at)
        if stage < self.last:
            for copy in self.copies(chunk, stage):
                copy.start()


class VectorSum:
    def __init__(self, lines, acc, recv, send_sem, recv_sem):
        self.lines, self.acc, self.recv, self.send_sem, self.recv_sem = lines, acc, recv, send_sem, recv_sem

    def copy(self, phase):
        return pltpu.make_async_remote_copy(
            src_ref=self.acc.at[phase], dst_ref=self.recv.at[phase], send_sem=self.send_sem.at[phase],
            recv_sem=self.recv_sem.at[phase], device_id=self.lines[phase].device, device_id_type=MESH,
        )

    def start(self, phase):
        self.copy(phase).start()

    def end(self, phase):
        self.copy(phase).wait()
        self.acc[phase + 1] = self.acc[phase] + self.recv[phase]


def back_of_pair(pair, buf, r):
    swap = unit(True)
    lanes_at = pl.multiple_of(pair * PAIR, PAIR)
    lanes_here = pl.ds(lanes_at, PAIR)
    row = lax.broadcasted_iota(jnp.int32, (TILE, TILE), 0)
    col = lax.broadcasted_iota(jnp.int32, (TILE, TILE), 1)
    parts = REACH // TILE
    block_len, ext_len = r["q"].shape[0], r["k"].shape[0]
    tiles = block_len // TILE
    qt_ref, kt_ref, dk_ref, dv_ref, drelk_ref, drelq_ref = (
        r[name] for name in ("qt", "kt", "dk_pair", "dv_pair", "drelk_t", "drelq_t")
    )
    for source, result in ((r["q"], qt_ref), (r["k"], kt_ref)):
        for at in range(0, source.shape[0], TILE):
            flipped = nn(swap, source[pl.ds(at, TILE), lanes_here])
            result[:, pl.ds(at, TILE)] = flipped.T.astype(jnp.bfloat16)
    dk_ref[...] = jnp.zeros_like(dk_ref)
    dv_ref[...] = jnp.zeros_like(dv_ref)
    drelk_ref[...] = jnp.zeros_like(drelk_ref)
    drelq_ref[...] = jnp.zeros_like(drelq_ref)
    for tile in range(tiles):
        first = tile * TILE
        q_tile = r["q"][pl.ds(first, TILE), lanes_here]
        grad_tile = r["grad"][pl.ds(first, TILE), lanes_here]
        v_tile = r["v"][pl.ds(first, REACH), lanes_here]
        q_heads = [head_lanes(q_tile, head) for head in range(2)]
        grad_heads = [head_lanes(grad_tile, head) for head in range(2)]
        dq_heads = []
        lefts = [[] for _ in range(parts)]
        for head in range(2):
            lanes = pl.ds(head * DH, DH)
            probs = r["probs"][buf, head, tile].astype(jnp.float32)
            weighted = probs * nt(v_tile, grad_heads[head])
            delta = jnp.sum(weighted, axis=0, keepdims=True)
            dscore = ((weighted - probs * delta) * score_scale).astype(jnp.bfloat16)
            turned = nt(swap, dscore)
            dband = pltpu.roll(turned, REACH - TILE + 1, 1, stride=1, stride_axis=0)
            dband = dband[:, : 2 * SPAN].astype(jnp.bfloat16)
            dq_heads.append(
                nn(turned.astype(jnp.bfloat16), r["k"][pl.ds(first, REACH), lanes_here])
                + nn(dband, r["relk"][:, lanes_here])
            )
            drelk_ref[lanes, :] += nn(qt_ref[lanes, pl.ds(first, TILE)], dband)
            for part in range(parts):
                flipped = nn(swap, dscore[part * TILE : (part + 1) * TILE, :])
                spun = pltpu.roll(flipped, 0, 1, stride=1, stride_axis=0)
                near = jnp.where(col >= row, spun, 0.0)
                dfrom = jnp.concatenate([near, spun - near], axis=1).astype(jnp.bfloat16)
                window = pl.ds((parts - 1 - part) * TILE, 2 * TILE)
                drelq_ref[lanes, window] += nn(kt_ref[lanes, pl.ds(first + part * TILE, TILE)], dfrom)
                lefts[part] += [flipped.astype(jnp.bfloat16), dfrom]
        dq_turned = jnp.where(col < DH, dq_heads[0], dq_heads[1]).astype(jnp.bfloat16)
        r["dq"][pl.ds(first, TILE), lanes_here] = nn(swap, dq_turned).astype(jnp.bfloat16)
        dv_ref[pl.ds(first, REACH), :] += nn(
            jnp.concatenate([r["probs"][buf, 0, tile], r["probs"][buf, 1, tile]], axis=1),
            jnp.concatenate(grad_heads, axis=0),
        )
        for part in range(parts):
            window = r["relq"][pl.ds((parts - 1 - part) * TILE, 2 * TILE), lanes_here]
            right = jnp.concatenate(
                [q_heads[0], head_lanes(window, 0), q_heads[1], head_lanes(window, 1)], axis=0
            )
            dk_ref[pl.ds(first + part * TILE, TILE), :] += nn(
                jnp.concatenate(lefts[part], axis=1), right
            )
    r["dv"][:, lanes_here] = dv_ref[...].astype(jnp.bfloat16)
    for at in range(0, ext_len, TILE):
        r["dk"][pl.ds(at, TILE), lanes_here] = nn(
            swap, dk_ref[pl.ds(at, TILE), :].astype(jnp.bfloat16)
        ).astype(jnp.bfloat16)
    r["dk"][pl.ds(ext_len, 2 * SPAN), lanes_here] = drelk_ref[...].T.astype(jnp.bfloat16)
    r["dq"][pl.ds(block_len, 2 * SPAN), lanes_here] = (
        drelq_ref[:, pl.ds(TILE, 2 * SPAN)].T.astype(jnp.bfloat16)
    )


SOONER = ("q", "k", "v", "grad", "relk", "relq")
LATER = ("x", "to_table", "from_table", "w_query", "w_key", "w_value", "hot", "resid")
FINISH_IN = SOONER + LATER + ("vectors", "outer", "inner", "output", "probs_in")
FINISH_OUT = ("outer", "inner", "rest", "vectors", "tokens_grad")
FINISH_SCRATCH = (
    "probs", "qt", "kt", "dk_pair", "dv_pair", "drelk_t", "drelq_t", "dq", "dk", "dv", "rest", "table",
    "xt_query", "xt_key",
    "halo", "halo_got", "own_grad", "acc", "recv", "vec_acc", "vec_recv", "own_sem", "send_sem", "recv_sem",
    "vec_send", "vec_got", "probs_sem", "halo_send", "halo_recv", "load_sem",
)


def finish_kernel(chunks, schedule, seq_count, *refs):
    r = dict(zip(FINISH_IN, refs))
    outs = dict(zip(FINISH_OUT, refs[len(FINISH_IN) :]))
    scratch = refs[len(FINISH_IN) + len(FINISH_OUT) :]
    r.update(zip(FINISH_SCRATCH, scratch))
    loads = {}
    for number, (name, held) in enumerate(zip(SOONER + LATER, scratch[len(FINISH_SCRATCH) :])):
        loads[name] = pltpu.make_async_copy(r[name], held, r["load_sem"].at[number])
        loads[name].start()
        r[name] = held
    block_len, width = r["q"].shape
    ext_len = r["k"].shape[0]
    pairs = width // PAIR
    total = Sum(chunks, r, outs, r["acc"], r["recv"], r["own_sem"], r["send_sem"], r["recv_sem"])
    row, place = lax.axis_index("rows"), lax.axis_index("seq")
    before = {"rows": row, "seq": lax.rem(place + seq_count - 1, seq_count)}
    after = {"rows": row, "seq": lax.rem(place + 1, seq_count)}
    total.greet([before, after])
    vec = VectorSum(total.plane_first, r["vec_acc"], r["vec_recv"], r["vec_send"], r["vec_got"])
    vec.acc[0] = r["vectors"][...]

    def probs_copy(pair, buf):
        return pltpu.make_async_copy(
            r["probs_in"].at[pl.ds(2 * pair, 2)], r["probs"].at[buf], r["probs_sem"].at[buf]
        )

    def between(pair):
        if 0 < pair <= total.phases:
            vec.end(pair - 1)
        if pair < total.phases:
            vec.start(pair)
        for c, stage in schedule[pair + 1]:
            total.step(c, stage)

    def one_pair(pair, carry):
        buf = lax.rem(pair, 2)

        @pl.when(pair + 1 < pairs)
        def _():
            probs_copy(pair + 1, 1 - buf).start()

        probs_copy(pair, buf).wait()
        back_of_pair(pair, buf, r)
        for at in range(pairs):
            pl.when(pair == at)(functools.partial(between, at))
        return carry

    def turn_tokens(rows):
        r["xt_key"][:, rows] = r["x"][rows, :].T

    def turn_tables(rows):
        r["xt_key"][:, pl.ds(pl.multiple_of(ext_len + rows.start, PAIR), rows.size)] = r["to_table"][rows, :].T
        r["xt_query"][:, pl.ds(pl.multiple_of(block_len + rows.start, PAIR), rows.size)] = (
            r["from_table"][rows, :].T
        )

    def turn():
        by_blocks(ext_len, turn_tokens)
        by_blocks(2 * SPAN, turn_tables)
        r["xt_query"][:, pl.ds(0, block_len)] = r["xt_key"][:, pl.ds(SPAN, block_len)]

    def query_cols(cols):
        r["rest"][pl.ds(0, width), cols] = nn(r["xt_query"][...], r["dq"][:, cols]).astype(jnp.bfloat16)

    def key_cols(cols):
        r["rest"][pl.ds(width, width), cols] = nn(r["xt_key"][...], r["dk"][:, cols]).astype(jnp.bfloat16)

    def value_cols(cols):
        r["rest"][pl.ds(2 * width, width), cols] = nn(
            r["xt_key"][:, pl.ds(0, ext_len)], r["dv"][:, cols]
        ).astype(jnp.bfloat16)

    def table_cols(cols):
        r["table"][pl.ds(0, 2 * SPAN), cols] = nt(
            r["dk"][pl.ds(ext_len, 2 * SPAN), :], r["w_key"][cols, :]
        ).astype(jnp.bfloat16)
        r["table"][pl.ds(2 * SPAN, 2 * SPAN), cols] = nt(
            r["dq"][pl.ds(block_len, 2 * SPAN), :], r["w_query"][cols, :]
        ).astype(jnp.bfloat16)

    def bucket_cols(cols):
        r["rest"][pl.ds(4 * width, 2 * SPAN), cols] = nn(r["hot"][...], r["table"][:, cols]).astype(
            jnp.bfloat16
        )

    def halo_cols(cols):
        for at in (0, ext_len - SPAN):
            rows = pl.ds(at, SPAN)
            grad = nt(r["dk"][rows, :], r["w_key"][cols, :]) + nt(r["dv"][rows, :], r["w_value"][cols, :])
            r["halo"][rows, cols] = grad.astype(jnp.bfloat16)

    def own_cols(cols):
        own, mid = pl.ds(0, block_len), pl.ds(SPAN, block_len)
        r["own_grad"][:, cols] = (
            r["resid"][:, cols]
            + nt(r["dq"][own, :], r["w_query"][cols, :])
            + nt(r["dk"][mid, :], r["w_key"][cols, :])
            + nt(r["dv"][mid, :], r["w_value"][cols, :])
        )

    output_copy = pltpu.make_async_copy(
        r["output"], r["rest"].at[pl.ds(3 * width, width)], r["own_sem"].at[len(chunks)]
    )
    halos = [
        pltpu.make_async_remote_copy(
            src_ref=r["halo"].at[pl.ds(at, SPAN)], dst_ref=r["halo_got"].at[number],
            send_sem=r["halo_send"].at[number], recv_sem=r["halo_recv"].at[number],
            device_id=device, device_id_type=MESH,
        )
        for number, (at, device) in enumerate(((0, before), (ext_len - SPAN, after)))
    ]

    probs_copy(0, 0).start()
    output_copy.start()
    for c, stage in schedule[0]:
        total.step(c, stage)
    for name in SOONER:
        loads[name].wait()
    lax.fori_loop(0, pairs, one_pair, 0)
    output_copy.wait()
    for name in LATER:
        loads[name].wait()
    turn()
    pieces = ((query_cols,), (key_cols,), (value_cols,), (table_cols, bucket_cols), (halo_cols,), (own_cols,))
    for piece, steps in zip(pieces, schedule[pairs + 1 :]):
        for body in piece:
            by_blocks(width, body)
        if piece[0] is halo_cols:
            for copy in halos:
                copy.start()
        for c, stage in steps:
            total.step(c, stage)
    for copy in halos:
        copy.wait()
    grad = r["own_grad"][...]
    for number in range(2):
        grad = grad + r["halo_got"][number].astype(jnp.float32)
    outs["tokens_grad"][...] = grad.astype(jnp.bfloat16)
    outs["vectors"][...] = vec.acc[total.phases]


CHUNKS = (
    ("outer", 2, False),
    ("outer", 2, False),
    ("outer", 2, True),
    ("inner", 3, False),
    ("inner", 3, False),
    ("rest", 2, False),
    ("rest", 2, True),
    ("rest", 2, False),
    ("rest", 1, False),
)
SCHEDULE = (
    ((4, 0), (2, 0), (1, 0),),
    ((0, 0), (4, 1), (2, 1), (3, 0),),
    ((1, 1),),
    ((4, 2), (0, 1), (3, 1), (2, 2),),
    ((4, 3),),
    ((1, 2), (4, 4),),
    ((3, 2), (2, 3), (4, 5), (1, 3),),
    (),
    ((5, 0), (4, 6), (0, 2),),
    ((2, 4), (5, 1), (6, 0), (1, 4), (3, 3), (0, 3), (4, 7),),
    ((7, 0), (6, 1), (5, 2), (7, 1), (0, 4),),
    ((8, 0), (1, 5), (6, 2), (8, 1), (1, 6), (7, 2), (2, 5), (3, 4), (5, 3), (8, 2), (0, 5), (6, 3), (1, 7), (3, 5), (0, 6), (2, 6), (7, 3), (8, 3), (4, 8), (5, 4), (7, 4), (6, 4), (8, 4), (0, 7), (3, 6), (5, 5), (1, 8), (8, 5), (6, 5), (7, 5), (3, 7), (2, 7),),
    ((7, 6), (6, 6), (8, 6), (0, 8), (5, 6), (1, 9), (6, 7), (8, 7), (7, 7), (2, 8), (5, 7), (3, 8), (6, 8), (4, 9), (8, 8), (5, 8), (1, 10), (3, 9), (0, 9), (7, 8), (2, 9), (8, 9), (5, 9), (6, 9), (0, 10), (7, 9), (5, 10), (2, 10), (8, 10), (4, 10), (6, 10), (3, 10), (7, 10),),
)

def finish(inputs, seq_count):
    unit_rows = PACK * 2 * seq_count
    width = inputs["q"].shape[1]
    block_len, ext_len = inputs["q"].shape[0], inputs["k"].shape[0]
    chunks, rows = chunks_of(CHUNKS, unit_rows, width)
    sems = len(chunks) * Sum.last
    rest_rows = 4 * width + 2 * SPAN
    bf = lambda *shape: pltpu.VMEM(shape, jnp.bfloat16)
    f32 = lambda *shape: pltpu.VMEM(shape, jnp.float32)
    dma = pltpu.SemaphoreType.DMA
    vec_shape = inputs["vectors"].shape
    any_spec = pl.BlockSpec(memory_space=pl.ANY)
    vmem = pl.BlockSpec(memory_space=pltpu.VMEM)
    tiles = block_len // TILE
    return pl.pallas_call(
        functools.partial(finish_kernel, chunks, SCHEDULE, seq_count),
        in_specs=[vmem if name == "vectors" else any_spec for name in FINISH_IN],
        out_specs=[any_spec] * 3 + [vmem] * 2,
        out_shape=[
            jax.ShapeDtypeStruct(inputs["outer"].shape, jnp.bfloat16),
            jax.ShapeDtypeStruct(inputs["inner"].shape, jnp.bfloat16),
            jax.ShapeDtypeStruct((rest_rows, width), jnp.bfloat16),
            jax.ShapeDtypeStruct(vec_shape, jnp.float32),
            jax.ShapeDtypeStruct((block_len, width), jnp.bfloat16),
        ],
        scratch_shapes=[
            bf(2, 2, tiles, REACH, TILE), bf(PAIR, block_len), bf(PAIR, ext_len),
            f32(ext_len, PAIR), f32(ext_len, PAIR), f32(PAIR, 2 * SPAN), f32(PAIR, 2 * SPAN + 2 * TILE),
            bf(block_len + 2 * SPAN, width), bf(ext_len + 2 * SPAN, width), bf(ext_len, width),
            bf(rest_rows, width), bf(4 * SPAN, width),
            bf(width, block_len + 2 * SPAN), bf(width, ext_len + 2 * SPAN), bf(ext_len, width), bf(2, SPAN, width), f32(block_len, width),
            bf(rows, width), bf(2 * rows, width),
            f32(Sum.phases + 1, *vec_shape), f32(Sum.phases, *vec_shape),
            dma((len(chunks) + 1,)), dma((sems,)), dma((sems,)), dma((Sum.phases,)), dma((Sum.phases,)),
            dma((2,)), dma((2,)), dma((2,)), dma((len(SOONER + LATER),)),
            *(pltpu.VMEM(inputs[name].shape, inputs[name].dtype) for name in SOONER + LATER),
        ],
        compiler_params=pltpu.CompilerParams(
            collective_id=0, has_side_effects=True, vmem_limit_bytes=60 * 2**20
        ),
        name="finish",
    )(*(inputs[name] for name in FINISH_IN))


def shifted(shard, axis, by):
    count = lax.axis_size(axis)
    pairs = [(i, i + by) for i in range(count) if 0 <= i + by < count]
    return lax.ppermute(shard, axis, pairs)


def f32dot(spec, left, right):
    return jnp.einsum(spec, left, right, preferred_element_type=jnp.float32)


def low(values):
    return values.astype(jnp.bfloat16)

def finish_plain(inputs):
    query, key_ext, value_ext = inputs["q"], inputs["k"], inputs["v"]
    block_len, width = query.shape
    w_query, w_key, w_value, hot = (inputs[name] for name in ("w_query", "w_key", "w_value", "hot"))
    dquery, dkey, dvalue, drelk, drelq = attend_back(
        query, key_ext, value_ext, inputs["grad"], inputs["probs_in"], inputs["relk"], inputs["relq"]
    )
    dkey = low(f32dot("ab,nbd->nad", unit(True), low(dkey).reshape(-1, TILE, width))).reshape(-1, width)
    dvalue = low(dvalue)
    drelk = low(drelk).T
    drelq = low(drelq[:, TILE : TILE + 2 * SPAN]).T
    query_part = f32dot("em,md->ed", jnp.concatenate([inputs["x"][SPAN : SPAN + block_len], inputs["from_table"]]).T, jnp.concatenate([dquery, drelq]))
    key_part = f32dot("em,md->ed", jnp.concatenate([inputs["x"], inputs["to_table"]]).T, jnp.concatenate([dkey, drelk]))
    value_part = f32dot("em,md->ed", inputs["x"].T, dvalue)
    table = jnp.concatenate(
        [low(f32dot("md,ed->me", drelk, w_key)), low(f32dot("md,ed->me", drelq, w_query))]
    )
    table_part = f32dot("rm,me->re", hot, table)
    rest = jnp.concatenate(
        [low(query_part), low(key_part), low(value_part), inputs["output"], low(table_part)]
    )
    ext_grad = f32dot("td,ed->te", dkey, w_key) + f32dot("td,ed->te", dvalue, w_value)
    tokens_grad = (
        inputs["resid"]
        + f32dot("td,ed->te", dquery, w_query)
        + ext_grad[SPAN : SPAN + block_len]
        + shifted(low(ext_grad[:SPAN]), "seq", -1).astype(jnp.float32)
        + shifted(low(ext_grad[SPAN + block_len :]), "seq", 1).astype(jnp.float32)
    )
    both = ("rows", "seq")
    sums = [
        lax.all_gather(
            lax.psum_scatter(part, both, scatter_dimension=0, tiled=True), both, axis=0, tiled=True
        )
        for part in (inputs["outer"], inputs["inner"], rest)
    ]
    return (*sums, lax.psum(inputs["vectors"], both), low(tokens_grad))


def finish_of(inputs):
    seq_count, rows_count = lax.axis_size("seq"), lax.axis_size("rows")
    if rows_count == 2 and seq_count == 16:
        return finish(inputs, seq_count)
    return finish_plain(inputs)

def shards(
    tokens, cotangent, w_query, w_key, w_value, w_output, w_inner, w_outer, rel_table,
    mid_gain, mid_bias, end_gain, end_bias, seq_lengths, pad_mask, rel_buckets,
):
    width = tokens.shape[-1]
    inputs = {
        "tokens": tokens[0], "cotangent": cotangent[0], "rel_table": rel_table, "w_query": w_query,
        "w_key": w_key, "w_value": w_value, "w_output": w_output, "w_inner": w_inner, "w_outer": w_outer,
        "rel_buckets": rel_buckets, "mid_gain": mid_gain, "mid_bias": mid_bias, "end_gain": end_gain,
        "end_bias": end_bias, "keep": pad_mask.reshape(-1, TILE), "lengths": seq_lengths,
    }
    kept = start(inputs, lax.axis_size("seq"))
    layer_out = kept.pop("layer_out")
    inputs.update(kept, probs_in=kept["probs_out"])
    outer_w, inner_w, rest_w, norm_parts, tokens_grad = finish_of(inputs)
    query_w, key_w, value_w, output_w = (rest_w[at * width : (at + 1) * width] for at in range(4))
    table_w = rest_w[4 * width :]
    return (
        layer_out[None], tokens_grad[None],
        *(w.astype(jnp.float32) for w in (query_w, key_w, value_w, output_w, inner_w, outer_w, table_w)),
        *(norm_parts[at] for at in range(4)),
    )


def solution(mesh):
    split = P("rows", "seq", None)
    return jax.shard_map(
        shards,
        mesh=mesh,
        in_specs=(split, split) + (P(),) * 11 + (P("rows", None), P("rows", None), P()),
        out_specs=(split, split) + (P(),) * 11,
        check_vma=False,
    )
```

time: 304 us -> 248 us (0.82)
  matrix products: 43.7 us -> 0 us
  Pallas kernels: 212 us -> 225 us
  other arithmetic: 30.6 us -> 18.4 us
  starting transfers between devices: 7.17 us -> 0 us
  local copies, waits for them, and re-layouts: 9.24 us -> 3.09 us
    dot_general x16 -> x0, matrix products: 43.7 us -> none  [f32dot(): return jnp.einsum(spec, left, right, preferred_element_type=jnp.float32)]
    pallas_call x2, Pallas kernels: 212 us -> 225 us  [the longest x1 155 us: finish(): pl.pallas_call(functools.partial(finish_kernel, chunks, SCHEDULE, seq_cou...]
    ppermute x2 -> x0, starting transfers between devices: 7.17 us -> none  [shifted(): return lax.ppermute(shard, axis, pairs)]
    concatenate x3 -> x0, other arithmetic: 4.69 us -> none  [the longest x1 2.36 us: shards(): jnp.concatenate([tokens.T, from_table_t], axis=1)]
  transfers between devices with their start and end apart: 2 -> 0, of which waited for: 0 -> 0; matrix products, arithmetic and copies ran while one was open for 7% -> 0% of each run, Pallas kernels for 0% -> 0%
where the time goes in v4:
time: 248 us; the launch traced here: 247 us
  Pallas kernels  225 us (91%)
  other arithmetic  18.4 us (7%)
  local copies, waits for them, and re-layouts  3.09 us (1%)
    pallas_call x1, Pallas kernels, finish(): pl.pallas_call(functools.partial(finish_kernel, chunks, SCHEDULE, seq_cou...  155 us
    pallas_call x1, Pallas kernels, start(): pl.pallas_call(functools.partial(start_kernel, seq_count), in_specs=[any_...  70.3 us
    convert_element_type x4, other arithmetic, shards(): w.astype(jnp.float32)  18.4 us

profile of v4, /device:TPU:0, one launch (start us, length us, event | category | flops | bytes accessed | tf_op | source)
XLA Modules:
  0.0 247.2 jit_solution(6738403571359834047)
XLA Ops:
  0.6 70.3 %start.1 = (bf16[768,768]{1,0:T(8,128)(2,1)}, bf16[256,768]{1,0:T(8,128)(2,1)}, bf16[768,768]{1,0:T(8,128)(2,1)}, bf16[768,768]{1,0:T(8,128)(2,1)}, bf16[512,768...) custom-call(bf16[256,768]{1,0:T(8,128)(2,1)} %bitcast.11, ...), custom_call_target="tpu_custom_call" | custom-call | tf_op jit(solution)/shard_map/start/pallas_call | solution.py:497
  70.9 154.7 %finish.1 = (bf16[3072,768]{1,0:T(8,128)(2,1)}, bf16[768,3072]{1,0:T(8,128)(2,1)}, bf16[3584,768]{1,0:T(8,128)(2,1)}, f32[8,768]{1,0:T(8,128)}, bf16[256,768]{1,0:T(8,128)(2,1)}) custom-call(bf16[256,768]{1,0:T(8,128)(2,1)} %get-tuple-element.36.refs_0_, bf16[768,768]{1,0:T(8,128)(2,1)} %get-tuple-element.37.refs_1_, ...), custom_call_target="tpu_custom_call" | custom-call | tf_op jit(solution)/shard_map/finish/pallas_call | solution.py:949
  225.7 1.6 slice_reduce_fusion
  227.3 0.0 slice-start.2
  227.3 2.5 %slice_convert_fusion.4 = f32[512,768]{1,0:T(8,128)} fusion(bf16[3584,768]{1,0:T(8,128)(2,1)} %get-tuple-element.53), kind=kLoop, calls=%fused_computation.4 | loop fusion | flops 393216 | bytes 2359296 | tf_op jit(solution)/shard_map/convert_element_type | solution.py:1056
  229.8 0.0 slice-start.3
  229.8 0.0 slice-start
  229.8 6.3 %slice_convert_fusion = (f32[768,768]{1,0:T(8,128)}, f32[768,768]{1,0:T(8,128)}, f32[768,768]{1,0:T(8,128)}, f32[768,768]{1,0:T(8,128)}) fusion(bf16[3584,768]{1,0:T(8,128)(2,1)} %get-tuple-element.53), kind=kLoop, calls=%fused_computation | loop fusion | flops 2359296 | bytes 14155776 | tf_op jit(solution)/shard_map/convert_element_type | solution.py:1056
  236.1 0.0 slice-start.1
  236.1 0.0 slice-done.2
  236.1 0.0 slice-done.3
  236.1 5.0 %convert_element_type.25 = f32[768,3072]{1,0:T(8,128)} convert(bf16[768,3072]{1,0:T(8,128)(2,1)S(1)} %bitcast.8) | non-fusion elementwise | flops 2359296 | bytes 14155776 | tf_op jit(solution)/shard_map/convert_element_type | solution.py:1056
  241.2 0.0 slice-done
  241.2 0.0 slice-done.1
  241.2 0.0 copy-start
  241.2 0.0 copy-start.1
  241.2 4.5 %convert_element_type.26 = f32[3072,768]{1,0:T(8,128)} convert(bf16[3072,768]{1,0:T(8,128)(2,1)S(1)} %bitcast.6) | non-fusion elementwise | flops 2359296 | bytes 14155776 | tf_op jit(solution)/shard_map/convert_element_type | solution.py:1056
  245.7 0.0 copy-done
  245.7 0.7 copy.31
  246.4 0.0 copy-done.1
  246.4 0.7 copy.32
  (2 shorter events, 0.0 us)
Async XLA Ops:
  227.3 8.9 %slice-start.2 = ((s8[4718592]{0:T(1024)(128)(4,1)}), s8[4194304]{0:T(1024)(128)(4,1)S(1)}, s32[]{:S(2)}) async-start(s8[4718592]{0:T(1024)(128)(4,1)} %bitcast.7), calls=%async_computation.2 | async-start | bytes 8388608
  229.8 6.3 %slice-start.3 = ((s8[4718592]{0:T(1024)(128)(4,1)}), s8[524288]{0:T(1024)(128)(4,1)S(1)}, s32[]{:S(2)}) async-start(s8[4718592]{0:T(1024)(128)(4,1)} %bitcast.7), calls=%async_computation.3 | async-start | bytes 1048576
  229.8 11.4 %slice-start = ((s8[4718592]{0:T(1024)(128)(4,1)}), s8[4194304]{0:T(1024)(128)(4,1)S(1)}, s32[]{:S(2)}) async-start(s8[4718592]{0:T(1024)(128)(4,1)} %bitcast.5), calls=%async_computation | async-start | bytes 8388608
  236.1 5.1 %slice-start.1 = ((s8[4718592]{0:T(1024)(128)(4,1)}), s8[524288]{0:T(1024)(128)(4,1)S(1)}, s32[]{:S(2)}) async-start(s8[4718592]{0:T(1024)(128)(4,1)} %bitcast.5), calls=%async_computation.1 | async-start | bytes 1048576
  241.2 4.5 %copy-start = (bf16[256,768]{1,0:T(8,128)(2,1)S(1)}, bf16[256,768]{1,0:T(8,128)(2,1)}, u32[]{:S(2)}) copy-start(bf16[256,768]{1,0:T(8,128)(2,1)} %get-tuple-element.35) | copy-start | bytes 1179652
  241.2 5.2 %copy-start.1 = (bf16[256,768]{1,0:T(8,128)(2,1)S(1)}, bf16[256,768]{1,0:T(8,128)(2,1)}, u32[]{:S(2)}) copy-start(bf16[256,768]{1,0:T(8,128)(2,1)} %get-tuple-element.52) | copy-start | bytes 1179652

commit v5 on v4

--- a/solution.py
+++ b/solution.py
@@ -247,13 +247,12 @@
 START_IN = START_HBM + START_VMEM + ("lengths",)
 START_KEPT = (
     "x", "q", "k", "v", "relk", "relq", "to_table", "from_table", "hot", "grad", "resid",
-    "outer", "inner", "output",
+    "active", "inner_low", "outer_low", "hidden_low", "mixed_low", "attn_t",
 )
 START_OUT = START_KEPT + ("probs_out", "layer_out", "vectors")
 START_SCRATCH = START_KEPT + (
     "rel_table", "w_query", "w_key", "w_value", "w_output", "w_inner", "w_outer", "cotangent",
-    "bias", "vt", "scores", "probs", "attn", "attn_t", "mixed", "hidden", "z_mid", "root_mid", "hidden_low",
-    "active", "slope", "inner_low", "sum_grad", "outer_low",
+    "bias", "vt", "scores", "probs", "attn", "mixed", "hidden", "z_mid", "root_mid", "slope", "sum_grad",
     "load_sem", "keep_sem", "probs_sem", "send_sem", "recv_sem",
 )
 
@@ -368,6 +367,7 @@
 
     lax.fori_loop(0, pairs, one_pair, 0)
 
+    keep("attn_t")
     for name in ("w_output", "w_inner", "w_outer", "cotangent"):
         loads[name].wait()
 
@@ -393,6 +393,7 @@
         r["hidden_low"][rows, :] = low(hidden)
 
     by_blocks(block_len, mid_rows, high)
+    keep("hidden_low")
 
     def active_cols(cols):
         active, slope = gelu_both(nn(r["hidden_low"][...], r["w_inner"][:, cols]))
@@ -400,6 +401,7 @@
         r["slope"][:, cols] = low(slope)
 
     by_blocks(inner_width, active_cols)
+    keep("active")
 
     def outer_cols(cols):
         r["mixed"][:, cols] = nn(r["active"][...], r["w_outer"][:, cols])
@@ -422,30 +424,19 @@
         r["outer_low"][rows, :] = low(sum_grad)
 
     by_blocks(block_len, end_rows, high)
+    keep("outer_low")
 
     def inner_cols(cols):
         grad = nt(r["outer_low"][...], r["w_outer"][cols, :])
         r["inner_low"][:, cols] = low(grad * r["slope"][:, cols].astype(jnp.float32))
 
     by_blocks(inner_width, inner_cols)
-
-    def outer_part(rows):
-        r["outer"][rows, :] = low(nn(r["active"][:, rows].T, r["outer_low"][...]))
-
-    by_blocks(inner_width, outer_part)
-    keep("outer")
+    keep("inner_low")
 
     def hidden_cols(cols):
         r["mixed"][:, cols] = r["sum_grad"][:, cols] + nt(r["inner_low"][...], r["w_inner"][cols, :])
 
     by_blocks(width, hidden_cols)
-    hidden_t = r["hidden_low"][...].T
-
-    def inner_part(cols):
-        r["inner"][:, cols] = low(nn(hidden_t, r["inner_low"][:, cols]))
-
-    by_blocks(inner_width, inner_part)
-    keep("inner")
 
     def resid_rows(rows):
         hidden_grad, z = r["mixed"][rows, :], r["z_mid"][rows, :]
@@ -455,18 +446,17 @@
         root = r["root_mid"][rows, pl.ds(0, 1)]
         resid = root * (grad - mean_of(grad) - z * mean_of(grad * z))
         r["resid"][rows, :] = resid
-        r["outer_low"][rows, :] = low(resid)
+        r["mixed_low"][rows, :] = low(resid)
 
     by_blocks(block_len, resid_rows, high)
     keep("resid")
+    keep("mixed_low")
 
     def grad_cols(cols):
-        r["grad"][:, cols] = low(nt(r["outer_low"][...], r["w_output"][cols, :]))
-        r["output"][:, cols] = low(nn(r["attn_t"][...], r["outer_low"][:, cols]))
+        r["grad"][:, cols] = low(nt(r["mixed_low"][...], r["w_output"][cols, :]))
 
     by_blocks(width, grad_cols)
     keep("grad")
-    keep("output")
     for pair in (pairs - 2, pairs - 1):
         probs_copy(pair, pair % 2).wait()
     for number, name in enumerate(START_KEPT):
@@ -484,8 +474,9 @@
         "x": (ext_len, width), "q": (block_len, width), "k": (ext_len, width), "v": (ext_len, width),
         "relk": (table_len, width), "relq": (table_len + 2 * TILE, width), "to_table": (table_len, width),
         "from_table": (table_len, width), "hot": (table_len, 2 * table_len), "grad": (block_len, width),
-        "resid": (block_len, width), "outer": (inner_width, width), "inner": (width, inner_width),
-        "output": (width, width),
+        "resid": (block_len, width), "active": (block_len, inner_width),
+        "inner_low": (block_len, inner_width), "outer_low": (block_len, width),
+        "hidden_low": (block_len, width), "mixed_low": (block_len, width), "attn_t": (width, block_len),
     }
     kinds = {name: jnp.float32 if name == "resid" else jnp.bfloat16 for name in START_KEPT}
     bf = lambda *shape: pltpu.VMEM(shape, jnp.bfloat16)
@@ -508,10 +499,8 @@
             *(pltpu.VMEM(sizes[name], kinds[name]) for name in START_KEPT),
             *(pltpu.VMEM(inputs[name].shape, inputs[name].dtype) for name in START_HBM[1:]),
             f32(ext_len, block_len), bf(PAIR, ext_len), f32(2, REACH, TILE), bf(2, 2, tiles, REACH, TILE),
-            bf(block_len, width), bf(width, block_len), f32(block_len, width), f32(block_len, width),
-            f32(block_len, width), f32(block_len, TILE), bf(block_len, width),
-            bf(block_len, inner_width), bf(block_len, inner_width), bf(block_len, inner_width),
-            f32(block_len, width), bf(block_len, width),
+            bf(block_len, width), f32(block_len, width), f32(block_len, width), f32(block_len, width),
+            f32(block_len, TILE), bf(block_len, inner_width), f32(block_len, width),
             dma((len(START_HBM),)), dma((len(START_KEPT),)), dma((2,)), dma((2,)), dma((2,)),
         ],
         compiler_params=pltpu.CompilerParams(
@@ -540,14 +529,13 @@
     return (core, near, cross, low_z, high_z), (core, low_z, high_z, near, cross)
 
 
-def add_rows(target, at, source, rows, out, out_at):
+def add_rows(left, right, out):
+    rows = out.shape[0]
     step = next(s for s in (48, 32, PACK) if rows % s == 0)
 
     def body(i, carry):
-        here = pl.multiple_of(i * step, PACK)
-        mine = pl.ds(pl.multiple_of(at + here, PACK), step)
-        goal = pl.ds(pl.multiple_of(out_at + here, PACK), step)
-        out[goal, :] = target[mine, :] + source[pl.ds(here, step), :]
+        here = pl.ds(pl.multiple_of(i * step, PACK), step)
+        out[here, :] = left[here, :] + right[here, :]
         return carry
 
     lax.fori_loop(0, rows // step, body, 0)
@@ -558,11 +546,10 @@
         self.index, self.which, self.start, self.half = index, which, start, half
         self.base, self.width, self.z_first = base, width, z_first
 
-    def part(self, refs, side):
+    def out(self, refs, side):
         if self.which == "inner":
-            block, low_row = (self.start // 2) // self.width, (self.start // 2) % self.width
-            col = (2 * block + side) * self.width
-            return refs["inner"].at[pl.ds(low_row, self.half), pl.ds(pl.multiple_of(col, PAIR), self.width)]
+            col = (self.start // self.width + side) * self.width
+            return refs["inner"].at[:, pl.ds(pl.multiple_of(col, PAIR), self.width)]
         first = pl.multiple_of(self.start + side * self.half, PACK)
         return refs[self.which].at[pl.ds(first, self.half)]
 
@@ -570,11 +557,10 @@
 def chunks_of(spec, unit, width):
     chunks, starts, base = [], {}, 0
     for which, units, z_first in spec:
-        half = units * unit // 2
         start = starts.get(which, 0)
-        chunks.append(Chunk(len(chunks), which, start, half, base, width, z_first))
-        starts[which] = start + 2 * half
-        base += half
+        chunks.append(Chunk(len(chunks), which, start, units * unit // 2, base, width, z_first))
+        starts[which] = start + units * unit
+        base += units * unit
     return chunks, base
 
 
@@ -582,13 +568,11 @@
     phases = 5
     last = 2 * phases
 
-    def __init__(self, chunks, ins, outs, acc, recv, own_sem, send_sem, recv_sem):
-        self.chunks, self.ins, self.outs = chunks, ins, outs
-        self.acc, self.recv = acc, recv
+    def __init__(self, chunks, outs, work, recv, own_sem, send_sem, recv_sem):
+        self.chunks, self.outs, self.work, self.recv = chunks, outs, work, recv
         self.own_sem, self.send_sem, self.recv_sem = own_sem, send_sem, recv_sem
         self.row = lax.axis_index("rows")
         self.plane_first, self.z_first = lines_of()
-        self.recv_at = [2 * chunk.base for chunk in chunks]
 
     def greet(self, more):
         barrier = pltpu.get_barrier_semaphore()
@@ -601,14 +585,21 @@
         return self.z_first if chunk.z_first else self.plane_first
 
     def offset(self, chunk, phase):
-        at, rows = chunk.base, chunk.half
+        at, rows = 0, chunk.half
         for line in self.lines(chunk)[1 : phase + 1]:
             rows //= 2
             at = at + line.side * rows
         return at
 
+    def working(self, chunk, at, rows):
+        return self.work.at[pl.ds(pl.multiple_of(chunk.base + self.row * chunk.half + at, PACK), rows)]
+
     def received(self, chunk, phase):
-        at = self.recv_at[chunk.index] + sum(chunk.half >> p for p in range(phase))
+        at = chunk.base + sum(chunk.half >> p for p in range(phase))
+        return self.recv.at[pl.ds(at, chunk.half >> phase)]
+
+    def summed(self, chunk, phase):
+        at = pl.multiple_of(chunk.base + self.offset(chunk, phase), PACK)
         return self.recv.at[pl.ds(at, chunk.half >> phase)]
 
     def copies(self, chunk, stage):
@@ -617,19 +608,17 @@
         line, rows = self.lines(chunk)[phase], chunk.half >> phase
         local = None
         if gather:
-            at = chunk.base + self.offset(chunk, phase)
-            source = self.recv.at[pl.ds(pl.multiple_of(at, PACK), rows)]
-            target = source
+            source = target = self.summed(chunk, phase)
             if phase == 0:
-                target = chunk.part(self.outs, self.row)
+                target = chunk.out(self.outs, self.row)
                 local = (source, target)
-        elif phase == 0:
-            source, target = chunk.part(self.ins, 1 - self.row), self.received(chunk, 0)
-            local = (chunk.part(self.ins, self.row), self.acc.at[pl.ds(chunk.base, rows)])
         else:
-            at = self.offset(chunk, phase - 1) + (1 - line.side) * rows
-            source = self.acc.at[pl.ds(pl.multiple_of(at, PACK), rows)]
             target = self.received(chunk, phase)
+            if phase == 0:
+                other = chunk.base + (1 - self.row) * chunk.half
+                source = self.work.at[pl.ds(pl.multiple_of(other, PACK), rows)]
+            else:
+                source = self.working(chunk, self.offset(chunk, phase - 1) + (1 - line.side) * rows, rows)
         sem = chunk.index * self.last + stage
         copies = [
             pltpu.make_async_remote_copy(
@@ -648,11 +637,8 @@
                 copy.wait()
         if 0 < stage <= self.phases:
             phase = stage - 1
-            at, rows = self.offset(chunk, phase), chunk.half >> phase
-            if stage == self.phases:
-                add_rows(self.acc, at, self.received(chunk, phase), rows, self.recv, chunk.base + at)
-            else:
-                add_rows(self.acc, at, self.received(chunk, phase), rows, self.acc, at)
+            mine = self.working(chunk, self.offset(chunk, phase), chunk.half >> phase)
+            add_rows(mine, self.received(chunk, phase), self.summed(chunk, phase) if stage == self.phases else mine)
         if stage < self.last:
             for copy in self.copies(chunk, stage):
                 copy.start()
@@ -752,50 +738,102 @@
     )
 
 
+SOONEST = ("outer_low", "hidden_low", "mixed_low", "attn_t")
 SOONER = ("q", "k", "v", "grad", "relk", "relq")
 LATER = ("x", "to_table", "from_table", "w_query", "w_key", "w_value", "hot", "resid")
-FINISH_IN = SOONER + LATER + ("vectors", "outer", "inner", "output", "probs_in")
+FINISH_IN = ("active", "inner_low") + SOONEST + SOONER + LATER + ("vectors", "probs_out")
 FINISH_OUT = ("outer", "inner", "rest", "vectors", "tokens_grad")
 FINISH_SCRATCH = (
-    "probs", "qt", "kt", "dk_pair", "dv_pair", "drelk_t", "drelq_t", "dq", "dk", "dv", "rest", "table",
-    "xt_query", "xt_key",
-    "halo", "halo_got", "own_grad", "acc", "recv", "vec_acc", "vec_recv", "own_sem", "send_sem", "recv_sem",
-    "vec_send", "vec_got", "probs_sem", "halo_send", "halo_recv", "load_sem",
+    "probs", "qt", "kt", "dk_pair", "dv_pair", "drelk_t", "drelq_t", "wide", "dv", "work", "table",
+    "xt_query", "xt_key", "hidden_t", "halo", "halo_got", "own_grad", "recv", "vec_acc", "vec_recv", "own_sem",
+    "send_sem", "recv_sem", "vec_send", "vec_got", "probs_sem", "halo_send", "halo_recv", "load_sem", "wide_sem",
 )
 
 
 def finish_kernel(chunks, schedule, seq_count, *refs):
-    r = dict(zip(FINISH_IN, refs))
+    given = dict(zip(FINISH_IN, refs))
     outs = dict(zip(FINISH_OUT, refs[len(FINISH_IN) :]))
     scratch = refs[len(FINISH_IN) + len(FINISH_OUT) :]
-    r.update(zip(FINISH_SCRATCH, scratch))
+    r = dict(zip(FINISH_SCRATCH, scratch))
+    block_len, width = given["q"].shape
+    ext_len = given["k"].shape[0]
+    folds = given["active"].shape[1] // width
+    wide_loads = {}
+    for number, name in enumerate(("active", "inner_low")):
+        wide_loads[name] = [
+            pltpu.make_async_copy(
+                given[name].at[:, pl.ds(fold * width, width)],
+                r["wide"].at[pl.ds((number * folds + fold) * block_len, block_len)],
+                r["wide_sem"].at[number * folds + fold],
+            )
+            for fold in range(folds)
+        ]
+    r["dk"] = r["wide"].at[pl.ds(0, ext_len + 2 * SPAN)]
+    r["dq"] = r["wide"].at[pl.ds(ext_len + 2 * SPAN, block_len + 2 * SPAN)]
     loads = {}
-    for number, (name, held) in enumerate(zip(SOONER + LATER, scratch[len(FINISH_SCRATCH) :])):
-        loads[name] = pltpu.make_async_copy(r[name], held, r["load_sem"].at[number])
+    for number, (name, held) in enumerate(
+        zip(SOONEST + SOONER + LATER, scratch[len(FINISH_SCRATCH) :])
+    ):
+        loads[name] = pltpu.make_async_copy(given[name], held, r["load_sem"].at[number])
+        r[name] = held
+    loads["outer_low"].start()
+    for copy in wide_loads["active"] + wide_loads["inner_low"]:
+        copy.start()
+    for name in SOONEST[1:] + SOONER + LATER:
         loads[name].start()
-        r[name] = held
-    block_len, width = r["q"].shape
-    ext_len = r["k"].shape[0]
     pairs = width // PAIR
-    total = Sum(chunks, r, outs, r["acc"], r["recv"], r["own_sem"], r["send_sem"], r["recv_sem"])
+    total = Sum(chunks, outs, r["work"], r["recv"], r["own_sem"], r["send_sem"], r["recv_sem"])
     row, place = lax.axis_index("rows"), lax.axis_index("seq")
     before = {"rows": row, "seq": lax.rem(place + seq_count - 1, seq_count)}
     after = {"rows": row, "seq": lax.rem(place + 1, seq_count)}
     total.greet([before, after])
     vec = VectorSum(total.plane_first, r["vec_acc"], r["vec_recv"], r["vec_send"], r["vec_got"])
-    vec.acc[0] = r["vectors"][...]
+    vec.acc[0] = given["vectors"][...]
 
     def probs_copy(pair, buf):
         return pltpu.make_async_copy(
-            r["probs_in"].at[pl.ds(2 * pair, 2)], r["probs"].at[buf], r["probs_sem"].at[buf]
+            given["probs_out"].at[pl.ds(2 * pair, 2)], r["probs"].at[buf], r["probs_sem"].at[buf]
         )
+
+    probs_copy(0, 0).start()
+    inner_base = folds * width
+    rest_base = 2 * folds * width
+
+    def outer_piece(chunk):
+        def body(i, carry):
+            at = pl.multiple_of(chunk.start + i * 256, 256)
+            fold, col = at // width, pl.multiple_of(at % width, 256)
+            active = r["wide"][pl.ds(pl.multiple_of(fold * block_len, block_len), block_len), pl.ds(col, 256)]
+            r["work"][pl.ds(at, 256), :] = nn(active.T, r["outer_low"][...]).astype(jnp.bfloat16)
+            return carry
+
+        lax.fori_loop(0, 2 * chunk.half // 256, body, 0)
+
+    def inner_piece(chunk):
+        for fold in range(chunk.start // width, (chunk.start + 2 * chunk.half) // width):
+
+            def inner_cols(cols, fold=fold):
+                inner_low = r["wide"][pl.ds((folds + fold) * block_len, block_len), cols]
+                r["work"][pl.ds(inner_base + fold * width, width), cols] = nn(
+                    r["hidden_t"][...], inner_low
+                ).astype(jnp.bfloat16)
+
+            by_blocks(width, inner_cols)
+
+    def output_piece():
+        def output_cols(cols):
+            r["work"][pl.ds(rest_base, width), cols] = nn(r["attn_t"][...], r["mixed_low"][:, cols]).astype(
+                jnp.bfloat16
+            )
+
+        by_blocks(width, output_cols)
 
     def between(pair):
         if 0 < pair <= total.phases:
             vec.end(pair - 1)
         if pair < total.phases:
             vec.start(pair)
-        for c, stage in schedule[pair + 1]:
+        for c, stage in later[pair]:
             total.step(c, stage)
 
     def one_pair(pair, carry):
@@ -826,13 +864,15 @@
         r["xt_query"][:, pl.ds(0, block_len)] = r["xt_key"][:, pl.ds(SPAN, block_len)]
 
     def query_cols(cols):
-        r["rest"][pl.ds(0, width), cols] = nn(r["xt_query"][...], r["dq"][:, cols]).astype(jnp.bfloat16)
+        r["work"][pl.ds(rest_base + width, width), cols] = nn(r["xt_query"][...], r["dq"][:, cols]).astype(jnp.bfloat16)
 
     def key_cols(cols):
-        r["rest"][pl.ds(width, width), cols] = nn(r["xt_key"][...], r["dk"][:, cols]).astype(jnp.bfloat16)
+        r["work"][pl.ds(rest_base + 2 * width, width), cols] = nn(
+            r["xt_key"][...], r["dk"][:, cols]
+        ).astype(jnp.bfloat16)
 
     def value_cols(cols):
-        r["rest"][pl.ds(2 * width, width), cols] = nn(
+        r["work"][pl.ds(rest_base + 3 * width, width), cols] = nn(
             r["xt_key"][:, pl.ds(0, ext_len)], r["dv"][:, cols]
         ).astype(jnp.bfloat16)
 
@@ -845,9 +885,9 @@
         ).astype(jnp.bfloat16)
 
     def bucket_cols(cols):
-        r["rest"][pl.ds(4 * width, 2 * SPAN), cols] = nn(r["hot"][...], r["table"][:, cols]).astype(
-            jnp.bfloat16
-        )
+        r["work"][pl.ds(rest_base + 4 * width, 2 * SPAN), cols] = nn(
+            r["hot"][...], r["table"][:, cols]
+        ).astype(jnp.bfloat16)
 
     def halo_cols(cols):
         for at in (0, ext_len - SPAN):
@@ -864,9 +904,6 @@
             + nt(r["dv"][mid, :], r["w_value"][cols, :])
         )
 
-    output_copy = pltpu.make_async_copy(
-        r["output"], r["rest"].at[pl.ds(3 * width, width)], r["own_sem"].at[len(chunks)]
-    )
     halos = [
         pltpu.make_async_remote_copy(
             src_ref=r["halo"].at[pl.ds(at, SPAN)], dst_ref=r["halo_got"].at[number],
@@ -876,26 +913,45 @@
         for number, (at, device) in enumerate(((0, before), (ext_len - SPAN, after)))
     ]
 
-    probs_copy(0, 0).start()
-    output_copy.start()
-    for c, stage in schedule[0]:
-        total.step(c, stage)
+    early = [chunk for chunk in chunks if chunk.which != "rest"]
+    later = schedule[len(early) + 2 :]
+
+    def advance(steps):
+        for c, stage in steps:
+            total.step(c, stage)
+
+    advance(schedule[0])
+    for name in ("outer_low", "hidden_low"):
+        loads[name].wait()
+    for copy in wide_loads["active"]:
+        copy.wait()
+    r["hidden_t"][...] = r["hidden_low"][...].T
+    fresh = True
+    for number, chunk in enumerate(early):
+        if chunk.which == "inner" and fresh:
+            for copy in wide_loads["inner_low"]:
+                copy.wait()
+            fresh = False
+        (inner_piece if chunk.which == "inner" else outer_piece)(chunk)
+        advance(schedule[number + 1])
+    for name in ("mixed_low", "attn_t"):
+        loads[name].wait()
+    output_piece()
+    advance(schedule[len(early) + 1])
     for name in SOONER:
         loads[name].wait()
     lax.fori_loop(0, pairs, one_pair, 0)
-    output_copy.wait()
     for name in LATER:
         loads[name].wait()
     turn()
     pieces = ((query_cols,), (key_cols,), (value_cols,), (table_cols, bucket_cols), (halo_cols,), (own_cols,))
-    for piece, steps in zip(pieces, schedule[pairs + 1 :]):
+    for piece, steps in zip(pieces, later[pairs:]):
         for body in piece:
             by_blocks(width, body)
         if piece[0] is halo_cols:
             for copy in halos:
                 copy.start()
-        for c, stage in steps:
-            total.step(c, stage)
+        advance(steps)
     for copy in halos:
         copy.wait()
     grad = r["own_grad"][...]
@@ -911,34 +967,42 @@
     ("outer", 2, True),
     ("inner", 3, False),
     ("inner", 3, False),
+    ("rest", 1, True),
     ("rest", 2, False),
-    ("rest", 2, True),
-    ("rest", 2, False),
+    ("rest", 1, True),
+    ("rest", 1, False),
+    ("rest", 1, True),
     ("rest", 1, False),
 )
 SCHEDULE = (
-    ((4, 0), (2, 0), (1, 0),),
-    ((0, 0), (4, 1), (2, 1), (3, 0),),
-    ((1, 1),),
-    ((4, 2), (0, 1), (3, 1), (2, 2),),
+    (),
+    ((0, 0),),
+    ((1, 0),),
+    ((0, 1), (2, 0),),
+    ((3, 0),),
+    (),
+    ((2, 1), (4, 0), (0, 2), (5, 0), (3, 1),),
+    ((0, 3), (1, 1), (5, 1),),
+    ((0, 4), (3, 2),),
+    ((1, 2), (0, 5), (3, 3), (4, 1), (5, 2),),
+    ((3, 4), (0, 6), (1, 3),),
+    ((4, 2), (3, 5), (2, 2), (0, 7),),
     ((4, 3),),
-    ((1, 2), (4, 4),),
-    ((3, 2), (2, 3), (4, 5), (1, 3),),
-    (),
-    ((5, 0), (4, 6), (0, 2),),
-    ((2, 4), (5, 1), (6, 0), (1, 4), (3, 3), (0, 3), (4, 7),),
-    ((7, 0), (6, 1), (5, 2), (7, 1), (0, 4),),
-    ((8, 0), (1, 5), (6, 2), (8, 1), (1, 6), (7, 2), (2, 5), (3, 4), (5, 3), (8, 2), (0, 5), (6, 3), (1, 7), (3, 5), (0, 6), (2, 6), (7, 3), (8, 3), (4, 8), (5, 4), (7, 4), (6, 4), (8, 4), (0, 7), (3, 6), (5, 5), (1, 8), (8, 5), (6, 5), (7, 5), (3, 7), (2, 7),),
-    ((7, 6), (6, 6), (8, 6), (0, 8), (5, 6), (1, 9), (6, 7), (8, 7), (7, 7), (2, 8), (5, 7), (3, 8), (6, 8), (4, 9), (8, 8), (5, 8), (1, 10), (3, 9), (0, 9), (7, 8), (2, 9), (8, 9), (5, 9), (6, 9), (0, 10), (7, 9), (5, 10), (2, 10), (8, 10), (4, 10), (6, 10), (3, 10), (7, 10),),
+    ((0, 8), (6, 0), (3, 6),),
+    ((7, 0), (1, 4), (6, 1), (4, 4), (7, 1),),
+    ((1, 5), (8, 0), (3, 7), (9, 0), (5, 3), (2, 3), (9, 1), (6, 2),),
+    ((8, 1), (10, 0), (5, 4), (7, 2), (4, 5), (10, 1), (1, 6), (6, 3), (8, 2), (5, 5), (2, 4), (7, 3), (10, 2), (3, 8), (8, 3), (9, 2), (7, 4), (6, 4), (10, 3), (8, 4), (5, 6), (0, 9), (2, 5), (1, 7), (9, 3), (4, 6), (10, 4), (6, 5), (2, 6), (5, 7), (7, 5), (1, 8), (9, 4), (6, 6), (7, 6), (4, 7), (8, 5), (2, 7), (8, 6), (9, 5), (10, 5), (1, 9), (6, 7), (0, 10), (5, 8), (9, 6), (4, 8), (8, 7), (9, 7), (6, 8), (1, 10), (10, 6), (3, 9), (5, 9), (7, 7), (2, 8), (9, 8), (10, 7), (8, 8), (7, 8), (10, 8), (5, 10),),
+    ((6, 9), (10, 9), (6, 10), (10, 10), (2, 9), (2, 10), (8, 9), (8, 10), (4, 9), (9, 9), (4, 10), (7, 9),),
+    ((7, 10), (3, 10), (9, 10),),
 )
 
 def finish(inputs, seq_count):
-    unit_rows = PACK * 2 * seq_count
     width = inputs["q"].shape[1]
     block_len, ext_len = inputs["q"].shape[0], inputs["k"].shape[0]
-    chunks, rows = chunks_of(CHUNKS, unit_rows, width)
+    inner_width = inputs["active"].shape[1]
+    chunks, rows = chunks_of(CHUNKS, PACK * 2 * seq_count, width)
     sems = len(chunks) * Sum.last
-    rest_rows = 4 * width + 2 * SPAN
+    rest_rows = rows - 2 * inner_width
     bf = lambda *shape: pltpu.VMEM(shape, jnp.bfloat16)
     f32 = lambda *shape: pltpu.VMEM(shape, jnp.float32)
     dma = pltpu.SemaphoreType.DMA
@@ -946,13 +1010,14 @@
     any_spec = pl.BlockSpec(memory_space=pl.ANY)
     vmem = pl.BlockSpec(memory_space=pltpu.VMEM)
     tiles = block_len // TILE
+    held = SOONEST + SOONER + LATER
     return pl.pallas_call(
         functools.partial(finish_kernel, chunks, SCHEDULE, seq_count),
         in_specs=[vmem if name == "vectors" else any_spec for name in FINISH_IN],
         out_specs=[any_spec] * 3 + [vmem] * 2,
         out_shape=[
-            jax.ShapeDtypeStruct(inputs["outer"].shape, jnp.bfloat16),
-            jax.ShapeDtypeStruct(inputs["inner"].shape, jnp.bfloat16),
+            jax.ShapeDtypeStruct((inner_width, width), jnp.bfloat16),
+            jax.ShapeDtypeStruct((width, inner_width), jnp.bfloat16),
             jax.ShapeDtypeStruct((rest_rows, width), jnp.bfloat16),
             jax.ShapeDtypeStruct(vec_shape, jnp.float32),
             jax.ShapeDtypeStruct((block_len, width), jnp.bfloat16),
@@ -960,17 +1025,16 @@
         scratch_shapes=[
             bf(2, 2, tiles, REACH, TILE), bf(PAIR, block_len), bf(PAIR, ext_len),
             f32(ext_len, PAIR), f32(ext_len, PAIR), f32(PAIR, 2 * SPAN), f32(PAIR, 2 * SPAN + 2 * TILE),
-            bf(block_len + 2 * SPAN, width), bf(ext_len + 2 * SPAN, width), bf(ext_len, width),
-            bf(rest_rows, width), bf(4 * SPAN, width),
-            bf(width, block_len + 2 * SPAN), bf(width, ext_len + 2 * SPAN), bf(ext_len, width), bf(2, SPAN, width), f32(block_len, width),
-            bf(rows, width), bf(2 * rows, width),
+            bf(2 * block_len * (inner_width // width), width), bf(ext_len, width), bf(rows, width),
+            bf(4 * SPAN, width), bf(width, block_len + 2 * SPAN), bf(width, ext_len + 2 * SPAN),
+            bf(width, block_len), bf(ext_len, width), bf(2, SPAN, width), f32(block_len, width), bf(rows, width),
             f32(Sum.phases + 1, *vec_shape), f32(Sum.phases, *vec_shape),
-            dma((len(chunks) + 1,)), dma((sems,)), dma((sems,)), dma((Sum.phases,)), dma((Sum.phases,)),
-            dma((2,)), dma((2,)), dma((2,)), dma((len(SOONER + LATER),)),
-            *(pltpu.VMEM(inputs[name].shape, inputs[name].dtype) for name in SOONER + LATER),
+            dma((len(chunks),)), dma((sems,)), dma((sems,)), dma((Sum.phases,)), dma((Sum.phases,)),
+            dma((2,)), dma((2,)), dma((2,)), dma((len(held),)), dma((2 * (inner_width // width),)),
+            *(pltpu.VMEM(inputs[name].shape, inputs[name].dtype) for name in held),
         ],
         compiler_params=pltpu.CompilerParams(
-            collective_id=0, has_side_effects=True, vmem_limit_bytes=60 * 2**20
+            collective_id=0, has_side_effects=True, vmem_limit_bytes=61 * 2**20
         ),
         name="finish",
     )(*(inputs[name] for name in FINISH_IN))
@@ -994,7 +1058,7 @@
     block_len, width = query.shape
     w_query, w_key, w_value, hot = (inputs[name] for name in ("w_query", "w_key", "w_value", "hot"))
     dquery, dkey, dvalue, drelk, drelq = attend_back(
-        query, key_ext, value_ext, inputs["grad"], inputs["probs_in"], inputs["relk"], inputs["relq"]
+        query, key_ext, value_ext, inputs["grad"], inputs["probs_out"], inputs["relk"], inputs["relq"]
     )
     dkey = low(f32dot("ab,nbd->nad", unit(True), low(dkey).reshape(-1, TILE, width))).reshape(-1, width)
     dvalue = low(dvalue)
@@ -1007,9 +1071,10 @@
         [low(f32dot("md,ed->me", drelk, w_key)), low(f32dot("md,ed->me", drelq, w_query))]
     )
     table_part = f32dot("rm,me->re", hot, table)
-    rest = jnp.concatenate(
-        [low(query_part), low(key_part), low(value_part), inputs["output"], low(table_part)]
-    )
+    output_part = f32dot("dt,te->de", inputs["attn_t"], inputs["mixed_low"])
+    rest = low(jnp.concatenate([output_part, query_part, key_part, value_part, table_part]))
+    outer_part = low(f32dot("tf,td->fd", inputs["active"], inputs["outer_low"]))
+    inner_part = low(f32dot("td,tf->df", inputs["hidden_low"], inputs["inner_low"]))
     ext_grad = f32dot("td,ed->te", dkey, w_key) + f32dot("td,ed->te", dvalue, w_value)
     tokens_grad = (
         inputs["resid"]
@@ -1023,7 +1088,7 @@
         lax.all_gather(
             lax.psum_scatter(part, both, scatter_dimension=0, tiled=True), both, axis=0, tiled=True
         )
-        for part in (inputs["outer"], inputs["inner"], rest)
+        for part in (outer_part, inner_part, rest)
     ]
     return (*sums, lax.psum(inputs["vectors"], both), low(tokens_grad))
 
@@ -1047,9 +1112,9 @@
     }
     kept = start(inputs, lax.axis_size("seq"))
     layer_out = kept.pop("layer_out")
-    inputs.update(kept, probs_in=kept["probs_out"])
+    inputs.update(kept)
     outer_w, inner_w, rest_w, norm_parts, tokens_grad = finish_of(inputs)
-    query_w, key_w, value_w, output_w = (rest_w[at * width : (at + 1) * width] for at in range(4))
+    output_w, query_w, key_w, value_w = (rest_w[at * width : (at + 1) * width] for at in range(4))
     table_w = rest_w[4 * width :]
     return (
         layer_out[None], tokens_grad[None],

time: 248 us -> 235 us (0.948)
  Pallas kernels: 225 us -> 213 us
    pallas_call x1, Pallas kernels: 70.3 us -> 62.5 us  [start(): pl.pallas_call(functools.partial(start_kernel, seq_count), in_specs=[any_...]
    pallas_call x1, Pallas kernels: 155 us -> 150 us  [finish(): pl.pallas_call(functools.partial(finish_kernel, chunks, SCHEDULE, seq_cou...]
where the time goes in v5:
time: 235 us
  Pallas kernels  213 us (91%)
  other arithmetic  18.4 us (8%)
  local copies, waits for them, and re-layouts  3.07 us (1%)
    pallas_call x1, Pallas kernels, finish(): pl.pallas_call(functools.partial(finish_kernel, chunks, SCHEDULE, seq_cou...  150 us
    pallas_call x1, Pallas kernels, start(): pl.pallas_call(functools.partial(start_kernel, seq_count), in_specs=[any_...  62.5 us
    convert_element_type x4, other arithmetic, shards(): w.astype(jnp.float32)  18.4 us

profile of v5, /device:TPU:0, one launch (start us, length us, event | category | flops | bytes accessed | tf_op | source)
XLA Modules:
  0.0 234.8 jit_solution(15640225381235428097)
XLA Ops:
  0.6 62.5 %start.1 = (bf16[768,768]{1,0:T(8,128)(2,1)}, bf16[256,768]{1,0:T(8,128)(2,1)}, bf16[768,768]{1,0:T(8,128)(2,1)}, bf16[768,768]{1,0:T(8,128)(2,1)}, bf16[512,768...) custom-call(bf16[256,768]{1,0:T(8,128)(2,1)} %bitcast.11, ...), custom_call_target="tpu_custom_call" | custom-call | tf_op jit(solution)/shard_map/start/pallas_call | solution.py:488
  63.1 150.2 %finish.1 = (bf16[3072,768]{1,0:T(8,128)(2,1)}, bf16[768,3072]{1,0:T(8,128)(2,1)}, bf16[3584,768]{1,0:T(8,128)(2,1)}, f32[8,768]{1,0:T(8,128)}, bf16[256,768]{1,0:T(8,128)(2,1)}) custom-call(bf16[256,3072]{1,0:T(8,128)(2,1)} %get-tuple-element.39.refs_0_, bf16[256,3072]{1,0:T(8,128)(2,1)} %get-tuple-element.40.refs_1_, ...), custom_call_target="tpu_custom_call" | custom-call | tf_op jit(solution)/shard_map/finish/pallas_call | solution.py:1014
  213.3 1.6 slice_reduce_fusion
  214.9 0.0 slice-start.2
  214.9 2.5 %slice_convert_fusion.4 = f32[512,768]{1,0:T(8,128)} fusion(bf16[3584,768]{1,0:T(8,128)(2,1)} %get-tuple-element.59), kind=kLoop, calls=%fused_computation.4 | loop fusion | flops 393216 | bytes 2359296 | tf_op jit(solution)/shard_map/convert_element_type | solution.py:1121
  217.4 0.0 slice-start.3
  217.4 0.0 slice-start
  217.4 6.3 %slice_convert_fusion = (f32[768,768]{1,0:T(8,128)}, f32[768,768]{1,0:T(8,128)}, f32[768,768]{1,0:T(8,128)}, f32[768,768]{1,0:T(8,128)}) fusion(bf16[3584,768]{1,0:T(8,128)(2,1)} %get-tuple-element.59), kind=kLoop, calls=%fused_computation | loop fusion | flops 2359296 | bytes 14155776 | tf_op jit(solution)/shard_map/convert_element_type | solution.py:1121
  223.7 0.0 slice-start.1
  223.7 0.0 slice-done.2
  223.7 0.0 slice-done.3
  223.8 5.0 %convert_element_type.25 = f32[768,3072]{1,0:T(8,128)} convert(bf16[768,3072]{1,0:T(8,128)(2,1)S(1)} %bitcast.8) | non-fusion elementwise | flops 2359296 | bytes 14155776 | tf_op jit(solution)/shard_map/convert_element_type | solution.py:1121
  228.8 0.0 slice-done
  228.8 0.0 slice-done.1
  228.8 0.0 copy-start
  228.8 0.0 copy-start.1
  228.8 4.5 %convert_element_type.26 = f32[3072,768]{1,0:T(8,128)} convert(bf16[3072,768]{1,0:T(8,128)(2,1)S(1)} %bitcast.6) | non-fusion elementwise | flops 2359296 | bytes 14155776 | tf_op jit(solution)/shard_map/convert_element_type | solution.py:1121
  233.3 0.0 copy-done
  233.3 0.7 copy.31
  234.1 0.0 copy-done.1
  234.1 0.7 copy.32
  (2 shorter events, 0.0 us)
Async XLA Ops:
  214.9 8.9 %slice-start.2 = ((s8[4718592]{0:T(1024)(128)(4,1)}), s8[4194304]{0:T(1024)(128)(4,1)S(1)}, s32[]{:S(2)}) async-start(s8[4718592]{0:T(1024)(128)(4,1)} %bitcast.7), calls=%async_computation.2 | async-start | bytes 8388608
  217.4 6.3 %slice-start.3 = ((s8[4718592]{0:T(1024)(128)(4,1)}), s8[524288]{0:T(1024)(128)(4,1)S(1)}, s32[]{:S(2)}) async-start(s8[4718592]{0:T(1024)(128)(4,1)} %bitcast.7), calls=%async_computation.3 | async-start | bytes 1048576
  217.4 11.4 %slice-start = ((s8[4718592]{0:T(1024)(128)(4,1)}), s8[4194304]{0:T(1024)(128)(4,1)S(1)}, s32[]{:S(2)}) async-start(s8[4718592]{0:T(1024)(128)(4,1)} %bitcast.5), calls=%async_computation | async-start | bytes 8388608
  223.7 5.1 %slice-start.1 = ((s8[4718592]{0:T(1024)(128)(4,1)}), s8[524288]{0:T(1024)(128)(4,1)S(1)}, s32[]{:S(2)}) async-start(s8[4718592]{0:T(1024)(128)(4,1)} %bitcast.5), calls=%async_computation.1 | async-start | bytes 1048576
  228.8 4.5 %copy-start = (bf16[256,768]{1,0:T(8,128)(2,1)S(1)}, bf16[256,768]{1,0:T(8,128)(2,1)}, u32[]{:S(2)}) copy-start(bf16[256,768]{1,0:T(8,128)(2,1)} %get-tuple-element.38) | copy-start | bytes 1179652
  228.8 5.2 %copy-start.1 = (bf16[256,768]{1,0:T(8,128)(2,1)S(1)}, bf16[256,768]{1,0:T(8,128)(2,1)}, u32[]{:S(2)}) copy-start(bf16[256,768]{1,0:T(8,128)(2,1)} %get-tuple-element.58) | copy-start | bytes 1179652

commit v6 on v5

--- a/solution.py
+++ b/solution.py
@@ -159,12 +159,12 @@
     return jnp.mean(values, axis=-1, keepdims=True)
 
 
-def by_blocks(width, body, step=256):
+def by_blocks(width, body, step=256, unroll=3):
     def one(i, carry):
         body(pl.ds(pl.multiple_of(i * step, step), step))
         return carry
 
-    lax.fori_loop(0, width // step, one, 0)
+    lax.fori_loop(0, width // step, one, 0, unroll=unroll)
 
 
 def column_of(row_values):
@@ -199,36 +199,58 @@
         r["bias"][pl.ds(block * TILE, TILE), :] = jnp.where(seen, 0.0, masked_score)
 
 
-def attend_pair(pair, buf, r):
-    eye = unit(False)
+def score_part(r, pair, tile, head, part, q_head, to_term):
+    lanes = pl.ds(pl.multiple_of(pair * PAIR, PAIR), PAIR)
+    first = tile * TILE
+    at = first + part * TILE
+    k_part = r["k"][pl.ds(at, TILE), lanes]
+    window = r["relq"][pl.ds((REACH // TILE - 1 - part) * TILE, 2 * TILE), lanes]
+    from_band = nt(head_lanes(k_part, head), window)
+    from_term = pltpu.roll(from_band, TILE + 1, 1, stride=1, stride_axis=0)[:, :TILE]
+    left = jnp.concatenate([k_part, unit(False)], axis=1)
+    right = jnp.concatenate([q_head, to_term], axis=1)
+    r["scores"][pair, tile, head, pl.ds(part * TILE, TILE), :] = (
+        nt(left, right) + from_term + r["bias"][pl.ds(at, TILE), pl.ds(first, TILE)]
+    )
+
+
+def parts_of(tile, block_len):
+    first = SPAN // TILE - tile
+    own = range(first, first + block_len // TILE)
+    return own, [part for part in range(REACH // TILE) if part not in own]
+
+
+def attend_own(pair, r):
+    lanes = pl.ds(pl.multiple_of(pair * PAIR, PAIR), PAIR)
+    block_len = r["q"].shape[0]
+    for tile in range(block_len // TILE):
+        q_tile = r["q"][pl.ds(tile * TILE, TILE), lanes]
+        for head in range(2):
+            q_head = head_lanes(q_tile, head)
+            band = nt(q_head, r["relk"][:, lanes])
+            band = jnp.concatenate([band, jnp.zeros((TILE, REACH - 2 * SPAN), jnp.float32)], axis=1)
+            to_term = pltpu.roll(band, 0, 1, stride=1, stride_axis=0).astype(jnp.bfloat16)
+            r["to_terms"][pair, tile, head] = to_term
+            for part in parts_of(tile, block_len)[0]:
+                score_part(r, pair, tile, head, part, q_head, to_term[:, part * TILE : (part + 1) * TILE])
+
+
+def attend_rest(pair, buf, r):
     log_two = score_scale * math.log2(math.e)
     lanes = pl.ds(pl.multiple_of(pair * PAIR, PAIR), PAIR)
-    tiles = r["q"].shape[0] // TILE
-    parts = REACH // TILE
+    block_len = r["q"].shape[0]
     for at in range(0, r["v"].shape[0], TILE):
         r["vt"][:, pl.ds(at, TILE)] = r["v"][pl.ds(at, TILE), lanes].T
-    for tile in range(tiles):
+    for tile in range(block_len // TILE):
         first = tile * TILE
         q_tile = r["q"][pl.ds(first, TILE), lanes]
         outs = []
         for head in range(2):
-            score_ref = r["scores"].at[head]
             q_head = head_lanes(q_tile, head)
-            band = nt(q_head, r["relk"][:, lanes])
-            band = jnp.concatenate([band, jnp.zeros((TILE, REACH - 2 * SPAN), jnp.float32)], axis=1)
-            to_term = pltpu.roll(band, 0, 1, stride=1, stride_axis=0).astype(jnp.bfloat16)
-            for part in range(parts):
-                at = first + part * TILE
-                k_part = r["k"][pl.ds(at, TILE), lanes]
-                window = r["relq"][pl.ds((parts - 1 - part) * TILE, 2 * TILE), lanes]
-                from_band = nt(head_lanes(k_part, head), window)
-                from_term = pltpu.roll(from_band, TILE + 1, 1, stride=1, stride_axis=0)[:, :TILE]
-                left = jnp.concatenate([k_part, eye], axis=1)
-                right = jnp.concatenate([q_head, to_term[:, part * TILE : (part + 1) * TILE]], axis=1)
-                score_ref[pl.ds(part * TILE, TILE), :] = (
-                    nt(left, right) + from_term + r["bias"][pl.ds(at, TILE), pl.ds(first, TILE)]
-                )
-            scores = score_ref[...]
+            for part in parts_of(tile, block_len)[1]:
+                to_term = r["to_terms"][pair, tile, head, :, pl.ds(part * TILE, TILE)]
+                score_part(r, pair, tile, head, part, q_head, to_term)
+            scores = r["scores"][pair, tile, head]
             top = jnp.max(scores, axis=0, keepdims=True)
             weights = jnp.exp2((scores - top) * log_two)
             total = jnp.sum(weights, axis=0, keepdims=True)
@@ -252,7 +274,7 @@
 START_OUT = START_KEPT + ("probs_out", "layer_out", "vectors")
 START_SCRATCH = START_KEPT + (
     "rel_table", "w_query", "w_key", "w_value", "w_output", "w_inner", "w_outer", "cotangent",
-    "bias", "vt", "scores", "probs", "attn", "mixed", "hidden", "z_mid", "root_mid", "slope", "sum_grad",
+    "bias", "vt", "scores", "to_terms", "probs", "attn", "mixed", "hidden", "z_mid", "root_mid", "slope", "sum_grad",
     "load_sem", "keep_sem", "probs_sem", "send_sem", "recv_sem",
 )
 
@@ -337,15 +359,26 @@
     by_blocks(width, relk_cols)
     keep("relk")
     loads["w_value"].wait()
+
+    def pair_rows(rows):
+        def pair_cols(cols):
+            r["k"][rows, cols] = low(nn(r["x"][rows, :], r["w_key"][:, cols]))
+            r["v"][rows, cols] = low(nn(r["x"][rows, :], r["w_value"][:, cols]))
+
+        by_blocks(width, pair_cols)
+
+    pair_rows(own)
+
+    def own_pair(pair, carry):
+        attend_own(pair, r)
+        return carry
+
+    lax.fori_loop(0, pairs, own_pair, 0)
     for copy in halos:
         copy.wait()
     keep("x")
-
-    def pair_cols(cols):
-        r["k"][:, cols] = low(nn(r["x"][...], r["w_key"][:, cols]))
-        r["v"][:, cols] = low(nn(r["x"][...], r["w_value"][:, cols]))
-
-    by_blocks(width, pair_cols)
+    pair_rows(pl.ds(0, SPAN))
+    pair_rows(pl.ds(SPAN + block_len, SPAN))
     keep("k")
     keep("v")
 
@@ -361,7 +394,7 @@
         def _():
             probs_copy(pair - 2, buf).wait()
 
-        attend_pair(pair, buf, r)
+        attend_rest(pair, buf, r)
         probs_copy(pair, buf).start()
         return carry
 
@@ -400,7 +433,7 @@
         r["active"][:, cols] = low(active)
         r["slope"][:, cols] = low(slope)
 
-    by_blocks(inner_width, active_cols)
+    by_blocks(inner_width, active_cols, unroll=12)
     keep("active")
 
     def outer_cols(cols):
@@ -430,7 +463,7 @@
         grad = nt(r["outer_low"][...], r["w_outer"][cols, :])
         r["inner_low"][:, cols] = low(grad * r["slope"][:, cols].astype(jnp.float32))
 
-    by_blocks(inner_width, inner_cols)
+    by_blocks(inner_width, inner_cols, unroll=12)
     keep("inner_low")
 
     def hidden_cols(cols):
@@ -498,7 +531,8 @@
         scratch_shapes=[
             *(pltpu.VMEM(sizes[name], kinds[name]) for name in START_KEPT),
             *(pltpu.VMEM(inputs[name].shape, inputs[name].dtype) for name in START_HBM[1:]),
-            f32(ext_len, block_len), bf(PAIR, ext_len), f32(2, REACH, TILE), bf(2, 2, tiles, REACH, TILE),
+            f32(ext_len, block_len), bf(PAIR, ext_len), f32(heads // 2, tiles, 2, REACH, TILE),
+            bf(heads // 2, tiles, 2, TILE, REACH), bf(2, 2, tiles, REACH, TILE),
             bf(block_len, width), f32(block_len, width), f32(block_len, width), f32(block_len, width),
             f32(block_len, TILE), bf(block_len, inner_width), f32(block_len, width),
             dma((len(START_HBM),)), dma((len(START_KEPT),)), dma((2,)), dma((2,)), dma((2,)),
@@ -1040,6 +1074,95 @@
     )(*(inputs[name] for name in FINISH_IN))
 
 
+WIDEN_STEP = 512
+
+
+def widen_pieces(shapes):
+    pieces = []
+    for number, (rows, cols) in enumerate(shapes):
+        step = WIDEN_STEP * shapes[0][1] // cols
+        pieces += [(number, at, min(step, rows - at)) for at in range(0, rows, step)]
+    return pieces
+
+
+def widen_kernel(shapes, splits, vec_rows, kept, *refs):
+    count, total = len(shapes), len(splits)
+    ins, vec_in, kept_in = refs[:count], refs[count], refs[count + 1 : count + 1 + kept]
+    refs = refs[count + 1 + kept :]
+    outs, vec_outs, kept_outs = refs[:total], refs[total : total + vec_rows], refs[total + vec_rows :][:kept]
+    scratch = refs[total + vec_rows + kept :]
+    narrow, wide = scratch[:count], scratch[count : 2 * count]
+    held, (load_sem, store_sem, kept_sem) = scratch[2 * count : 2 * count + kept], scratch[2 * count + kept :]
+    pieces = widen_pieces(shapes)
+    loads = [
+        pltpu.make_async_copy(
+            ins[number].at[pl.ds(at, rows)], narrow[number].at[pl.ds(at, rows)], load_sem.at[i]
+        )
+        for i, (number, at, rows) in enumerate(pieces)
+    ]
+    for load in loads:
+        load.start()
+    fetches = [pltpu.make_async_copy(kept_in[i], held[i], kept_sem.at[i]) for i in range(kept)]
+    stores = [pltpu.make_async_copy(held[i], kept_outs[i], kept_sem.at[i]) for i in range(kept)]
+    for fetch in fetches:
+        fetch.start()
+    for number in range(vec_rows):
+        vec_outs[number][...] = vec_in[number, :]
+    for fetch, store in zip(fetches, stores):
+        fetch.wait()
+        store.start()
+    for load, (number, at, rows) in zip(loads, pieces):
+        load.wait()
+        cols = shapes[number][1]
+        step = 32 if cols <= 1024 else 16
+
+        def body(i, carry, number=number, at=at, step=step):
+            here = pl.ds(pl.multiple_of(at + i * step, PACK), step)
+            wide[number][here, :] = narrow[number][here, :].astype(jnp.float32)
+            return carry
+
+        lax.fori_loop(0, rows // step, body, 0)
+        for out, (source, first, high) in enumerate(splits):
+            low_row, high_row = max(at, first), min(at + rows, first + high)
+            if source == number and low_row < high_row:
+                store = pltpu.make_async_copy(
+                    wide[number].at[pl.ds(low_row, high_row - low_row)],
+                    outs[out].at[pl.ds(low_row - first, high_row - low_row)],
+                    store_sem.at[len(stores) - kept],
+                )
+                store.start()
+                stores.append(store)
+    for store in stores:
+        store.wait()
+
+
+def widen(arrays, splits, vectors, vec_rows, kept):
+    shapes = [a.shape for a in arrays]
+    pieces = widen_pieces(shapes)
+    any_spec = pl.BlockSpec(memory_space=pl.ANY)
+    vmem = pl.BlockSpec(memory_space=pltpu.VMEM)
+    dma = pltpu.SemaphoreType.DMA
+    width = vectors.shape[1]
+    return pl.pallas_call(
+        functools.partial(widen_kernel, shapes, splits, vec_rows, len(kept)),
+        in_specs=[any_spec] * len(arrays) + [vmem] + [any_spec] * len(kept),
+        out_specs=[any_spec] * len(splits) + [vmem] * vec_rows + [any_spec] * len(kept),
+        out_shape=[
+            *(jax.ShapeDtypeStruct((rows, shapes[number][1]), jnp.float32) for number, _, rows in splits),
+            *(jax.ShapeDtypeStruct((width,), jnp.float32) for _ in range(vec_rows)),
+            *(jax.ShapeDtypeStruct(a.shape, a.dtype) for a in kept),
+        ],
+        scratch_shapes=[
+            *(pltpu.VMEM(shape, jnp.bfloat16) for shape in shapes),
+            *(pltpu.VMEM(shape, jnp.float32) for shape in shapes),
+            *(pltpu.VMEM(a.shape, a.dtype) for a in kept),
+            dma((len(pieces),)), dma((len(pieces) + len(splits),)), dma((len(kept),)),
+        ],
+        compiler_params=pltpu.CompilerParams(vmem_limit_bytes=60 * 2**20),
+        name="widen",
+    )(*arrays, vectors, *kept)
+
+
 def shifted(shard, axis, by):
     count = lax.axis_size(axis)
     pairs = [(i, i + by) for i in range(count) if 0 <= i + by < count]
@@ -1114,12 +1237,14 @@
     layer_out = kept.pop("layer_out")
     inputs.update(kept)
     outer_w, inner_w, rest_w, norm_parts, tokens_grad = finish_of(inputs)
-    output_w, query_w, key_w, value_w = (rest_w[at * width : (at + 1) * width] for at in range(4))
-    table_w = rest_w[4 * width :]
+    splits = [(0, 0, outer_w.shape[0]), (1, 0, width)]
+    splits += [(2, at * width, width) for at in range(4)] + [(2, 4 * width, rest_w.shape[0] - 4 * width)]
+    values = widen([outer_w, inner_w, rest_w], splits, norm_parts, 4, [layer_out, tokens_grad])
+    outer_w, inner_w, output_w, query_w, key_w, value_w, table_w, *norms = values
+    *norms, layer_out, tokens_grad = norms
     return (
-        layer_out[None], tokens_grad[None],
-        *(w.astype(jnp.float32) for w in (query_w, key_w, value_w, output_w, inner_w, outer_w, table_w)),
-        *(norm_parts[at] for at in range(4)),
+        layer_out[None], tokens_grad[None], query_w, key_w, value_w, output_w, inner_w, outer_w, table_w,
+        *norms,
     )
 
 

time: 235 us -> 217 us (0.923)
  other arithmetic: 18.4 us -> 0 us
  local copies, waits for them, and re-layouts: 3.07 us -> 0 us
  Pallas kernels: 213 us -> 216 us
    convert_element_type x4 -> x0, other arithmetic: 18.4 us -> none  [shards(): w.astype(jnp.float32)]
    pallas_call x0 -> x1, Pallas kernels: none -> 17.2 us  [widen(): pl.pallas_call(functools.partial(widen_kernel, shapes, splits, vec_rows,...]
    pallas_call x1, Pallas kernels: 62.5 us -> 49.7 us  [start(): pl.pallas_call(functools.partial(start_kernel, seq_count), in_specs=[any_...]
where the time goes in v6:
time: 217 us
  Pallas kernels  216 us (100%)
    pallas_call x1, Pallas kernels, finish(): pl.pallas_call(functools.partial(finish_kernel, chunks, SCHEDULE, seq_cou...  149 us
    pallas_call x1, Pallas kernels, start(): pl.pallas_call(functools.partial(start_kernel, seq_count), in_specs=[any_...  49.7 us
    pallas_call x1, Pallas kernels, widen(): pl.pallas_call(functools.partial(widen_kernel, shapes, splits, vec_rows,...  17.2 us

profile of v6, /device:TPU:0, one launch (start us, length us, event | category | flops | bytes accessed | tf_op | source)
XLA Modules:
  0.0 216.8 jit_solution(11272223158385075500)
XLA Ops:
  0.6 49.7 %start.1 = (bf16[768,768]{1,0:T(8,128)(2,1)}, bf16[256,768]{1,0:T(8,128)(2,1)}, bf16[768,768]{1,0:T(8,128)(2,1)}, bf16[768,768]{1,0:T(8,128)(2,1)}, bf16[512,768...) custom-call(bf16[256,768]{1,0:T(8,128)(2,1)} %bitcast.5, ...), custom_call_target="tpu_custom_call" | custom-call | tf_op jit(solution)/shard_map/start/pallas_call | solution.py:521
  50.4 149.1 %finish.1 = (bf16[3072,768]{1,0:T(8,128)(2,1)}, bf16[768,3072]{1,0:T(8,128)(2,1)}, bf16[3584,768]{1,0:T(8,128)(2,1)}, f32[8,768]{1,0:T(8,128)}, bf16[256,768]{1,0:T(8,128)(2,1)}) custom-call(bf16[256,3072]{1,0:T(8,128)(2,1)} %get-tuple-element.51.refs_0_, bf16[256,3072]{1,0:T(8,128)(2,1)} %get-tuple-element.52.refs_1_, ...), custom_call_target="tpu_custom_call" | custom-call | tf_op jit(solution)/shard_map/finish/pallas_call | solution.py:1048
  199.5 17.2 %widen.1 = (f32[3072,768]{1,0:T(8,128)}, f32[768,3072]{1,0:T(8,128)}, f32[768,768]{1,0:T(8,128)}, f32[768,768]{1,0:T(8,128)}, f32[768,768]{1,0:T(8,128)}, /*inde...) custom-call(bf16[3072,768]{1,0:T(8,128)(2,1)} %get-tuple-element.70., ...), custom_call_target="tpu_custom_call" | custom-call | tf_op jit(solution)/shard_map/widen/pallas_call | solution.py:1146

commit v7 on v6

--- a/solution.py
+++ b/solution.py
@@ -373,7 +373,7 @@
         attend_own(pair, r)
         return carry
 
-    lax.fori_loop(0, pairs, own_pair, 0)
+    lax.fori_loop(0, pairs, own_pair, 0, unroll=2)
     for copy in halos:
         copy.wait()
     keep("x")
@@ -425,7 +425,7 @@
         r["hidden"][rows, :] = hidden
         r["hidden_low"][rows, :] = low(hidden)
 
-    by_blocks(block_len, mid_rows, high)
+    by_blocks(block_len, mid_rows, high, 4)
     keep("hidden_low")
 
     def active_cols(cols):
@@ -456,7 +456,7 @@
         r["sum_grad"][rows, :] = sum_grad
         r["outer_low"][rows, :] = low(sum_grad)
 
-    by_blocks(block_len, end_rows, high)
+    by_blocks(block_len, end_rows, high, 4)
     keep("outer_low")
 
     def inner_cols(cols):
@@ -481,7 +481,7 @@
         r["resid"][rows, :] = resid
         r["mixed_low"][rows, :] = low(resid)
 
-    by_blocks(block_len, resid_rows, high)
+    by_blocks(block_len, resid_rows, high, 4)
     keep("resid")
     keep("mixed_low")
 
@@ -955,16 +955,16 @@
             total.step(c, stage)
 
     advance(schedule[0])
-    for name in ("outer_low", "hidden_low"):
-        loads[name].wait()
+    loads["outer_low"].wait()
     for copy in wide_loads["active"]:
         copy.wait()
-    r["hidden_t"][...] = r["hidden_low"][...].T
     fresh = True
     for number, chunk in enumerate(early):
         if chunk.which == "inner" and fresh:
             for copy in wide_loads["inner_low"]:
                 copy.wait()
+            loads["hidden_low"].wait()
+            r["hidden_t"][...] = r["hidden_low"][...].T
             fresh = False
         (inner_piece if chunk.which == "inner" else outer_piece)(chunk)
         advance(schedule[number + 1])

time: 217 us -> 217 us (level)
  no operation moved by 1% of the time
where the time goes in v7:
time: 217 us
  Pallas kernels  216 us (100%)
    pallas_call x1, Pallas kernels, finish(): pl.pallas_call(functools.partial(finish_kernel, chunks, SCHEDULE, seq_cou...  149 us
    pallas_call x1, Pallas kernels, start(): pl.pallas_call(functools.partial(start_kernel, seq_count), in_specs=[any_...  49.7 us
    pallas_call x1, Pallas kernels, widen(): pl.pallas_call(functools.partial(widen_kernel, shapes, splits, vec_rows,...  17.2 us

profile of v7, /device:TPU:0, one launch (start us, length us, event | category | flops | bytes accessed | tf_op | source)
XLA Modules:
  0.0 216.7 jit_solution(15776583834717929872)
XLA Ops:
  0.6 49.7 %start.1 = (bf16[768,768]{1,0:T(8,128)(2,1)}, bf16[256,768]{1,0:T(8,128)(2,1)}, bf16[768,768]{1,0:T(8,128)(2,1)}, bf16[768,768]{1,0:T(8,128)(2,1)}, bf16[512,768...) custom-call(bf16[256,768]{1,0:T(8,128)(2,1)} %bitcast.5, ...), custom_call_target="tpu_custom_call" | custom-call | tf_op jit(solution)/shard_map/start/pallas_call | solution.py:521
  50.4 148.9 %finish.1 = (bf16[3072,768]{1,0:T(8,128)(2,1)}, bf16[768,3072]{1,0:T(8,128)(2,1)}, bf16[3584,768]{1,0:T(8,128)(2,1)}, f32[8,768]{1,0:T(8,128)}, bf16[256,768]{1,0:T(8,128)(2,1)}) custom-call(bf16[256,3072]{1,0:T(8,128)(2,1)} %get-tuple-element.51.refs_0_, bf16[256,3072]{1,0:T(8,128)(2,1)} %get-tuple-element.52.refs_1_, ...), custom_call_target="tpu_custom_call" | custom-call | tf_op jit(solution)/shard_map/finish/pallas_call | solution.py:1048
  199.3 17.2 %widen.1 = (f32[3072,768]{1,0:T(8,128)}, f32[768,3072]{1,0:T(8,128)}, f32[768,768]{1,0:T(8,128)}, f32[768,768]{1,0:T(8,128)}, f32[768,768]{1,0:T(8,128)}, /*inde...) custom-call(bf16[3072,768]{1,0:T(8,128)(2,1)} %get-tuple-element.70., ...), custom_call_target="tpu_custom_call" | custom-call | tf_op jit(solution)/shard_map/widen/pallas_call | solution.py:1146
